TPU v7x, 512 devices: a whole 4x8x8 slice. The times are simulated.
512 devices in a mesh: dp: 2 (over x_hi), seq: 256 (over y, z, x_lo, core).
Axes of the slice: x: 4 (x_hi: 2, x_lo: 2; x = x_hi * 2 + x_lo), y: 8, z: 8, core: 2. Of those that a mesh axis runs over, the one named last changes fastest.
Arguments:
- query_raw: bfloat16 [2, 65536, 1024], P('dp', 'seq'), may hold values from -60 to 60
- unnormalized_keys: bfloat16 [2, 65536, 512], P('dp', 'seq'), may hold values from -60 to 60
- values: bfloat16 [2, 65536, 512], P('dp', 'seq'), may hold values from -6 to 6
- output_gradient: bfloat16 [2, 65536, 1024], P('dp', 'seq'), may hold values from -6 to 6
- query_gain: float32 [256], replicated, may hold values from 0.5 to 4
- key_norm_gain: float32 [256], replicated, may hold values from 0.5 to 4
- document_ids: int32 [2, 65536], P('dp', 'seq'), may hold values from 0 to 31, never falling along the last dimension, each value on 1 to 8192 neighbouring positions
Outputs:
- attended: bfloat16 [2, 65536, 1024], P('dp', 'seq')
- unnormalized_query_gradient: bfloat16 [2, 65536, 1024], P('dp', 'seq')
- unnormalized_key_gradient: bfloat16 [2, 65536, 512], P('dp', 'seq')
- value_grad: bfloat16 [2, 65536, 512], P('dp', 'seq')
- query_gain_grad: float32 [256], replicated
- key_gain_grad: float32 [256], replicated
Inputs may be any that keep to these rules, and one draw needn't show every extreme that they name: `document_ids`: ids never fall along a sequence; every document has 1 to 8192 tokens, one exactly 8192.
All inputs are finite; a program needn't handle non-finite values.
Results may differ from a plain program's by a relative error of at most 0.011.
The roundings to bfloat16 on the way count: a program that leaves them out, or rounds other values in their place, can miss the bound.
Values may be sent and summed in bfloat16 or wider, within the bound.
No kernel may reach another device: no remote copies, remote signals or barrier semaphores. Data moves between devices by JAX's collectives and lax.ppermute only.
A program may use at most 64 MiB of HBM per device.

v0:
```python
from functools import reduce

import jax
import jax.numpy as jnp
from jax import lax
from jax.sharding import PartitionSpec as P

HEAD_SIZE = 256
LOOKBACK_SPAN = 1024


def from_behind(value, axis, by):
    count = lax.axis_size(axis)
    pairs = [(i, i + by) for i in range(count) if 0 <= i + by < count]
    return lax.ppermute(value, axis, pairs)


def apply_norm(raw_rows, gain_vec, head_count):
    float_rows = raw_rows.astype(jnp.float32).reshape(raw_rows.shape[0], head_count, HEAD_SIZE)
    inverse = lax.rsqrt(jnp.mean(float_rows * float_rows, axis=-1, keepdims=True) + 1e-06)
    unit_rows = float_rows * inverse
    return (unit_rows * gain_vec, unit_rows, inverse)


def backward_norm(upstream, unit_rows, inverse, gain_vec):
    scaled = upstream * gain_vec
    inner_mean = jnp.mean(scaled * unit_rows, axis=-1, keepdims=True)
    return (inverse * (scaled - unit_rows * inner_mean), jnp.sum(upstream * unit_rows, axis=(0, 1)))


def per_device(
    query_raw, unnormalized_keys, values, output_gradient, query_gain, key_norm_gain, document_ids
):
    shard_rows = query_raw.shape[1]
    q_heads = query_raw.shape[2] // HEAD_SIZE
    kv_heads = unnormalized_keys.shape[2] // HEAD_SIZE
    query_group_width = q_heads // kv_heads
    reach_shards = LOOKBACK_SPAN // shard_rows
    score_scale = HEAD_SIZE ** (-0.5)
    normalized_queries, query_unit, query_inverse = apply_norm(query_raw[0], query_gain, q_heads)
    normalized_keys, unit_keys, key_inverse_norm = apply_norm(
        unnormalized_keys[0], key_norm_gain, kv_heads
    )
    query_rows = normalized_queries.astype(jnp.bfloat16).reshape(
        shard_rows, kv_heads, query_group_width, HEAD_SIZE
    )
    gradient_rows = output_gradient[0].reshape(shard_rows, kv_heads, query_group_width, HEAD_SIZE)
    own_tags = document_ids[0] + 1
    own_part = (
        normalized_keys.astype(jnp.bfloat16).reshape(shard_rows, kv_heads * HEAD_SIZE),
        values[0],
        own_tags,
    )
    received = [own_part]
    for distance in range(1, reach_shards + 1):
        received.append(from_behind((own_part[0], own_part[1], own_part[2]), "seq", distance))
    positions = jnp.arange(shard_rows)

    def mask_for(distance, key_tags):
        token_gap = positions[:, None] - positions[None, :] + distance * shard_rows
        return (
            (token_gap >= 0)
            & (token_gap < LOOKBACK_SPAN)
            & (own_tags[:, None] == key_tags[None, :])
        )

    mask_list = [
        mask_for(shard_index, received[shard_index][2]) for shard_index in range(reach_shards + 1)
    ]
    key_list = [
        received[shard_index][0].reshape(shard_rows, kv_heads, HEAD_SIZE)
        for shard_index in range(reach_shards + 1)
    ]
    value_list = [
        received[shard_index][1].reshape(shard_rows, kv_heads, HEAD_SIZE)
        for shard_index in range(reach_shards + 1)
    ]

    def guarded(shard_index, compute_fn):
        if shard_index == 0:
            return compute_fn()
        return compute_fn()

    score_list = []
    for shard_index in range(reach_shards + 1):

        def score_shard(mask_now=mask_list[shard_index], key_block=key_list[shard_index]):
            raw_scores = jnp.einsum(
                "qhgd,khd->hgqk", query_rows, key_block, preferred_element_type=jnp.float32
            )
            return jnp.where(mask_now, raw_scores * score_scale, -jnp.inf)

        score_list.append(guarded(shard_index, score_shard))
    row_max = reduce(
        jnp.maximum, [jnp.max(scores, axis=-1, keepdims=True) for scores in score_list]
    )
    row_total = sum(
        (jnp.sum(jnp.exp(scores - row_max), axis=-1, keepdims=True) for scores in score_list)
    )
    log_total = row_max + jnp.log(row_total)
    output_parts = []
    for shard_index in range(reach_shards + 1):

        def weigh_shard(scores=score_list[shard_index], value_block=value_list[shard_index]):
            weights = jnp.exp(scores - log_total).astype(jnp.bfloat16)
            return jnp.einsum(
                "hgqk,khd->qhgd", weights, value_block, preferred_element_type=jnp.float32
            )

        output_parts.append(guarded(shard_index, weigh_shard))
    attended = sum(output_parts).astype(jnp.bfloat16)
    row_delta = jnp.einsum(
        "qhgd,qhgd->hgq", attended, gradient_rows, preferred_element_type=jnp.float32
    )[..., None]
    query_parts = []
    grad_list = []
    for shard_index in range(reach_shards + 1):

        def grad_shard(
            scores=score_list[shard_index],
            key_block=key_list[shard_index],
            value_block=value_list[shard_index],
        ):
            probabilities = jnp.exp(scores - log_total)
            weights = probabilities.astype(jnp.bfloat16)
            prob_grads = jnp.einsum(
                "qhgd,khd->hgqk", gradient_rows, value_block, preferred_element_type=jnp.float32
            )
            score_grads = (probabilities * (prob_grads - row_delta) * score_scale).astype(
                jnp.bfloat16
            )
            query_portion = jnp.einsum(
                "hgqk,khd->qhgd", score_grads, key_block, preferred_element_type=jnp.float32
            )
            key_portion = jnp.einsum(
                "hgqk,qhgd->khd", score_grads, query_rows, preferred_element_type=jnp.float32
            )
            value_part = jnp.einsum(
                "hgqk,qhgd->khd", weights, gradient_rows, preferred_element_type=jnp.float32
            )
            return (
                query_portion,
                jnp.stack(
                    [
                        key_portion.reshape(shard_rows, kv_heads * HEAD_SIZE),
                        value_part.reshape(shard_rows, kv_heads * HEAD_SIZE),
                    ]
                ),
            )

        query_portion, pair_part = guarded(shard_index, grad_shard)
        query_parts.append(query_portion)
        grad_list.append(pair_part)
    query_grads = sum(query_parts)
    combined = grad_list[0]
    for distance in range(1, reach_shards + 1):
        combined = combined + from_behind(grad_list[distance], "seq", -distance)
    unnormalized_query_gradient, query_part_gain = backward_norm(
        query_grads.reshape(shard_rows, q_heads, HEAD_SIZE), query_unit, query_inverse, query_gain
    )
    unnormalized_key_gradient, key_part_gain = backward_norm(
        combined[0].reshape(shard_rows, kv_heads, HEAD_SIZE),
        unit_keys,
        key_inverse_norm,
        key_norm_gain,
    )
    query_gain_grad, key_gain_grad = lax.psum((query_part_gain, key_part_gain), ("dp", "seq"))
    return (
        attended.reshape(1, shard_rows, q_heads * HEAD_SIZE),
        unnormalized_query_gradient.reshape(1, shard_rows, q_heads * HEAD_SIZE).astype(
            jnp.bfloat16
        ),
        unnormalized_key_gradient.reshape(1, shard_rows, kv_heads * HEAD_SIZE).astype(jnp.bfloat16),
        combined[1].reshape(1, shard_rows, kv_heads * HEAD_SIZE).astype(jnp.bfloat16),
        query_gain_grad,
        key_gain_grad,
    )


def solution(mesh):
    return jax.shard_map(
        per_device,
        mesh=mesh,
        in_specs=(
            P("dp", "seq", None),
            P("dp", "seq", None),
            P("dp", "seq", None),
            P("dp", "seq", None),
            P(),
            P(),
            P("dp", "seq"),
        ),
        out_specs=(
            P("dp", "seq", None),
            P("dp", "seq", None),
            P("dp", "seq", None),
            P("dp", "seq", None),
            P(),
            P(),
        ),
        check_vma=False,
    )
```

profile of v0, /device:TPU:1, one launch (start us, length us, event | category | flops | bytes accessed | tf_op | source)
XLA Modules:
  0.0 294.1 jit_solution(3382329622353592024)
XLA Ops:
  1.3 4.5 %collective-permute-start = (s32[256]{0:T(256)S(1)}, s32[256]{0:T(256)S(1)}, u32[]{:S(2)}, u32[]{:S(2)}) collective-permute-start(s32[256]{0:T(256)S(1)} %bitcast.340), channel_id=1, source_target_pairs={{0,1},{1,2},{2,3},{3,4},{4,5},{5,6},{6,7},{7,8},{8,9},{9,10},{10,1... | collective-permute-start | bytes 3080 | tf_op jit(solution)/shard_map/ppermute | solution.py:15
  5.8 4.0 %collective-permute-start.2 = (s32[256]{0:T(256)S(1)}, s32[256]{0:T(256)S(1)}, u32[]{:S(2)}, u32[]{:S(2)}) collective-permute-start(s32[256]{0:T(256)S(1)} %bitcast.341), channel_id=1, source_target_pairs={{0,2},{1,3},{2,4},{3,5},{4,6},{5,7},{6,8},{7,9},{8,10},{9,11},{10,... | collective-permute-start | bytes 3080 | tf_op jit(solution)/shard_map/ppermute | solution.py:15
  9.8 2.2 collective-permute-start.4
  12.0 4.0 %collective-permute-start.6 = (s32[256]{0:T(256)S(1)}, s32[256]{0:T(256)S(1)}, u32[]{:S(2)}, u32[]{:S(2)}) collective-permute-start(s32[256]{0:T(256)S(1)} %bitcast.343), channel_id=1, source_target_pairs={{0,4},{1,5},{2,6},{3,7},{4,8},{5,9},{6,10},{7,11},{8,12},{9,13},{1... | collective-permute-start | bytes 3080 | tf_op jit(solution)/shard_map/ppermute | solution.py:15
  16.0 1.1 copy.314
  19.0 4.0 %collective-permute-start.7 = (bf16[256,512]{0,1:T(8,128)(2,1)}, bf16[256,512]{0,1:T(8,128)(2,1)S(1)}, u32[]{:S(2)}, u32[]{:S(2)}) collective-permute-start(bf16[256,512]{0,1:T(8,128)(2,1)} %fusion.45), channel_id=1, source_target_pairs={{0,4},{1,5},{2,6},{3,7},{4,8},{5,9},{6,10},{7,11},{8,12},{9,13},{1... | collective-permute-start | bytes 786440 | tf_op jit(solution)/shard_map/ppermute | solution.py:15
  23.0 1.1 convert_multiply_fusion
  24.3 3.0 %mul.250 = f32[256,4,256]{2,1,0:T(4,128)} reshape(f32[1,256,1024]{2,1,0:T(8,128)} %convert_multiply_fusion) | data formatting | bytes 2097152 | tf_op jit(solution)/shard_map/mul | solution.py:20
  27.3 1.6 reduce_sum.107
  33.1 1.3 mul.271
  34.4 2.7 mul.272
  37.7 6.9 %collective-permute-start.5 = (bf16[256,512]{0,1:T(8,128)(2,1)}, bf16[256,512]{0,1:T(8,128)(2,1)S(1)}, u32[]{:S(2)}, u32[]{:S(2)}) collective-permute-start(bf16[256,512]{0,1:T(8,128)(2,1)} %fusion.45), channel_id=1, source_target_pairs={{0,3},{1,4},{2,5},{3,6},{4,7},{5,8},{6,9},{7,10},{8,11},{9,12},{10... | collective-permute-start | bytes 786440 | tf_op jit(solution)/shard_map/ppermute | solution.py:15
  44.6 3.1 %collective-permute-start.3 = (bf16[256,512]{0,1:T(8,128)(2,1)}, bf16[256,512]{0,1:T(8,128)(2,1)S(1)}, u32[]{:S(2)}, u32[]{:S(2)}) collective-permute-start(bf16[256,512]{0,1:T(8,128)(2,1)} %fusion.45), channel_id=1, source_target_pairs={{0,2},{1,3},{2,4},{3,5},{4,6},{5,7},{6,8},{7,9},{8,10},{9,11},{10,... | collective-permute-start | bytes 786440 | tf_op jit(solution)/shard_map/ppermute | solution.py:15
  47.7 2.2 collective-permute-start.1
  50.0 3.2 %collective-permute-start.8 = (bf16[256,512]{1,0:T(8,128)(2,1)}, bf16[256,512]{1,0:T(8,128)(2,1)}, u32[]{:S(2)}, u32[]{:S(2)}) collective-permute-start(bf16[256,512]{1,0:T(8,128)(2,1)} %bitcast.22), channel_id=1, source_target_pairs={{0,1},{1,2},{2,3},{3,4},{4,5},{5,6},{6,7},{7,8},{8,9},{9,10},{10,1... | collective-permute-start | bytes 786440 | tf_op jit(solution)/shard_map/ppermute | solution.py:15
  54.0 2.9 collective-permute-start.10
  56.9 1.3 select_reduce_fusion
  58.2 3.1 %collective-permute-start.11 = (bf16[256,512]{1,0:T(8,128)(2,1)}, bf16[256,512]{1,0:T(8,128)(2,1)}, u32[]{:S(2)}, u32[]{:S(2)}) collective-permute-start(bf16[256,512]{1,0:T(8,128)(2,1)} %bitcast.22), channel_id=1, source_target_pairs={{0,4},{1,5},{2,6},{3,7},{4,8},{5,9},{6,10},{7,11},{8,12},{9,13},{1... | collective-permute-start | bytes 786440 | tf_op jit(solution)/shard_map/ppermute | solution.py:15
  61.7 3.8 %collective-permute-start.9 = (bf16[256,512]{1,0:T(8,128)(2,1)}, bf16[256,512]{1,0:T(8,128)(2,1)}, u32[]{:S(2)}, u32[]{:S(2)}) collective-permute-start(bf16[256,512]{1,0:T(8,128)(2,1)} %bitcast.22), channel_id=1, source_target_pairs={{0,2},{1,3},{2,4},{3,5},{4,6},{5,7},{6,8},{7,9},{8,10},{9,11},{10,... | collective-permute-start | bytes 786440 | tf_op jit(solution)/shard_map/ppermute | solution.py:15
  67.9 1.4 fusion.73
  69.3 1.8 copy.329
  71.1 3.1 %convolution_add_fusion.1 = f32[2,2,256,256]{2,3,1,0:T(8,128)} fusion(f32[2,2,256,256]{2,3,1,0:T(8,128)} %fusion.73, bf16[256,2,256,1]{0,2,3,1:T(8,128)(2,1)} %bitcast.333, f32[2,2,256,256]{2,3,1,0:T(8,128)} %copy-done.4, f32[2,2,256]{2,1,0:T(2,128)S(1)} %log_add_fusion, pred[256,256]{0,1:T(8,128)(4,1)} %copy-done.20), kind=kOutput, calls=%fused_computation.3 | convolution fusion | flops 135266304 | bytes 3477504 | tf_op jit(solution)/shard_map/hgqk,khd->qhgd/dot_general | solution.py:106
  74.2 1.8 copy.333
  76.0 2.7 fusion.81
  78.7 1.8 copy.335
  80.4 2.4 fusion.77
  82.8 1.8 copy.331
  84.6 3.5 %fusion.30 = bf16[2,2,256,256]{2,3,1,0:T(8,128)(2,1)} fusion(f32[2,2,256,256]{2,3,1,0:T(8,128)} %fusion.77, f32[2,2,256,256]{2,3,1,0:T(8,128)} %fusion.81, f32[2,2,256,256]{2,3,1,0:T(8,128)} %convolution_add_fusion.1, bf16[256,2,256,1]{0,2,3,1:T(8,128)(2,1)} %bitcast.324, f32[2,2,256,256]{2,3,1,0:T(8,128)} %copy-done.2, f32[2,2,256]{2,1,0:T(2,128)S(1)} %log_add_fusion, ...), kind=kOutput, calls=%fused_computation.44 | convolution fusion | flops 136052736 | bytes 5050368 | tf_op jit(solution)/shard_map/hgqk,khd->qhgd/dot_general | solution.py:106
  88.1 2.1 copy.399
  90.1 2.9 multiply_reduce_fusion
  93.0 1.7 copy.400
  94.7 1.7 fusion.86
  106.6 3.8 %collective-permute-start.12 = (f32[2,256,512]{1,2,0:T(8,128)}, f32[2,256,512]{1,2,0:T(8,128)}, u32[]{:S(2)}, u32[]{:S(2)}) collective-permute-start(f32[2,256,512]{1,2,0:T(8,128)} %pad_maximum_fusion), channel_id=1, source_target_pairs={{1,0},{2,1},{3,2},{4,3},{5,4},{6,5},{7,6},{8,7},{9,8},{10,9},{11,1... | collective-permute-start | bytes 3145736 | tf_op jit(solution)/shard_map/ppermute | solution.py:15
  111.8 1.3 collective-permute-start.13
  113.1 1.1 pad_maximum_fusion.2
  114.3 1.3 collective-permute-start.14
  116.6 1.6 collective-permute-start.15
  119.9 2.1 fusion.34
  122.2 1.4 mul.290
  123.5 2.8 mul.291
  126.3 2.6 copy.353
  128.8 2.0 copy.370
  133.0 1.2 multiply_convert_fusion
  134.2 5.1 %collective-permute-done.13 = f32[2,256,512]{1,2,0:T(8,128)} collective-permute-done((f32[2,256,512]{1,2,0:T(8,128)}, f32[2,256,512]{1,2,0:T(8,128)}, u32[]{:S(2)}, u32[]{:S(2)}) %collective-permute-start.13) | collective-permute-done | bytes 1048608 | tf_op jit(solution)/shard_map/ppermute | solution.py:15
  139.3 35.8 %collective-permute-done.14 = f32[2,256,512]{1,2,0:T(8,128)} collective-permute-done((f32[2,256,512]{1,2,0:T(8,128)}, f32[2,256,512]{1,2,0:T(8,128)}, u32[]{:S(2)}, u32[]{:S(2)}) %collective-permute-start.14) | collective-permute-done | bytes 1048608 | tf_op jit(solution)/shard_map/ppermute | solution.py:15
  175.0 8.1 %collective-permute-done.15 = f32[2,256,512]{1,2,0:T(8,128)} collective-permute-done((f32[2,256,512]{1,2,0:T(8,128)}, f32[2,256,512]{1,2,0:T(8,128)}, u32[]{:S(2)}, u32[]{:S(2)}) %collective-permute-start.15) | collective-permute-done | bytes 1048608 | tf_op jit(solution)/shard_map/ppermute | solution.py:15
  183.2 2.5 fusion.33
  189.3 104.9 %all-reduce = (f32[256]{0:T(256)}, f32[256]{0:T(256)}) all-reduce(f32[256]{0:T(256)S(1)} %copy-done.42, f32[256]{0:T(256)S(1)} %reduce_sum.118), channel_id=1, replica_groups=mesh['dp'=2,'seq'=256] {'dp','seq'}, use_global_device_ids=true, to_apply=%region_15.16 | all-reduce | flops 512 | bytes 4096 | tf_op jit(solution)/shard_map/psum | solution.py:167
  (157 shorter events, 30.6 us)
Async XLA Ops:
  1.3 36.4 %collective-permute-start = (s32[256]{0:T(256)S(1)}, s32[256]{0:T(256)S(1)}, u32[]{:S(2)}, u32[]{:S(2)}) collective-permute-start(s32[256]{0:T(256)S(1)} %bitcast.340), channel_id=1, source_target_pairs={{0,1},{1,2},{2,3},{3,4},{4,5},{5,6},{6,7},{7,8},{8,9},{9,10},{10,1... | collective-permute-start | bytes 3080 | tf_op jit(solution)/shard_map/ppermute | solution.py:15
  5.8 38.8 %collective-permute-start.2 = (s32[256]{0:T(256)S(1)}, s32[256]{0:T(256)S(1)}, u32[]{:S(2)}, u32[]{:S(2)}) collective-permute-start(s32[256]{0:T(256)S(1)} %bitcast.341), channel_id=1, source_target_pairs={{0,2},{1,3},{2,4},{3,5},{4,6},{5,7},{6,8},{7,9},{8,10},{9,11},{10,... | collective-permute-start | bytes 3080 | tf_op jit(solution)/shard_map/ppermute | solution.py:15
  9.8 37.9 %collective-permute-start.4 = (s32[256]{0:T(256)S(1)}, s32[256]{0:T(256)S(1)}, u32[]{:S(2)}, u32[]{:S(2)}) collective-permute-start(s32[256]{0:T(256)S(1)} %bitcast.342), channel_id=1, source_target_pairs={{0,3},{1,4},{2,5},{3,6},{4,7},{5,8},{6,9},{7,10},{8,11},{9,12},{10... | collective-permute-start | bytes 3080 | tf_op jit(solution)/shard_map/ppermute | solution.py:15
  12.0 37.9 %collective-permute-start.6 = (s32[256]{0:T(256)S(1)}, s32[256]{0:T(256)S(1)}, u32[]{:S(2)}, u32[]{:S(2)}) collective-permute-start(s32[256]{0:T(256)S(1)} %bitcast.343), channel_id=1, source_target_pairs={{0,4},{1,5},{2,6},{3,7},{4,8},{5,9},{6,10},{7,11},{8,12},{9,13},{1... | collective-permute-start | bytes 3080 | tf_op jit(solution)/shard_map/ppermute | solution.py:15
  17.1 5.8 %copy-start.10 = (bf16[1,256,1024]{2,1,0:T(8,128)(2,1)S(1)}, bf16[1,256,1024]{2,1,0:T(8,128)(2,1)}, u32[]{:S(2)}) copy-start(bf16[1,256,1024]{2,1,0:T(8,128)(2,1)} %param.7) | copy-start | bytes 1572868
  17.2 36.3 %copy-start.8 = (f32[256,2,256]{0,2,1:T(8,128)}, f32[256,2,256]{0,2,1:T(8,128)S(1)}, u32[]{:S(2)}) copy-start(f32[256,2,256]{0,2,1:T(8,128)S(1)} %get-tuple-element.52) | copy-start | bytes 1572868
  19.0 35.0 %collective-permute-start.7 = (bf16[256,512]{0,1:T(8,128)(2,1)}, bf16[256,512]{0,1:T(8,128)(2,1)S(1)}, u32[]{:S(2)}, u32[]{:S(2)}) collective-permute-start(bf16[256,512]{0,1:T(8,128)(2,1)} %fusion.45), channel_id=1, source_target_pairs={{0,4},{1,5},{2,6},{3,7},{4,8},{5,9},{6,10},{7,11},{8,12},{9,13},{1... | collective-permute-start | bytes 786440 | tf_op jit(solution)/shard_map/ppermute | solution.py:15
  24.3 4.8 %copy-start.6 = (f32[1,256,1024]{1,2,0:T(8,128)}, f32[1,256,1024]{1,2,0:T(8,128)S(1)}, u32[]{:S(2)}) copy-start(f32[1,256,1024]{1,2,0:T(8,128)S(1)} %copy.315) | copy-start | bytes 3145732
  29.9 2.0 copy-start.34
  37.7 20.5 %collective-permute-start.5 = (bf16[256,512]{0,1:T(8,128)(2,1)}, bf16[256,512]{0,1:T(8,128)(2,1)S(1)}, u32[]{:S(2)}, u32[]{:S(2)}) collective-permute-start(bf16[256,512]{0,1:T(8,128)(2,1)} %fusion.45), channel_id=1, source_target_pairs={{0,3},{1,4},{2,5},{3,6},{4,7},{5,8},{6,9},{7,10},{8,11},{9,12},{10... | collective-permute-start | bytes 786440 | tf_op jit(solution)/shard_map/ppermute | solution.py:15
  44.6 17.1 %collective-permute-start.3 = (bf16[256,512]{0,1:T(8,128)(2,1)}, bf16[256,512]{0,1:T(8,128)(2,1)S(1)}, u32[]{:S(2)}, u32[]{:S(2)}) collective-permute-start(bf16[256,512]{0,1:T(8,128)(2,1)} %fusion.45), channel_id=1, source_target_pairs={{0,2},{1,3},{2,4},{3,5},{4,6},{5,7},{6,8},{7,9},{8,10},{9,11},{10,... | collective-permute-start | bytes 786440 | tf_op jit(solution)/shard_map/ppermute | solution.py:15
  47.7 18.2 %collective-permute-start.1 = (bf16[256,512]{0,1:T(8,128)(2,1)}, bf16[256,512]{0,1:T(8,128)(2,1)S(1)}, u32[]{:S(2)}, u32[]{:S(2)}) collective-permute-start(bf16[256,512]{0,1:T(8,128)(2,1)} %fusion.45), channel_id=1, source_target_pairs={{0,1},{1,2},{2,3},{3,4},{4,5},{5,6},{6,7},{7,8},{8,9},{9,10},{10,1... | collective-permute-start | bytes 786440 | tf_op jit(solution)/shard_map/ppermute | solution.py:15
  50.0 19.3 %collective-permute-start.8 = (bf16[256,512]{1,0:T(8,128)(2,1)}, bf16[256,512]{1,0:T(8,128)(2,1)}, u32[]{:S(2)}, u32[]{:S(2)}) collective-permute-start(bf16[256,512]{1,0:T(8,128)(2,1)} %bitcast.22), channel_id=1, source_target_pairs={{0,1},{1,2},{2,3},{3,4},{4,5},{5,6},{6,7},{7,8},{8,9},{9,10},{10,1... | collective-permute-start | bytes 786440 | tf_op jit(solution)/shard_map/ppermute | solution.py:15
  53.5 13.3 %copy-start.18 = (pred[256,256]{0,1:T(8,128)(4,1)}, pred[256,256]{0,1:T(8,128)(4,1)S(1)}, u32[]{:S(2)}) copy-start(pred[256,256]{0,1:T(8,128)(4,1)S(1)} %get-tuple-element.57) | copy-start | bytes 196612
  53.5 13.3 %copy-start.20 = (pred[256,256]{0,1:T(8,128)(4,1)}, pred[256,256]{0,1:T(8,128)(4,1)S(1)}, u32[]{:S(2)}) copy-start(pred[256,256]{0,1:T(8,128)(4,1)S(1)} %get-tuple-element.55) | copy-start | bytes 196612
  53.9 2.9 copy-start.27
  54.0 20.2 %collective-permute-start.10 = (bf16[256,512]{1,0:T(8,128)(2,1)}, bf16[256,512]{1,0:T(8,128)(2,1)}, u32[]{:S(2)}, u32[]{:S(2)}) collective-permute-start(bf16[256,512]{1,0:T(8,128)(2,1)} %bitcast.22), channel_id=1, source_target_pairs={{0,3},{1,4},{2,5},{3,6},{4,7},{5,8},{6,9},{7,10},{8,11},{9,12},{10... | collective-permute-start | bytes 786440 | tf_op jit(solution)/shard_map/ppermute | solution.py:15
  58.2 3.5 %copy-start.29 = (bf16[256,512]{0,1:T(8,128)(2,1)}, bf16[256,512]{0,1:T(8,128)(2,1)S(1)}, u32[]{:S(2)}) copy-start(bf16[256,512]{0,1:T(8,128)(2,1)S(1)} %collective-permute-done.5) | copy-start | bytes 786436
  58.2 20.4 %collective-permute-start.11 = (bf16[256,512]{1,0:T(8,128)(2,1)}, bf16[256,512]{1,0:T(8,128)(2,1)}, u32[]{:S(2)}, u32[]{:S(2)}) collective-permute-start(bf16[256,512]{1,0:T(8,128)(2,1)} %bitcast.22), channel_id=1, source_target_pairs={{0,4},{1,5},{2,6},{3,7},{4,8},{5,9},{6,10},{7,11},{8,12},{9,13},{1... | collective-permute-start | bytes 786440 | tf_op jit(solution)/shard_map/ppermute | solution.py:15
  61.7 5.1 %copy-start = (f32[2,2,256,256]{2,3,1,0:T(8,128)}, f32[2,2,256,256]{2,3,1,0:T(8,128)S(1)}, u32[]{:S(2)}) copy-start(f32[2,2,256,256]{2,3,1,0:T(8,128)S(1)} %get-tuple-element.63) | copy-start | bytes 3145732
  61.7 4.2 %copy-start.25 = (bf16[256,512]{0,1:T(8,128)(2,1)}, bf16[256,512]{0,1:T(8,128)(2,1)S(1)}, u32[]{:S(2)}) copy-start(bf16[256,512]{0,1:T(8,128)(2,1)S(1)} %collective-permute-done.3) | copy-start | bytes 786436
  61.7 21.1 %collective-permute-start.9 = (bf16[256,512]{1,0:T(8,128)(2,1)}, bf16[256,512]{1,0:T(8,128)(2,1)}, u32[]{:S(2)}, u32[]{:S(2)}) collective-permute-start(bf16[256,512]{1,0:T(8,128)(2,1)} %bitcast.22), channel_id=1, source_target_pairs={{0,2},{1,3},{2,4},{3,5},{4,6},{5,7},{6,8},{7,9},{8,10},{9,11},{10,... | collective-permute-start | bytes 786440 | tf_op jit(solution)/shard_map/ppermute | solution.py:15
  65.9 1.8 copy-start.2
  66.8 1.2 copy-start.16
  94.7 1.8 copy-start.5
  94.7 1.8 copy-start.21
  94.7 1.8 copy-start.31
  94.7 1.8 copy-start.35
  96.5 1.2 copy-start.3
  96.5 1.3 copy-start.24
  98.2 1.2 copy-start.1
  98.2 1.2 copy-start.19
  98.2 1.3 copy-start.22
  106.6 27.6 %collective-permute-start.12 = (f32[2,256,512]{1,2,0:T(8,128)}, f32[2,256,512]{1,2,0:T(8,128)}, u32[]{:S(2)}, u32[]{:S(2)}) collective-permute-start(f32[2,256,512]{1,2,0:T(8,128)} %pad_maximum_fusion), channel_id=1, source_target_pairs={{1,0},{2,1},{3,2},{4,3},{5,4},{6,5},{7,6},{8,7},{9,8},{10,9},{11,1... | collective-permute-start | bytes 3145736 | tf_op jit(solution)/shard_map/ppermute | solution.py:15
  111.8 27.4 %collective-permute-start.13 = (f32[2,256,512]{1,2,0:T(8,128)}, f32[2,256,512]{1,2,0:T(8,128)}, u32[]{:S(2)}, u32[]{:S(2)}) collective-permute-start(f32[2,256,512]{1,2,0:T(8,128)} %pad_maximum_fusion.1), channel_id=1, source_target_pairs={{2,0},{3,1},{4,2},{5,3},{6,4},{7,5},{8,6},{9,7},{10,8},{11,9},{12,... | collective-permute-start | bytes 3145736 | tf_op jit(solution)/shard_map/ppermute | solution.py:15
  114.3 60.8 %collective-permute-start.14 = (f32[2,256,512]{1,2,0:T(8,128)}, f32[2,256,512]{1,2,0:T(8,128)}, u32[]{:S(2)}, u32[]{:S(2)}) collective-permute-start(f32[2,256,512]{1,2,0:T(8,128)} %pad_maximum_fusion.2), channel_id=1, source_target_pairs={{3,0},{4,1},{5,2},{6,3},{7,4},{8,5},{9,6},{10,7},{11,8},{12,9},{13... | collective-permute-start | bytes 3145736 | tf_op jit(solution)/shard_map/ppermute | solution.py:15
  115.6 2.7 copy-start.9
  115.6 2.7 copy-start.37
  116.6 2.0 copy-start.33
  116.6 66.5 %collective-permute-start.15 = (f32[2,256,512]{1,2,0:T(8,128)}, f32[2,256,512]{1,2,0:T(8,128)}, u32[]{:S(2)}, u32[]{:S(2)}) collective-permute-start(f32[2,256,512]{1,2,0:T(8,128)} %pad_maximum_fusion.3), channel_id=1, source_target_pairs={{4,0},{5,1},{6,2},{7,3},{8,4},{9,5},{10,6},{11,7},{12,8},{13,9},{1... | collective-permute-start | bytes 3145736 | tf_op jit(solution)/shard_map/ppermute | solution.py:15
  118.6 1.2 copy-start.7
  118.6 1.3 copy-start.26
  118.6 1.2 copy-start.41
  130.9 1.2 copy-start.14
  130.9 1.5 copy-start.15
  131.2 1.4 copy-start.11
  131.2 1.7 copy-start.13
  131.3 1.7 copy-start.39
  (11 other events, 9.3 us)
where the time goes:
time: 297 us; the launch traced here: 294 us
  blocking collectives  105 us (35%)
  starting transfers between devices  51.9 us (17%)
  waiting for transfers between devices  49 us (16%)
  local copies, waits for them, and re-layouts  43.6 us (15%)
  matrix products  26.3 us (9%)
  other arithmetic  17.1 us (6%)
    psum x1, blocking collectives, per_device(): lax.psum((query_part_gain, key_part_gain), ('dp', 'seq'))  105 us
    ppermute x16, starting transfers between devices, from_behind(): return lax.ppermute(value, axis, pairs)  51.9 us
    ppermute x16, waiting for transfers between devices, from_behind(): return lax.ppermute(value, axis, pairs)  49 us
    unnamed x96, local copies, waits for them, and re-layouts  17.6 us
    dot_general x5, matrix products, weigh_shard(): jnp.einsum('hgqk,khd->qhgd', weights, value_block, preferred_element_type...  12.9 us
    ppermute x4, local copies, waits for them, and re-layouts, from_behind(): return lax.ppermute(value, axis, pairs)  7.2 us
  transfers between devices with their start and end apart: 16, of which 3 were waited for; matrix products, arithmetic and copies ran while one was open for 18% of the time, Pallas kernels for 0%

commit v1 on v0

v1 whole, which is shorter than its diff:
```python
import jax
import jax.numpy as jnp
from jax import lax
from jax.experimental import pallas as pl
from jax.experimental.pallas import tpu as pltpu
from jax.sharding import Mesh
from jax.sharding import PartitionSpec as P

HEAD = 256
ROWS = 256
REACH = 4
BLOCKS = 6
EXTRA = 16
SCALE = HEAD**-0.5
EPSILON = 1e-06
SEQ = ("y", "z", "x", "core")
f32, bf16 = jnp.float32, jnp.bfloat16


def norm_rows(raw):
    rows = raw.astype(f32)
    inverse = lax.rsqrt(jnp.mean(rows * rows, axis=-1, keepdims=True) + EPSILON)
    return rows * inverse, inverse


def norm_backward(upstream, unit, inverse, gain):
    scaled = upstream * gain
    inner = jnp.mean(scaled * unit, axis=-1, keepdims=True)
    return inverse * (scaled - unit * inner)


def dot(a, b, dims=((1,), (0,))):
    return lax.dot_general(a, b, (dims, ((), ())), preferred_element_type=f32)


def attention_kernel(
    q_gain, k_gain, qg_own, qg_peer, kv_own, kv_peer, kv_one, kv_one_x, kv_two, kv_two_x,
    attended, q_grad, swap, kv_grad_own, kv_grad_one, kv_grad_two, gains,
    key, key_t, value, value_t, tag, key_grad, value_grad, score, query, upstream, upstream_t,
):
    core = lax.axis_index("core")
    parts = (
        (kv_two, core), (kv_two_x, 1 - core), (kv_one, 2 + core), (kv_one_x, 3 - core),
        (kv_own, 4 + core), (kv_peer, 5 - core),
    )
    for part, block in parts:
        unit, _ = norm_rows(part[:ROWS, :HEAD])
        normed = (unit * k_gain[...]).astype(bf16)
        key[block] = normed
        key_t[block] = normed.T
        value[block] = part[:ROWS, HEAD:]
        value_t[block] = part[:ROWS, HEAD:].T
        ids = part[ROWS : ROWS + EXTRA, :ROWS].astype(f32)[:1]
        tag[block] = jnp.broadcast_to(ids, (128, ROWS)).T
        key_grad[block] = jnp.zeros((ROWS, HEAD), f32)
        value_grad[block] = jnp.zeros((ROWS, HEAD), f32)

    key_at = lax.broadcasted_iota(jnp.int32, (ROWS, 2 * ROWS), 0)
    query_at = lax.broadcasted_iota(jnp.int32, (ROWS, 2 * ROWS), 1) % ROWS
    q_gain_grad = jnp.zeros((1, HEAD), f32)

    for qg, tags, first, att_out, grad_out in (
        (qg_own, kv_own, core, attended, q_grad),
        (qg_peer, kv_peer, 1 - core, swap.at[:, : 2 * HEAD], swap.at[:, 2 * HEAD :]),
    ):
        for h in range(2):
            unit, _ = norm_rows(qg[:, h * HEAD : (h + 1) * HEAD])
            normed = (unit * q_gain[...]).astype(bf16)
            query[h * ROWS : (h + 1) * ROWS] = normed * jnp.asarray(SCALE, bf16)
            up = qg[:, (2 + h) * HEAD : (3 + h) * HEAD]
            upstream[h * ROWS : (h + 1) * ROWS] = up
            upstream_t[:, h * ROWS : (h + 1) * ROWS] = up.T
        ids = tags[ROWS : ROWS + EXTRA, :ROWS].astype(f32)[:1]
        query_tag = jnp.concatenate([ids, ids], axis=1)

        top = None
        for t in range(REACH + 1):
            scores = dot(key[first + t], query[...], ((1,), (1,)))
            allowed = tag[first + t][:, :1] == query_tag
            if t == 0:
                allowed = allowed & (query_at < key_at)
            if t == REACH:
                allowed = allowed & (query_at >= key_at)
            scores = jnp.where(allowed, scores, -1e30)
            score[t] = scores
            here = jnp.max(scores, axis=0, keepdims=True)
            top = here if top is None else jnp.maximum(top, here)
        total = jnp.zeros((1, 2 * ROWS), f32)
        for t in range(REACH + 1):
            powers = jnp.exp(score[t] - top)
            score[t] = powers
            total = total + jnp.sum(powers, axis=0, keepdims=True)
        share = 1.0 / total
        att_t = jnp.zeros((HEAD, 2 * ROWS), f32)
        for t in range(REACH + 1):
            probs = score[t] * share
            score[t] = probs
            weights = probs.astype(bf16)
            att_t = att_t + dot(value_t[first + t], weights)
            value_grad[first + t] += dot(weights, upstream[...])
        att_t = att_t.astype(bf16).astype(f32)
        delta = jnp.sum(att_t * upstream_t[...].astype(f32), axis=0, keepdims=True)
        grad_t = jnp.zeros((HEAD, 2 * ROWS), f32)
        for t in range(REACH + 1):
            prob_grads = dot(value[first + t], upstream_t[...])
            score_grads = (score[t] * (prob_grads - delta)).astype(bf16)
            grad_t = grad_t + dot(key_t[first + t], score_grads)
            key_grad[first + t] += dot(score_grads, query[...])
        for h in range(2):
            att_out[:, h * HEAD : (h + 1) * HEAD] = att_t[:, h * ROWS : (h + 1) * ROWS].T.astype(bf16)
            normed_grad = grad_t[:, h * ROWS : (h + 1) * ROWS].T * SCALE
            unit, inverse = norm_rows(qg[:, h * HEAD : (h + 1) * HEAD])
            q_gain_grad = q_gain_grad + jnp.sum(normed_grad * unit, axis=0, keepdims=True)
            grad_out[:, h * HEAD : (h + 1) * HEAD] = norm_backward(
                normed_grad, unit, inverse, q_gain[...]
            ).astype(bf16)

    k_gain_grad = jnp.zeros((1, HEAD), f32)
    for part, block in parts:
        unit, _ = norm_rows(part[:ROWS, :HEAD])
        k_gain_grad = k_gain_grad + jnp.sum(key_grad[block] * unit, axis=0, keepdims=True)
    gains[...] = jnp.concatenate([q_gain_grad, k_gain_grad], axis=1)
    for i in range(2):
        for at, out in ((0, kv_grad_two), (2, kv_grad_one), (4, kv_grad_own)):
            out[i, :, :HEAD] = key_grad[at + i].astype(out.dtype)
            out[i, :, HEAD:] = value_grad[at + i].astype(out.dtype)


def finish_kernel(k_gain, kv_own, kv_peer, grad_own, grad_one, grad_two, own, peer):
    core = lax.axis_index("core")
    for part, block, out in ((kv_own, core, own), (kv_peer, 1 - core, peer)):
        total = grad_own[block] + grad_one[block].astype(f32) + grad_two[block].astype(f32)
        unit, inverse = norm_rows(part[:ROWS, :HEAD])
        out[:, :HEAD] = norm_backward(total[:, :HEAD], unit, inverse, k_gain[...]).astype(bf16)
        out[:, HEAD:] = total[:, HEAD:].astype(bf16)


def vmem(count):
    return [pl.BlockSpec(memory_space=pltpu.VMEM)] * count


def attention(*operands):
    shape = jax.ShapeDtypeStruct
    return pl.pallas_call(
        attention_kernel,
        out_shape=(
            shape((ROWS, 2 * HEAD), bf16),
            shape((ROWS, 2 * HEAD), bf16),
            shape((ROWS, 4 * HEAD), bf16),
            shape((2, ROWS, 2 * HEAD), f32),
            shape((2, ROWS, 2 * HEAD), bf16),
            shape((2, ROWS, 2 * HEAD), bf16),
            shape((1, 2 * HEAD), f32),
        ),
        in_specs=vmem(len(operands)),
        out_specs=tuple(vmem(7)),
        scratch_shapes=[
            pltpu.VMEM((BLOCKS, ROWS, HEAD), bf16),
            pltpu.VMEM((BLOCKS, HEAD, ROWS), bf16),
            pltpu.VMEM((BLOCKS, ROWS, HEAD), bf16),
            pltpu.VMEM((BLOCKS, HEAD, ROWS), bf16),
            pltpu.VMEM((BLOCKS, ROWS, 128), f32),
            pltpu.VMEM((BLOCKS, ROWS, HEAD), f32),
            pltpu.VMEM((BLOCKS, ROWS, HEAD), f32),
            pltpu.VMEM((REACH + 1, ROWS, 2 * ROWS), f32),
            pltpu.VMEM((2 * ROWS, HEAD), bf16),
            pltpu.VMEM((2 * ROWS, HEAD), bf16),
            pltpu.VMEM((HEAD, 2 * ROWS), bf16),
        ],
        compiler_params=pltpu.CompilerParams(vmem_limit_bytes=40 << 20),
        cost_estimate=pl.CostEstimate(
            flops=8 << 30, bytes_accessed=8 << 20, transcendentals=3 << 20
        ),
        name="attention",
    )(*operands)


def finish(*operands):
    return pl.pallas_call(
        finish_kernel,
        out_shape=(jax.ShapeDtypeStruct((ROWS, 2 * HEAD), bf16),) * 2,
        in_specs=vmem(len(operands)),
        out_specs=tuple(vmem(2)),
        compiler_params=pltpu.CompilerParams(vmem_limit_bytes=16 << 20),
        name="finish",
    )(*operands)


def per_device(query_raw, unnormalized_keys, values, output_gradient, query_gain, key_gain, document_ids):
    queries, keys, values, upstream = query_raw[0], unnormalized_keys[0], values[0], output_gradient[0]
    core = lax.axis_index("core")
    shards = 1
    for name in SEQ:
        shards *= lax.axis_size(name)
    wide = 2 * HEAD

    def hop(array, chips, cross=False):
        pairs = [(i, (i ^ cross) + 2 * chips) for i in range(shards)]
        return lax.ppermute(array, SEQ, [(i, j) for i, j in pairs if 0 <= j < shards])

    def swap(array):
        return lax.ppermute(array, "core", [(0, 1), (1, 0)])

    first = core == 0
    ids = jnp.pad((document_ids[0] + 1).astype(bf16)[None], ((0, EXTRA - 1), (0, wide - ROWS)))

    def pack(mine):
        return jnp.concatenate(
            [
                jnp.concatenate(
                    [jnp.where(mine, a[:, :HEAD], a[:, HEAD:]) for a in (keys, values)], axis=1
                ),
                ids,
            ],
            axis=0,
        )

    kv_mine, kv_other = pack(first), pack(~first)

    def pack_queries(mine):
        return jnp.concatenate(
            [jnp.where(mine, a[:, :wide], a[:, wide:]) for a in (queries, upstream)], axis=1
        )

    qg_mine, qg_other = pack_queries(first), pack_queries(~first)
    kv_two, kv_two_x = hop(kv_mine, 2), hop(kv_other, 2, True)
    kv_one, kv_one_x = hop(kv_mine, 1), hop(kv_other, 1, True)
    kv_peer, qg_peer = swap(kv_other), swap(qg_other)
    q_gain, k_gain = query_gain[None], key_gain[None]
    attended, q_grad, to_peer, grad_own, grad_one, grad_two, gains = attention(
        q_gain, k_gain, qg_mine, qg_peer, kv_mine, kv_peer, kv_one, kv_one_x, kv_two, kv_two_x
    )
    grad_two, grad_one = hop(grad_two, -2), hop(grad_one, -1)
    from_peer = swap(to_peer)
    for axes in (("z",), ("y",), ("x", "core"), ("dp",)):
        gains = lax.optimization_barrier(lax.psum(gains, axes))
    kv_grad, kv_grad_peer = finish(k_gain, kv_mine, kv_peer, grad_own, grad_one, grad_two)
    kv_grad_x = swap(kv_grad_peer)

    def join(mine, other):
        return jnp.concatenate([jnp.where(first, mine, other), jnp.where(first, other, mine)], axis=1)[None]

    return (
        join(attended, from_peer[:, :wide]),
        join(q_grad, from_peer[:, wide:]),
        join(kv_grad[:, :HEAD], kv_grad_x[:, :HEAD]),
        join(kv_grad[:, HEAD:], kv_grad_x[:, HEAD:]),
        gains[0, :HEAD],
        gains[0, HEAD:],
    )


def solution(mesh):
    parts, shards = mesh.devices.shape
    z = min(8, shards // 4)
    fine = Mesh(mesh.devices.reshape(parts, shards // (4 * z), z, 2, 2), ("dp", *SEQ))
    rows, ids = P("dp", SEQ, None), P("dp", SEQ)
    return jax.shard_map(
        per_device,
        mesh=fine,
        in_specs=(rows, rows, rows, rows, P(), P(), ids),
        out_specs=(rows, rows, rows, rows, P(), P()),
        check_vma=False,
    )
```

time: 297 us -> 124 us (0.42)
  waiting for transfers between devices: 49 us -> 5.09 us
  local copies, waits for them, and re-layouts: 43.6 us -> 1.94 us
  blocking collectives: 105 us -> 68.9 us
  matrix products: 26.3 us -> 0 us
  starting transfers between devices: 51.9 us -> 30.8 us
  other arithmetic: 17.1 us -> 5.71 us
  Pallas kernels: 0 us -> 10.2 us
    ppermute x16 -> x10, waiting for transfers between devices: 49 us -> 5.09 us  [the longest x6 5.08 us: hop(): lax.ppermute(array, SEQ, [(i, j) for i, j in pairs if 0 <= j < shards])]
    psum x1 -> x4, blocking collectives: 105 us -> 68.9 us  [per_device(): gains = lax.optimization_barrier(lax.psum(gains, axes))]
    dot_general x30 -> x0, matrix products: 26.3 us -> none  [the longest x5 12.9 us: weigh_shard(): jnp.einsum('hgqk,khd->qhgd', weights, value_block, preferred_element_type...]
    ppermute x16 -> x10, starting transfers between devices: 51.9 us -> 30.8 us  [the longest x6 16.8 us: hop(): lax.ppermute(array, SEQ, [(i, j) for i, j in pairs if 0 <= j < shards])]
    unnamed x96 -> x10, local copies, waits for them, and re-layouts: 17.6 us -> 1.37 us
    mul x5 -> x0, local copies, waits for them, and re-layouts: 11.2 us -> none  [the longest x2 4.1 us: backward_norm(): unit_rows * inner_mean]
    pallas_call x0 -> x2, Pallas kernels: none -> 10.2 us  [the longest x1 9.83 us: attention(): pl.pallas_call(attention_kernel, out_shape=(shape((ROWS, 2 * HEAD), bf16)...]
    ppermute x4 -> x0, local copies, waits for them, and re-layouts: 7.2 us -> none  [from_behind(): return lax.ppermute(value, axis, pairs)]
  transfers between devices with their start and end apart: 16 -> 10, of which waited for: 3 -> 2; matrix products, arithmetic and copies ran while one was open for 18% -> 3% of each run, Pallas kernels for 0% -> 0%
where the time goes in v1:
time: 124 us; the launch traced here: 123 us
  blocking collectives  68.9 us (56%)
  starting transfers between devices  30.8 us (25%)
  Pallas kernels  10.2 us (8%)
  other arithmetic  5.71 us (5%)
  waiting for transfers between devices  5.09 us (4%)
  local copies, waits for them, and re-layouts  1.94 us (2%)
    psum x4, blocking collectives, per_device(): gains = lax.optimization_barrier(lax.psum(gains, axes))  68.9 us
    ppermute x6, starting transfers between devices, hop(): lax.ppermute(array, SEQ, [(i, j) for i, j in pairs if 0 <= j < shards])  16.8 us
    ppermute x4, starting transfers between devices, swap(): return lax.ppermute(array, 'core', [(0, 1), (1, 0)])  13.9 us
    pallas_call x1, Pallas kernels, attention(): pl.pallas_call(attention_kernel, out_shape=(shape((ROWS, 2 * HEAD), bf16)...  9.83 us
    ppermute x6, waiting for transfers between devices, hop(): lax.ppermute(array, SEQ, [(i, j) for i, j in pairs if 0 <= j < shards])  5.08 us
    broadcast_in_dim x4, other arithmetic, join(): jnp.concatenate([jnp.where(first, mine, other), jnp.where(first, other, m...  3.17 us
  transfers between devices with their start and end apart: 10, of which 2 were waited for; matrix products, arithmetic and copies ran while one was open for 3% of the time, Pallas kernels for 0%

profile of v1, /device:TPU:1, one launch (start us, length us, event | category | flops | bytes accessed | tf_op | source)
XLA Modules:
  0.0 123.4 jit_solution(17027577735712786720)
XLA Ops:
  0.6 0.0 copy-start.4
  0.6 0.7 copy-done.4
  1.3 1.1 broadcast_select_fusion.8
  2.5 0.0 copy-start.2
  2.5 0.0 copy-start.3
  2.5 5.5 %collective-permute-start.5 = (bf16[272,512]{1,0:T(8,128)(2,1)S(1)}, bf16[272,512]{1,0:T(8,128)(2,1)S(1)}, u32[]{:S(2)}, u32[]{:S(2)}) collective-permute-start(bf16[272,512]{1,0:T(8,128)(2,1)S(1)} %get-tuple-element.44), channel_id=1, source_target_pairs={{0,5},{1,4},{2,7},{3,6},{4,9},{5,8},{6,11},{7,10},{8,13},{9,12},{1... | collective-permute-start | bytes 835592 | tf_op jit(solution)/shard_map/ppermute | solution.py:199
  8.1 0.0 copy-done.2
  8.1 0.0 copy-done.3
  8.1 0.1 broadcast_select_fusion
  8.2 0.1 pad_maximum_fusion.1
  8.2 4.7 %collective-permute-start = (bf16[256,1024]{1,0:T(8,128)(2,1)S(1)}, bf16[256,1024]{1,0:T(8,128)(2,1)S(1)}, u32[]{:S(2)}, u32[]{:S(2)}) collective-permute-start(bf16[256,1024]{1,0:T(8,128)(2,1)S(1)} %pad_maximum_fusion.1), channel_id=1, source_target_pairs={{0,1},{1,0},{2,3},{3,2},{4,5},{5,4},{6,7},{7,6},{8,9},{9,8},{10,11... | collective-permute-start | bytes 1572872 | tf_op jit(solution)/shard_map/ppermute | solution.py:202
  12.9 1.3 %collective-permute-start.3 = (bf16[272,512]{1,0:T(8,128)(2,1)S(1)}, bf16[272,512]{1,0:T(8,128)(2,1)S(1)}, u32[]{:S(2)}, u32[]{:S(2)}) collective-permute-start(bf16[272,512]{1,0:T(8,128)(2,1)S(1)} %get-tuple-element.44), channel_id=1, source_target_pairs={{0,3},{1,2},{2,5},{3,4},{4,7},{5,6},{6,9},{7,8},{8,11},{9,10},{10,... | collective-permute-start | bytes 835592 | tf_op jit(solution)/shard_map/ppermute | solution.py:199
  14.3 1.9 %collective-permute-start.1 = (bf16[272,512]{1,0:T(8,128)(2,1)S(1)}, bf16[272,512]{1,0:T(8,128)(2,1)S(1)}, u32[]{:S(2)}, u32[]{:S(2)}) collective-permute-start(bf16[272,512]{1,0:T(8,128)(2,1)S(1)} %get-tuple-element.44), channel_id=1, source_target_pairs={{0,1},{1,0},{2,3},{3,2},{4,5},{5,4},{6,7},{7,6},{8,9},{9,8},{10,11... | collective-permute-start | bytes 835592 | tf_op jit(solution)/shard_map/ppermute | solution.py:202
  16.2 3.4 %collective-permute-start.4 = (bf16[272,512]{1,0:T(8,128)(2,1)S(1)}, bf16[272,512]{1,0:T(8,128)(2,1)S(1)}, u32[]{:S(2)}, u32[]{:S(2)}) collective-permute-start(bf16[272,512]{1,0:T(8,128)(2,1)S(1)} %get-tuple-element.45.kv_own), channel_id=1, source_target_pairs={{0,4},{1,5},{2,6},{3,7},{4,8},{5,9},{6,10},{7,11},{8,12},{9,13},{1... | collective-permute-start | bytes 835592 | tf_op jit(solution)/shard_map/ppermute | solution.py:199
  19.6 0.0 collective-permute-done.5.kv_two_x
  19.6 4.0 %collective-permute-start.2 = (bf16[272,512]{1,0:T(8,128)(2,1)S(1)}, bf16[272,512]{1,0:T(8,128)(2,1)S(1)}, u32[]{:S(2)}, u32[]{:S(2)}) collective-permute-start(bf16[272,512]{1,0:T(8,128)(2,1)S(1)} %get-tuple-element.45.kv_own), channel_id=1, source_target_pairs={{0,2},{1,3},{2,4},{3,5},{4,6},{5,7},{6,8},{7,9},{8,10},{9,11},{10,... | collective-permute-start | bytes 835592 | tf_op jit(solution)/shard_map/ppermute | solution.py:199
  23.6 0.0 copy-start.1
  23.6 0.1 pad_maximum_fusion.qg_own
  23.7 0.0 collective-permute-done.3.kv_one_x
  23.7 0.0 collective-permute-done.1.kv_peer
  23.7 1.4 %collective-permute-done.4.kv_two = bf16[272,512]{1,0:T(8,128)(2,1)S(1)} collective-permute-done((bf16[272,512]{1,0:T(8,128)(2,1)S(1)}, bf16[272,512]{1,0:T(8,128)(2,1)S(1)}, u32[]{:S(2)}, u32[]{:S(2)}) %collective-permute-start.4) | collective-permute-done | bytes 278560 | tf_op jit(solution)/shard_map/ppermute | solution.py:199
  25.1 3.7 %collective-permute-done.2.kv_one = bf16[272,512]{1,0:T(8,128)(2,1)S(1)} collective-permute-done((bf16[272,512]{1,0:T(8,128)(2,1)S(1)}, bf16[272,512]{1,0:T(8,128)(2,1)S(1)}, u32[]{:S(2)}, u32[]{:S(2)}) %collective-permute-start.2) | collective-permute-done | bytes 278560 | tf_op jit(solution)/shard_map/ppermute | solution.py:199
  28.8 0.0 collective-permute-done.qg_peer
  28.8 0.0 copy-start
  28.8 0.0 copy-done.1
  28.8 0.7 copy-done
  29.5 9.8 %attention.1 = (bf16[256,512]{1,0:T(8,128)(2,1)S(1)}, bf16[256,512]{1,0:T(8,128)(2,1)S(1)}, bf16[256,1024]{1,0:T(8,128)(2,1)}, f32[2,256,512]{2,1,0:T(8,128)S(1)...) custom-call(f32[1,256]{1,0:T(1,128)S(1)} %bitcast.18, f32[1,256]{1,0:T(1,128)S(1)} %bitcast.16, ...), custom_call_target="tpu_custom_call" | custom-call | flops 8589934592 | bytes 8388608 | tf_op jit(solution)/shard_map/attention/pallas_call | solution.py:144
  39.3 1.3 %collective-permute-start.7 = (bf16[2,256,512]{2,1,0:T(8,128)(2,1)}, bf16[2,256,512]{2,1,0:T(8,128)(2,1)S(1)}, u32[]{:S(2)}, u32[]{:S(2)}) collective-permute-start(bf16[2,256,512]{2,1,0:T(8,128)(2,1)} %get-tuple-element.19), channel_id=1, source_target_pairs={{2,0},{3,1},{4,2},{5,3},{6,4},{7,5},{8,6},{9,7},{10,8},{11,9},{12,... | collective-permute-start | bytes 1572872 | tf_op jit(solution)/shard_map/ppermute | solution.py:199
  40.6 1.3 %collective-permute-start.8 = (bf16[2,256,512]{2,1,0:T(8,128)(2,1)}, bf16[2,256,512]{2,1,0:T(8,128)(2,1)S(1)}, u32[]{:S(2)}, u32[]{:S(2)}) collective-permute-start(bf16[2,256,512]{2,1,0:T(8,128)(2,1)} %get-tuple-element.20), channel_id=1, source_target_pairs={{4,0},{5,1},{6,2},{7,3},{8,4},{9,5},{10,6},{11,7},{12,8},{13,9},{1... | collective-permute-start | bytes 1572872 | tf_op jit(solution)/shard_map/ppermute | solution.py:199
  41.9 3.5 %collective-permute-start.6 = (bf16[256,1024]{1,0:T(8,128)(2,1)}, bf16[256,1024]{1,0:T(8,128)(2,1)}, u32[]{:S(2)}, u32[]{:S(2)}) collective-permute-start(bf16[256,1024]{1,0:T(8,128)(2,1)} %get-tuple-element.16), channel_id=1, source_target_pairs={{0,1},{1,0},{2,3},{3,2},{4,5},{5,4},{6,7},{7,6},{8,9},{9,8},{10,11... | collective-permute-start | bytes 1572872 | tf_op jit(solution)/shard_map/ppermute | solution.py:202
  45.4 37.6 %psum.28 = f32[1,512]{1,0:T(1,128)S(1)} all-reduce(f32[1,512]{1,0:T(1,128)S(1)} %get-tuple-element.23), channel_id=1, replica_groups=mesh['dp'=2,'y'=8,'z'=8,'x'=2,'core'=2] {'z'}, use_global_device_ids=true, to_apply=%region_0.1 | all-reduce | flops 512 | bytes 4096 | tf_op jit(solution)/shard_map/psum | solution.py:236
  83.0 14.2 %psum.29 = f32[1,512]{1,0:T(1,128)S(1)} all-reduce(f32[1,512]{1,0:T(1,128)S(1)} %psum.28), channel_id=1, replica_groups=mesh['dp'=2,'y'=8,'z'=8,'x'=2,'core'=2] {'y'}, use_global_device_ids=true, to_apply=%region_1.2 | all-reduce | flops 512 | bytes 4096 | tf_op jit(solution)/shard_map/psum | solution.py:236
  97.2 11.8 %psum.30 = f32[1,512]{1,0:T(1,128)S(1)} all-reduce(f32[1,512]{1,0:T(1,128)S(1)} %psum.29), channel_id=1, replica_groups=mesh['dp'=2,'y'=8,'z'=8,'x'=2,'core'=2] {'x','core'}, use_global_device_ids=true, to_apply=%region_2.3 | all-reduce | flops 512 | bytes 4096 | tf_op jit(solution)/shard_map/psum | solution.py:236
  109.0 5.3 %psum.31 = f32[1,512]{1,0:T(1,128)S(1)} all-reduce(f32[1,512]{1,0:T(1,128)S(1)} %psum.30), channel_id=1, replica_groups=mesh['dp'=2,'y'=8,'z'=8,'x'=2,'core'=2] {'dp'}, use_global_device_ids=true, to_apply=%region_3.4 | all-reduce | flops 512 | bytes 4096 | tf_op jit(solution)/shard_map/psum | solution.py:236
  114.3 0.6 fusion.3
  114.9 0.0 collective-permute-done.7.grad_one
  114.9 0.0 collective-permute-done.8.grad_two
  114.9 0.4 finish.1
  115.3 3.8 %collective-permute-start.9 = (bf16[256,512]{1,0:T(8,128)(2,1)S(1)}, bf16[256,512]{1,0:T(8,128)(2,1)S(1)}, u32[]{:S(2)}, u32[]{:S(2)}) collective-permute-start(bf16[256,512]{1,0:T(8,128)(2,1)S(1)} %get-tuple-element.22), channel_id=1, source_target_pairs={{0,1},{1,0},{2,3},{3,2},{4,5},{5,4},{6,7},{7,6},{8,9},{9,8},{10,11... | collective-permute-start | bytes 786440 | tf_op jit(solution)/shard_map/ppermute | solution.py:202
  119.1 0.0 collective-permute-done.6
  119.1 1.1 broadcast_select_fusion.3
  120.2 0.9 maximum_bitcast_fusion.1
  121.0 0.9 maximum_bitcast_fusion
  121.9 0.0 collective-permute-done.9
  121.9 0.1 broadcast_select_fusion.11
  122.0 0.7 maximum_bitcast_fusion.3
  122.7 0.7 maximum_bitcast_fusion.2
  (2 shorter events, 0.0 us)
Async XLA Ops:
  0.6 0.7 copy-start.4
  2.5 5.6 %copy-start.2 = (bf16[1,256,1024]{2,1,0:T(8,128)(2,1)S(1)}, bf16[1,256,1024]{2,1,0:T(8,128)(2,1)}, u32[]{:S(2)}) copy-start(bf16[1,256,1024]{2,1,0:T(8,128)(2,1)} %param.10) | copy-start | bytes 1572868
  2.5 5.6 %copy-start.3 = (bf16[1,256,1024]{2,1,0:T(8,128)(2,1)S(1)}, bf16[1,256,1024]{2,1,0:T(8,128)(2,1)}, u32[]{:S(2)}) copy-start(bf16[1,256,1024]{2,1,0:T(8,128)(2,1)} %param.7) | copy-start | bytes 1572868
  2.5 17.1 %collective-permute-start.5 = (bf16[272,512]{1,0:T(8,128)(2,1)S(1)}, bf16[272,512]{1,0:T(8,128)(2,1)S(1)}, u32[]{:S(2)}, u32[]{:S(2)}) collective-permute-start(bf16[272,512]{1,0:T(8,128)(2,1)S(1)} %get-tuple-element.44), channel_id=1, source_target_pairs={{0,5},{1,4},{2,7},{3,6},{4,9},{5,8},{6,11},{7,10},{8,13},{9,12},{1... | collective-permute-start | bytes 835592 | tf_op jit(solution)/shard_map/ppermute | solution.py:199
  8.2 20.6 %collective-permute-start = (bf16[256,1024]{1,0:T(8,128)(2,1)S(1)}, bf16[256,1024]{1,0:T(8,128)(2,1)S(1)}, u32[]{:S(2)}, u32[]{:S(2)}) collective-permute-start(bf16[256,1024]{1,0:T(8,128)(2,1)S(1)} %pad_maximum_fusion.1), channel_id=1, source_target_pairs={{0,1},{1,0},{2,3},{3,2},{4,5},{5,4},{6,7},{7,6},{8,9},{9,8},{10,11... | collective-permute-start | bytes 1572872 | tf_op jit(solution)/shard_map/ppermute | solution.py:202
  12.9 10.8 %collective-permute-start.3 = (bf16[272,512]{1,0:T(8,128)(2,1)S(1)}, bf16[272,512]{1,0:T(8,128)(2,1)S(1)}, u32[]{:S(2)}, u32[]{:S(2)}) collective-permute-start(bf16[272,512]{1,0:T(8,128)(2,1)S(1)} %get-tuple-element.44), channel_id=1, source_target_pairs={{0,3},{1,2},{2,5},{3,4},{4,7},{5,6},{6,9},{7,8},{8,11},{9,10},{10,... | collective-permute-start | bytes 835592 | tf_op jit(solution)/shard_map/ppermute | solution.py:199
  14.3 9.5 %collective-permute-start.1 = (bf16[272,512]{1,0:T(8,128)(2,1)S(1)}, bf16[272,512]{1,0:T(8,128)(2,1)S(1)}, u32[]{:S(2)}, u32[]{:S(2)}) collective-permute-start(bf16[272,512]{1,0:T(8,128)(2,1)S(1)} %get-tuple-element.44), channel_id=1, source_target_pairs={{0,1},{1,0},{2,3},{3,2},{4,5},{5,4},{6,7},{7,6},{8,9},{9,8},{10,11... | collective-permute-start | bytes 835592 | tf_op jit(solution)/shard_map/ppermute | solution.py:202
  16.2 8.9 %collective-permute-start.4 = (bf16[272,512]{1,0:T(8,128)(2,1)S(1)}, bf16[272,512]{1,0:T(8,128)(2,1)S(1)}, u32[]{:S(2)}, u32[]{:S(2)}) collective-permute-start(bf16[272,512]{1,0:T(8,128)(2,1)S(1)} %get-tuple-element.45.kv_own), channel_id=1, source_target_pairs={{0,4},{1,5},{2,6},{3,7},{4,8},{5,9},{6,10},{7,11},{8,12},{9,13},{1... | collective-permute-start | bytes 835592 | tf_op jit(solution)/shard_map/ppermute | solution.py:199
  19.6 9.2 %collective-permute-start.2 = (bf16[272,512]{1,0:T(8,128)(2,1)S(1)}, bf16[272,512]{1,0:T(8,128)(2,1)S(1)}, u32[]{:S(2)}, u32[]{:S(2)}) collective-permute-start(bf16[272,512]{1,0:T(8,128)(2,1)S(1)} %get-tuple-element.45.kv_own), channel_id=1, source_target_pairs={{0,2},{1,3},{2,4},{3,5},{4,6},{5,7},{6,8},{7,9},{8,10},{9,11},{10,... | collective-permute-start | bytes 835592 | tf_op jit(solution)/shard_map/ppermute | solution.py:199
  23.6 5.2 %copy-start.1 = (f32[256]{0:T(256)S(1)}, f32[256]{0:T(256)}, u32[]{:S(2)}) copy-start(f32[256]{0:T(256)} %param.11) | copy-start | bytes 3076
  28.8 0.7 copy-start
  39.3 75.6 %collective-permute-start.7 = (bf16[2,256,512]{2,1,0:T(8,128)(2,1)}, bf16[2,256,512]{2,1,0:T(8,128)(2,1)S(1)}, u32[]{:S(2)}, u32[]{:S(2)}) collective-permute-start(bf16[2,256,512]{2,1,0:T(8,128)(2,1)} %get-tuple-element.19), channel_id=1, source_target_pairs={{2,0},{3,1},{4,2},{5,3},{6,4},{7,5},{8,6},{9,7},{10,8},{11,9},{12,... | collective-permute-start | bytes 1572872 | tf_op jit(solution)/shard_map/ppermute | solution.py:199
  40.6 74.3 %collective-permute-start.8 = (bf16[2,256,512]{2,1,0:T(8,128)(2,1)}, bf16[2,256,512]{2,1,0:T(8,128)(2,1)S(1)}, u32[]{:S(2)}, u32[]{:S(2)}) collective-permute-start(bf16[2,256,512]{2,1,0:T(8,128)(2,1)} %get-tuple-element.20), channel_id=1, source_target_pairs={{4,0},{5,1},{6,2},{7,3},{8,4},{9,5},{10,6},{11,7},{12,8},{13,9},{1... | collective-permute-start | bytes 1572872 | tf_op jit(solution)/shard_map/ppermute | solution.py:199
  41.9 77.2 %collective-permute-start.6 = (bf16[256,1024]{1,0:T(8,128)(2,1)}, bf16[256,1024]{1,0:T(8,128)(2,1)}, u32[]{:S(2)}, u32[]{:S(2)}) collective-permute-start(bf16[256,1024]{1,0:T(8,128)(2,1)} %get-tuple-element.16), channel_id=1, source_target_pairs={{0,1},{1,0},{2,3},{3,2},{4,5},{5,4},{6,7},{7,6},{8,9},{9,8},{10,11... | collective-permute-start | bytes 1572872 | tf_op jit(solution)/shard_map/ppermute | solution.py:202
  115.3 6.7 %collective-permute-start.9 = (bf16[256,512]{1,0:T(8,128)(2,1)S(1)}, bf16[256,512]{1,0:T(8,128)(2,1)S(1)}, u32[]{:S(2)}, u32[]{:S(2)}) collective-permute-start(bf16[256,512]{1,0:T(8,128)(2,1)S(1)} %get-tuple-element.22), channel_id=1, source_target_pairs={{0,1},{1,0},{2,3},{3,2},{4,5},{5,4},{6,7},{7,6},{8,9},{9,8},{10,11... | collective-permute-start | bytes 786440 | tf_op jit(solution)/shard_map/ppermute | solution.py:202

commit v2 on v1

--- a/solution.py
+++ b/solution.py
@@ -61,7 +61,7 @@
 
     for qg, tags, first, att_out, grad_out in (
         (qg_own, kv_own, core, attended, q_grad),
-        (qg_peer, kv_peer, 1 - core, swap.at[:, : 2 * HEAD], swap.at[:, 2 * HEAD :]),
+        (qg_peer, kv_peer, 1 - core, swap.at[:ROWS, : 2 * HEAD], swap.at[:ROWS, 2 * HEAD :]),
     ):
         for h in range(2):
             unit, _ = norm_rows(qg[:, h * HEAD : (h + 1) * HEAD])
@@ -119,7 +119,15 @@
     for part, block in parts:
         unit, _ = norm_rows(part[:ROWS, :HEAD])
         k_gain_grad = k_gain_grad + jnp.sum(key_grad[block] * unit, axis=0, keepdims=True)
-    gains[...] = jnp.concatenate([q_gain_grad, k_gain_grad], axis=1)
+    sums = jnp.concatenate([q_gain_grad, k_gain_grad], axis=1)
+    gains[...] = sums
+    high = sums.astype(bf16).astype(f32)
+    middle = (sums - high).astype(bf16).astype(f32)
+    low = sums - high - middle
+    row = lax.broadcasted_iota(jnp.int32, (EXTRA, 2 * HEAD), 0)
+    pieces = jnp.where(row == 0, high, jnp.where(row == 1, middle, jnp.where(row == 2, low, 0.0)))
+    swap[ROWS:, : 2 * HEAD] = pieces.astype(bf16)
+    swap[ROWS:, 2 * HEAD :] = jnp.zeros((EXTRA, 2 * HEAD), bf16)
     for i in range(2):
         for at, out in ((0, kv_grad_two), (2, kv_grad_one), (4, kv_grad_own)):
             out[i, :, :HEAD] = key_grad[at + i].astype(out.dtype)
@@ -135,6 +143,34 @@
         out[:, HEAD:] = total[:, HEAD:].astype(bf16)
 
 
+def place(out, mine, other):
+    core = lax.axis_index("core")
+    width = mine.shape[1]
+
+    @pl.when(core == 0)
+    def _():
+        out[:, :width] = mine
+        out[:, width:] = other
+
+    @pl.when(core == 1)
+    def _():
+        out[:, :width] = other
+        out[:, width:] = mine
+
+
+def join_queries_kernel(att_mine, grad_mine, from_peer, gains, attended, q_grad, pair_gains):
+    wide = 2 * HEAD
+    place(attended, att_mine[...], from_peer[:ROWS, :wide])
+    place(q_grad, grad_mine[...], from_peer[:ROWS, wide:])
+    pieces = from_peer[ROWS:, :wide].astype(f32)
+    pair_gains[...] = gains[...] + (pieces[0:1] + (pieces[1:2] + pieces[2:3]))
+
+
+def join_keys_kernel(mine, other, key_grad, value_grad):
+    place(key_grad, mine[:, :HEAD], other[:, :HEAD])
+    place(value_grad, mine[:, HEAD:], other[:, HEAD:])
+
+
 def vmem(count):
     return [pl.BlockSpec(memory_space=pltpu.VMEM)] * count
 
@@ -146,7 +182,7 @@
         out_shape=(
             shape((ROWS, 2 * HEAD), bf16),
             shape((ROWS, 2 * HEAD), bf16),
-            shape((ROWS, 4 * HEAD), bf16),
+            shape((ROWS + EXTRA, 4 * HEAD), bf16),
             shape((2, ROWS, 2 * HEAD), f32),
             shape((2, ROWS, 2 * HEAD), bf16),
             shape((2, ROWS, 2 * HEAD), bf16),
@@ -175,14 +211,14 @@
     )(*operands)
 
 
-def finish(*operands):
+def small(kernel, outs, name, *operands):
     return pl.pallas_call(
-        finish_kernel,
-        out_shape=(jax.ShapeDtypeStruct((ROWS, 2 * HEAD), bf16),) * 2,
+        kernel,
+        out_shape=tuple(jax.ShapeDtypeStruct(*out) for out in outs),
         in_specs=vmem(len(operands)),
-        out_specs=tuple(vmem(2)),
+        out_specs=tuple(vmem(len(outs))),
         compiler_params=pltpu.CompilerParams(vmem_limit_bytes=16 << 20),
-        name="finish",
+        name=name,
     )(*operands)
 
 
@@ -230,24 +266,28 @@
     attended, q_grad, to_peer, grad_own, grad_one, grad_two, gains = attention(
         q_gain, k_gain, qg_mine, qg_peer, kv_mine, kv_peer, kv_one, kv_one_x, kv_two, kv_two_x
     )
+    from_peer = swap(to_peer)
     grad_two, grad_one = hop(grad_two, -2), hop(grad_one, -1)
-    from_peer = swap(to_peer)
-    for axes in (("z",), ("y",), ("x", "core"), ("dp",)):
-        gains = lax.optimization_barrier(lax.psum(gains, axes))
-    kv_grad, kv_grad_peer = finish(k_gain, kv_mine, kv_peer, grad_own, grad_one, grad_two)
+    attended, q_grad, gains = small(
+        join_queries_kernel,
+        [((ROWS, 4 * HEAD), bf16), ((ROWS, 4 * HEAD), bf16), ((1, wide), f32)],
+        "join_queries", attended, q_grad, from_peer, gains,
+    )
+    gains = lax.optimization_barrier(lax.psum(gains, ("y",)))
+    gains = lax.psum(gains, ("dp", "x"))
+    gains, grad_one, grad_two = lax.optimization_barrier((gains, grad_one, grad_two))
+    kv_grad, kv_grad_peer = small(
+        finish_kernel,
+        [((ROWS, wide), bf16)] * 2,
+        "finish", k_gain, kv_mine, kv_peer, grad_own, grad_one, grad_two,
+    )
+    gains, kv_grad, kv_grad_peer = lax.optimization_barrier((gains, kv_grad, kv_grad_peer))
     kv_grad_x = swap(kv_grad_peer)
-
-    def join(mine, other):
-        return jnp.concatenate([jnp.where(first, mine, other), jnp.where(first, other, mine)], axis=1)[None]
-
-    return (
-        join(attended, from_peer[:, :wide]),
-        join(q_grad, from_peer[:, wide:]),
-        join(kv_grad[:, :HEAD], kv_grad_x[:, :HEAD]),
-        join(kv_grad[:, HEAD:], kv_grad_x[:, HEAD:]),
-        gains[0, :HEAD],
-        gains[0, HEAD:],
-    )
+    gains = lax.psum(gains, ("z",))
+    key_grad, value_grad = small(
+        join_keys_kernel, [((ROWS, wide), bf16)] * 2, "join_keys", kv_grad, kv_grad_x
+    )
+    return attended[None], q_grad[None], key_grad[None], value_grad[None], gains[0, :HEAD], gains[0, HEAD:]
 
 
 def solution(mesh):

time: 124 us -> 116 us (0.935)
  the two profiles are of different devices: /device:TPU:1 before, /device:TPU:2 now
where the time goes in v2:
time: 116 us; the launch traced here: 115 us
  blocking collectives  63.9 us (55%)
  starting transfers between devices  27.4 us (24%)
  Pallas kernels  11.2 us (10%)
  waiting for transfers between devices  8.58 us (7%)
  local copies, waits for them, and re-layouts  1.94 us (2%)
  other arithmetic  1.37 us (1%)
    psum x1, blocking collectives, per_device(): gains = lax.optimization_barrier(lax.psum(gains, ('y',)))  34.1 us
    ppermute x6, starting transfers between devices, hop(): lax.ppermute(array, SEQ, [(i, j) for i, j in pairs if 0 <= j < shards])  18.6 us
    psum x1, blocking collectives, per_device(): gains = lax.psum(gains, ('dp', 'x'))  15.6 us
    psum x1, blocking collectives, per_device(): gains = lax.psum(gains, ('z',))  14.2 us
    pallas_call x1, Pallas kernels, attention(): pl.pallas_call(attention_kernel, out_shape=(shape((ROWS, 2 * HEAD), bf16)...  8.89 us
    ppermute x4, starting transfers between devices, swap(): return lax.ppermute(array, 'core', [(0, 1), (1, 0)])  8.82 us
    ppermute x6, waiting for transfers between devices, hop(): lax.ppermute(array, SEQ, [(i, j) for i, j in pairs if 0 <= j < shards])  8.57 us
  transfers between devices with their start and end apart: 10, of which 2 were waited for; matrix products, arithmetic and copies ran while one was open for 1% of the time, Pallas kernels for 1%

profile of v2, /device:TPU:2, one launch (start us, length us, event | category | flops | bytes accessed | tf_op | source)
XLA Modules:
  0.0 115.2 jit_solution(5489132972613925294)
XLA Ops:
  0.6 0.0 copy-start.4
  0.6 0.7 copy-done.4
  1.3 1.1 broadcast_select_fusion.4
  2.5 0.0 copy-start.2
  2.5 0.0 copy-start.3
  2.5 3.9 %collective-permute-start.5 = (bf16[272,512]{1,0:T(8,128)(2,1)S(1)}, bf16[272,512]{1,0:T(8,128)(2,1)S(1)}, u32[]{:S(2)}, u32[]{:S(2)}) collective-permute-start(bf16[272,512]{1,0:T(8,128)(2,1)S(1)} %get-tuple-element.56), channel_id=1, source_target_pairs={{0,5},{1,4},{2,7},{3,6},{4,9},{5,8},{6,11},{7,10},{8,13},{9,12},{1... | collective-permute-start | bytes 835592 | tf_op jit(solution)/shard_map/ppermute | solution.py:235
  6.4 0.0 copy-done.2
  6.4 0.0 copy-done.3
  6.4 0.1 broadcast_select_fusion
  6.5 0.1 pad_maximum_fusion.1
  6.6 2.6 %collective-permute-start = (bf16[256,1024]{1,0:T(8,128)(2,1)S(1)}, bf16[256,1024]{1,0:T(8,128)(2,1)S(1)}, u32[]{:S(2)}, u32[]{:S(2)}) collective-permute-start(bf16[256,1024]{1,0:T(8,128)(2,1)S(1)} %pad_maximum_fusion.1), channel_id=1, source_target_pairs={{0,1},{1,0},{2,3},{3,2},{4,5},{5,4},{6,7},{7,6},{8,9},{9,8},{10,11... | collective-permute-start | bytes 1572872 | tf_op jit(solution)/shard_map/ppermute | solution.py:238
  9.2 3.9 %collective-permute-start.3 = (bf16[272,512]{1,0:T(8,128)(2,1)S(1)}, bf16[272,512]{1,0:T(8,128)(2,1)S(1)}, u32[]{:S(2)}, u32[]{:S(2)}) collective-permute-start(bf16[272,512]{1,0:T(8,128)(2,1)S(1)} %get-tuple-element.56), channel_id=1, source_target_pairs={{0,3},{1,2},{2,5},{3,4},{4,7},{5,6},{6,9},{7,8},{8,11},{9,10},{10,... | collective-permute-start | bytes 835592 | tf_op jit(solution)/shard_map/ppermute | solution.py:235
  13.0 2.4 %collective-permute-start.1 = (bf16[272,512]{1,0:T(8,128)(2,1)S(1)}, bf16[272,512]{1,0:T(8,128)(2,1)S(1)}, u32[]{:S(2)}, u32[]{:S(2)}) collective-permute-start(bf16[272,512]{1,0:T(8,128)(2,1)S(1)} %get-tuple-element.56), channel_id=1, source_target_pairs={{0,1},{1,0},{2,3},{3,2},{4,5},{5,4},{6,7},{7,6},{8,9},{9,8},{10,11... | collective-permute-start | bytes 835592 | tf_op jit(solution)/shard_map/ppermute | solution.py:238
  15.4 4.3 %collective-permute-start.4 = (bf16[272,512]{1,0:T(8,128)(2,1)S(1)}, bf16[272,512]{1,0:T(8,128)(2,1)S(1)}, u32[]{:S(2)}, u32[]{:S(2)}) collective-permute-start(bf16[272,512]{1,0:T(8,128)(2,1)S(1)} %get-tuple-element.57.kv_own), channel_id=1, source_target_pairs={{0,4},{1,5},{2,6},{3,7},{4,8},{5,9},{6,10},{7,11},{8,12},{9,13},{1... | collective-permute-start | bytes 835592 | tf_op jit(solution)/shard_map/ppermute | solution.py:235
  19.7 0.0 collective-permute-done.5.kv_two_x
  19.8 3.4 %collective-permute-start.2 = (bf16[272,512]{1,0:T(8,128)(2,1)S(1)}, bf16[272,512]{1,0:T(8,128)(2,1)S(1)}, u32[]{:S(2)}, u32[]{:S(2)}) collective-permute-start(bf16[272,512]{1,0:T(8,128)(2,1)S(1)} %get-tuple-element.57.kv_own), channel_id=1, source_target_pairs={{0,2},{1,3},{2,4},{3,5},{4,6},{5,7},{6,8},{7,9},{8,10},{9,11},{10,... | collective-permute-start | bytes 835592 | tf_op jit(solution)/shard_map/ppermute | solution.py:235
  23.2 0.0 copy-start.1
  23.2 0.1 pad_maximum_fusion.qg_own
  23.2 0.0 collective-permute-done.3.kv_one_x
  23.2 0.0 collective-permute-done.1.kv_peer
  23.2 3.5 %collective-permute-done.4.kv_two = bf16[272,512]{1,0:T(8,128)(2,1)S(1)} collective-permute-done((bf16[272,512]{1,0:T(8,128)(2,1)S(1)}, bf16[272,512]{1,0:T(8,128)(2,1)S(1)}, u32[]{:S(2)}, u32[]{:S(2)}) %collective-permute-start.4) | collective-permute-done | bytes 278560 | tf_op jit(solution)/shard_map/ppermute | solution.py:235
  26.8 5.1 %collective-permute-done.2.kv_one = bf16[272,512]{1,0:T(8,128)(2,1)S(1)} collective-permute-done((bf16[272,512]{1,0:T(8,128)(2,1)S(1)}, bf16[272,512]{1,0:T(8,128)(2,1)S(1)}, u32[]{:S(2)}, u32[]{:S(2)}) %collective-permute-start.2) | collective-permute-done | bytes 278560 | tf_op jit(solution)/shard_map/ppermute | solution.py:235
  31.8 0.0 collective-permute-done.qg_peer
  31.8 0.0 copy-start
  31.8 0.0 copy-done.1
  31.8 0.7 copy-done
  32.5 8.9 %attention.1 = (bf16[256,512]{1,0:T(8,128)(2,1)S(1)}, bf16[256,512]{1,0:T(8,128)(2,1)S(1)}, bf16[272,1024]{1,0:T(8,128)(2,1)S(1)}, f32[2,256,512]{2,1,0:T(8,128)...) custom-call(f32[1,256]{1,0:T(1,128)S(1)} %bitcast.14, ...), custom_call_target="tpu_custom_call" | custom-call | flops 8589934592 | bytes 8388608 | tf_op jit(solution)/shard_map/attention/pallas_call | solution.py:180
  41.4 1.9 %collective-permute-start.6 = (bf16[272,1024]{1,0:T(8,128)(2,1)S(1)}, bf16[272,1024]{1,0:T(8,128)(2,1)S(1)}, u32[]{:S(2)}, u32[]{:S(2)}) collective-permute-start(bf16[272,1024]{1,0:T(8,128)(2,1)S(1)} %get-tuple-element.28), channel_id=1, source_target_pairs={{0,1},{1,0},{2,3},{3,2},{4,5},{5,4},{6,7},{7,6},{8,9},{9,8},{10,11... | collective-permute-start | bytes 1671176 | tf_op jit(solution)/shard_map/ppermute | solution.py:238
  43.3 1.9 %collective-permute-start.7 = (bf16[2,256,512]{2,1,0:T(8,128)(2,1)}, bf16[2,256,512]{2,1,0:T(8,128)(2,1)S(1)}, u32[]{:S(2)}, u32[]{:S(2)}) collective-permute-start(bf16[2,256,512]{2,1,0:T(8,128)(2,1)} %get-tuple-element.33), channel_id=1, source_target_pairs={{2,0},{3,1},{4,2},{5,3},{6,4},{7,5},{8,6},{9,7},{10,8},{11,9},{12,... | collective-permute-start | bytes 1572872 | tf_op jit(solution)/shard_map/ppermute | solution.py:235
  45.2 1.3 %collective-permute-start.8 = (bf16[2,256,512]{2,1,0:T(8,128)(2,1)S(1)}, bf16[2,256,512]{2,1,0:T(8,128)(2,1)S(1)}, u32[]{:S(2)}, u32[]{:S(2)}) collective-permute-start(bf16[2,256,512]{2,1,0:T(8,128)(2,1)S(1)} %get-tuple-element.34), channel_id=1, source_target_pairs={{4,0},{5,1},{6,2},{7,3},{8,4},{9,5},{10,6},{11,7},{12,8},{13,9},{1... | collective-permute-start | bytes 1572872 | tf_op jit(solution)/shard_map/ppermute | solution.py:235
  46.5 0.0 collective-permute-done.6.from_peer
  46.5 1.1 join_queries.1
  47.6 34.1 %psum.21 = f32[1,512]{1,0:T(1,128)S(1)} all-reduce(f32[1,512]{1,0:T(1,128)S(1)} %get-tuple-element.32), channel_id=1, replica_groups=mesh['dp'=2,'y'=8,'z'=8,'x'=2,'core'=2] {'y'}, use_global_device_ids=true, to_apply=%region_0.1 | all-reduce | flops 512 | bytes 4096 | tf_op jit(solution)/shard_map/psum | solution.py:276
  81.8 15.6 %psum.22 = f32[1,512]{1,0:T(1,128)S(1)} all-reduce(f32[1,512]{1,0:T(1,128)S(1)} %psum.21), channel_id=1, replica_groups=mesh['dp'=2,'y'=8,'z'=8,'x'=2,'core'=2] {'dp','x'}, use_global_device_ids=true, to_apply=%region_1.2 | all-reduce | flops 512 | bytes 4096 | tf_op jit(solution)/shard_map/psum | solution.py:277
  97.3 0.0 collective-permute-done.7.grad_one
  97.3 0.0 collective-permute-done.8.grad_two
  97.3 0.4 finish.1
  97.7 1.9 %collective-permute-start.9 = (bf16[256,512]{1,0:T(8,128)(2,1)S(1)}, bf16[256,512]{1,0:T(8,128)(2,1)S(1)}, u32[]{:S(2)}, u32[]{:S(2)}) collective-permute-start(bf16[256,512]{1,0:T(8,128)(2,1)S(1)} %get-tuple-element.42), channel_id=1, source_target_pairs={{0,1},{1,0},{2,3},{3,2},{4,5},{5,4},{6,7},{7,6},{8,9},{9,8},{10,11... | collective-permute-start | bytes 786440 | tf_op jit(solution)/shard_map/ppermute | solution.py:238
  99.6 14.2 %psum.23 = f32[1,512]{1,0:T(1,128)S(1)} all-reduce(f32[1,512]{1,0:T(1,128)S(1)} %psum.22), channel_id=1, replica_groups=mesh['dp'=2,'y'=8,'z'=8,'x'=2,'core'=2] {'z'}, use_global_device_ids=true, to_apply=%region_2.3 | all-reduce | flops 512 | bytes 4096 | tf_op jit(solution)/shard_map/psum | solution.py:286
  113.8 0.6 fusion.3
  114.4 0.0 collective-permute-done.9.other
  114.4 0.8 join_keys.1
  (2 shorter events, 0.0 us)
Async XLA Ops:
  0.6 0.7 copy-start.4
  2.5 3.9 %copy-start.2 = (bf16[1,256,1024]{2,1,0:T(8,128)(2,1)S(1)}, bf16[1,256,1024]{2,1,0:T(8,128)(2,1)}, u32[]{:S(2)}) copy-start(bf16[1,256,1024]{2,1,0:T(8,128)(2,1)} %param.10) | copy-start | bytes 1572868
  2.5 3.9 %copy-start.3 = (bf16[1,256,1024]{2,1,0:T(8,128)(2,1)S(1)}, bf16[1,256,1024]{2,1,0:T(8,128)(2,1)}, u32[]{:S(2)}) copy-start(bf16[1,256,1024]{2,1,0:T(8,128)(2,1)} %param.7) | copy-start | bytes 1572868
  2.5 17.2 %collective-permute-start.5 = (bf16[272,512]{1,0:T(8,128)(2,1)S(1)}, bf16[272,512]{1,0:T(8,128)(2,1)S(1)}, u32[]{:S(2)}, u32[]{:S(2)}) collective-permute-start(bf16[272,512]{1,0:T(8,128)(2,1)S(1)} %get-tuple-element.56), channel_id=1, source_target_pairs={{0,5},{1,4},{2,7},{3,6},{4,9},{5,8},{6,11},{7,10},{8,13},{9,12},{1... | collective-permute-start | bytes 835592 | tf_op jit(solution)/shard_map/ppermute | solution.py:235
  6.6 25.2 %collective-permute-start = (bf16[256,1024]{1,0:T(8,128)(2,1)S(1)}, bf16[256,1024]{1,0:T(8,128)(2,1)S(1)}, u32[]{:S(2)}, u32[]{:S(2)}) collective-permute-start(bf16[256,1024]{1,0:T(8,128)(2,1)S(1)} %pad_maximum_fusion.1), channel_id=1, source_target_pairs={{0,1},{1,0},{2,3},{3,2},{4,5},{5,4},{6,7},{7,6},{8,9},{9,8},{10,11... | collective-permute-start | bytes 1572872 | tf_op jit(solution)/shard_map/ppermute | solution.py:238
  9.2 14.1 %collective-permute-start.3 = (bf16[272,512]{1,0:T(8,128)(2,1)S(1)}, bf16[272,512]{1,0:T(8,128)(2,1)S(1)}, u32[]{:S(2)}, u32[]{:S(2)}) collective-permute-start(bf16[272,512]{1,0:T(8,128)(2,1)S(1)} %get-tuple-element.56), channel_id=1, source_target_pairs={{0,3},{1,2},{2,5},{3,4},{4,7},{5,6},{6,9},{7,8},{8,11},{9,10},{10,... | collective-permute-start | bytes 835592 | tf_op jit(solution)/shard_map/ppermute | solution.py:235
  13.0 10.2 %collective-permute-start.1 = (bf16[272,512]{1,0:T(8,128)(2,1)S(1)}, bf16[272,512]{1,0:T(8,128)(2,1)S(1)}, u32[]{:S(2)}, u32[]{:S(2)}) collective-permute-start(bf16[272,512]{1,0:T(8,128)(2,1)S(1)} %get-tuple-element.56), channel_id=1, source_target_pairs={{0,1},{1,0},{2,3},{3,2},{4,5},{5,4},{6,7},{7,6},{8,9},{9,8},{10,11... | collective-permute-start | bytes 835592 | tf_op jit(solution)/shard_map/ppermute | solution.py:238
  15.4 11.3 %collective-permute-start.4 = (bf16[272,512]{1,0:T(8,128)(2,1)S(1)}, bf16[272,512]{1,0:T(8,128)(2,1)S(1)}, u32[]{:S(2)}, u32[]{:S(2)}) collective-permute-start(bf16[272,512]{1,0:T(8,128)(2,1)S(1)} %get-tuple-element.57.kv_own), channel_id=1, source_target_pairs={{0,4},{1,5},{2,6},{3,7},{4,8},{5,9},{6,10},{7,11},{8,12},{9,13},{1... | collective-permute-start | bytes 835592 | tf_op jit(solution)/shard_map/ppermute | solution.py:235
  19.8 12.0 %collective-permute-start.2 = (bf16[272,512]{1,0:T(8,128)(2,1)S(1)}, bf16[272,512]{1,0:T(8,128)(2,1)S(1)}, u32[]{:S(2)}, u32[]{:S(2)}) collective-permute-start(bf16[272,512]{1,0:T(8,128)(2,1)S(1)} %get-tuple-element.57.kv_own), channel_id=1, source_target_pairs={{0,2},{1,3},{2,4},{3,5},{4,6},{5,7},{6,8},{7,9},{8,10},{9,11},{10,... | collective-permute-start | bytes 835592 | tf_op jit(solution)/shard_map/ppermute | solution.py:235
  23.2 8.7 %copy-start.1 = (f32[256]{0:T(256)S(1)}, f32[256]{0:T(256)}, u32[]{:S(2)}) copy-start(f32[256]{0:T(256)} %param.11) | copy-start | bytes 3076
  31.8 0.7 copy-start
  41.4 5.1 %collective-permute-start.6 = (bf16[272,1024]{1,0:T(8,128)(2,1)S(1)}, bf16[272,1024]{1,0:T(8,128)(2,1)S(1)}, u32[]{:S(2)}, u32[]{:S(2)}) collective-permute-start(bf16[272,1024]{1,0:T(8,128)(2,1)S(1)} %get-tuple-element.28), channel_id=1, source_target_pairs={{0,1},{1,0},{2,3},{3,2},{4,5},{5,4},{6,7},{7,6},{8,9},{9,8},{10,11... | collective-permute-start | bytes 1671176 | tf_op jit(solution)/shard_map/ppermute | solution.py:238
  43.3 54.0 %collective-permute-start.7 = (bf16[2,256,512]{2,1,0:T(8,128)(2,1)}, bf16[2,256,512]{2,1,0:T(8,128)(2,1)S(1)}, u32[]{:S(2)}, u32[]{:S(2)}) collective-permute-start(bf16[2,256,512]{2,1,0:T(8,128)(2,1)} %get-tuple-element.33), channel_id=1, source_target_pairs={{2,0},{3,1},{4,2},{5,3},{6,4},{7,5},{8,6},{9,7},{10,8},{11,9},{12,... | collective-permute-start | bytes 1572872 | tf_op jit(solution)/shard_map/ppermute | solution.py:235
  45.2 52.1 %collective-permute-start.8 = (bf16[2,256,512]{2,1,0:T(8,128)(2,1)S(1)}, bf16[2,256,512]{2,1,0:T(8,128)(2,1)S(1)}, u32[]{:S(2)}, u32[]{:S(2)}) collective-permute-start(bf16[2,256,512]{2,1,0:T(8,128)(2,1)S(1)} %get-tuple-element.34), channel_id=1, source_target_pairs={{4,0},{5,1},{6,2},{7,3},{8,4},{9,5},{10,6},{11,7},{12,8},{13,9},{1... | collective-permute-start | bytes 1572872 | tf_op jit(solution)/shard_map/ppermute | solution.py:235
  97.7 16.7 %collective-permute-start.9 = (bf16[256,512]{1,0:T(8,128)(2,1)S(1)}, bf16[256,512]{1,0:T(8,128)(2,1)S(1)}, u32[]{:S(2)}, u32[]{:S(2)}) collective-permute-start(bf16[256,512]{1,0:T(8,128)(2,1)S(1)} %get-tuple-element.42), channel_id=1, source_target_pairs={{0,1},{1,0},{2,3},{3,2},{4,5},{5,4},{6,7},{7,6},{8,9},{9,8},{10,11... | collective-permute-start | bytes 786440 | tf_op jit(solution)/shard_map/ppermute | solution.py:238

commit v3 on v2

--- a/solution.py
+++ b/solution.py
@@ -35,7 +35,7 @@
 
 def attention_kernel(
     q_gain, k_gain, qg_own, qg_peer, kv_own, kv_peer, kv_one, kv_one_x, kv_two, kv_two_x,
-    attended, q_grad, swap, kv_grad_own, kv_grad_one, kv_grad_two, gains,
+    attended, q_grad, swap, kv_grad_own, kv_one_first, kv_one_second, kv_two_first, kv_two_second, gains,
     key, key_t, value, value_t, tag, key_grad, value_grad, score, query, upstream, upstream_t,
 ):
     core = lax.axis_index("core")
@@ -128,19 +128,35 @@
     pieces = jnp.where(row == 0, high, jnp.where(row == 1, middle, jnp.where(row == 2, low, 0.0)))
     swap[ROWS:, : 2 * HEAD] = pieces.astype(bf16)
     swap[ROWS:, 2 * HEAD :] = jnp.zeros((EXTRA, 2 * HEAD), bf16)
-    for i in range(2):
-        for at, out in ((0, kv_grad_two), (2, kv_grad_one), (4, kv_grad_own)):
-            out[i, :, :HEAD] = key_grad[at + i].astype(out.dtype)
-            out[i, :, HEAD:] = value_grad[at + i].astype(out.dtype)
-
-
-def finish_kernel(k_gain, kv_own, kv_peer, grad_own, grad_one, grad_two, own, peer):
-    core = lax.axis_index("core")
-    for part, block, out in ((kv_own, core, own), (kv_peer, 1 - core, peer)):
-        total = grad_own[block] + grad_one[block].astype(f32) + grad_two[block].astype(f32)
-        unit, inverse = norm_rows(part[:ROWS, :HEAD])
-        out[:, :HEAD] = norm_backward(total[:, :HEAD], unit, inverse, k_gain[...]).astype(bf16)
-        out[:, HEAD:] = total[:, HEAD:].astype(bf16)
+    outs = (kv_two_first, kv_two_second, kv_one_first, kv_one_second, kv_grad_own.at[0], kv_grad_own.at[1])
+    for block, out in enumerate(outs):
+        out[:, :HEAD] = key_grad[block].astype(out.dtype)
+        out[:, HEAD:] = value_grad[block].astype(out.dtype)
+
+
+def finish_kernel(
+    k_gain, kv_own, kv_peer, grad_own, side_first, side_second, ahead_first, ahead_second, own, peer
+):
+    core, x = lax.axis_index("core"), lax.axis_index("x")
+    for block, side, ahead in ((0, side_first, ahead_first), (1, side_second, ahead_second)):
+        total = grad_own[block] + ahead[...].astype(f32)
+        total = total + jnp.where(x == 0, side[...].astype(f32), 0.0)
+        raw = jnp.where(
+            core == block, kv_own[:ROWS, :HEAD].astype(f32), kv_peer[:ROWS, :HEAD].astype(f32)
+        )
+        unit, inverse = norm_rows(raw)
+        key_grad = norm_backward(total[:, :HEAD], unit, inverse, k_gain[...]).astype(bf16)
+        value_grad = total[:, HEAD:].astype(bf16)
+
+        @pl.when(core == block)
+        def _():
+            own[:, :HEAD] = key_grad
+            own[:, HEAD:] = value_grad
+
+        @pl.when(core != block)
+        def _():
+            peer[:, :HEAD] = key_grad
+            peer[:, HEAD:] = value_grad
 
 
 def place(out, mine, other):
@@ -184,12 +200,11 @@
             shape((ROWS, 2 * HEAD), bf16),
             shape((ROWS + EXTRA, 4 * HEAD), bf16),
             shape((2, ROWS, 2 * HEAD), f32),
-            shape((2, ROWS, 2 * HEAD), bf16),
-            shape((2, ROWS, 2 * HEAD), bf16),
+            *(shape((ROWS, 2 * HEAD), bf16),) * 4,
             shape((1, 2 * HEAD), f32),
         ),
         in_specs=vmem(len(operands)),
-        out_specs=tuple(vmem(7)),
+        out_specs=tuple(vmem(9)),
         scratch_shapes=[
             pltpu.VMEM((BLOCKS, ROWS, HEAD), bf16),
             pltpu.VMEM((BLOCKS, HEAD, ROWS), bf16),
@@ -234,10 +249,10 @@
         pairs = [(i, (i ^ cross) + 2 * chips) for i in range(shards)]
         return lax.ppermute(array, SEQ, [(i, j) for i, j in pairs if 0 <= j < shards])
 
-    def swap(array):
-        return lax.ppermute(array, "core", [(0, 1), (1, 0)])
-
-    first = core == 0
+    def swap(array, axis="core"):
+        return lax.ppermute(array, axis, [(0, 1), (1, 0)])
+
+    first, lead = core == 0, lax.axis_index("x") == 0
     ids = jnp.pad((document_ids[0] + 1).astype(bf16)[None], ((0, EXTRA - 1), (0, wide - ROWS)))
 
     def pack(mine):
@@ -251,7 +266,7 @@
             axis=0,
         )
 
-    kv_mine, kv_other = pack(first), pack(~first)
+    kv_mine, kv_other = lax.optimization_barrier((pack(first), pack(~first)))
 
     def pack_queries(mine):
         return jnp.concatenate(
@@ -260,34 +275,45 @@
 
     qg_mine, qg_other = pack_queries(first), pack_queries(~first)
     kv_two, kv_two_x = hop(kv_mine, 2), hop(kv_other, 2, True)
-    kv_one, kv_one_x = hop(kv_mine, 1), hop(kv_other, 1, True)
     kv_peer, qg_peer = swap(kv_other), swap(qg_other)
+    kv_one = swap(jnp.where(lead, kv_mine, kv_two), "x")
+    kv_one_x = swap(jnp.where(lead, kv_peer, kv_two_x), "x")
     q_gain, k_gain = query_gain[None], key_gain[None]
-    attended, q_grad, to_peer, grad_own, grad_one, grad_two, gains = attention(
+    attended, q_grad, to_peer, grad_own, one_first, one_second, two_first, two_second, gains = attention(
         q_gain, k_gain, qg_mine, qg_peer, kv_mine, kv_peer, kv_one, kv_one_x, kv_two, kv_two_x
     )
     from_peer = swap(to_peer)
-    grad_two, grad_one = hop(grad_two, -2), hop(grad_one, -1)
+    side_first, side_second = swap(one_first, "x"), swap(one_second, "x")
     attended, q_grad, gains = small(
         join_queries_kernel,
         [((ROWS, 4 * HEAD), bf16), ((ROWS, 4 * HEAD), bf16), ((1, wide), f32)],
         "join_queries", attended, q_grad, from_peer, gains,
     )
-    gains = lax.optimization_barrier(lax.psum(gains, ("y",)))
     gains = lax.psum(gains, ("dp", "x"))
-    gains, grad_one, grad_two = lax.optimization_barrier((gains, grad_one, grad_two))
+    gains, side_first, side_second = lax.optimization_barrier((gains, side_first, side_second))
+
+    def onward(two, side):
+        return (two.astype(f32) + jnp.where(lead, 0.0, side.astype(f32))).astype(bf16)
+
+    onward_first, onward_second = onward(two_first, side_first), onward(two_second, side_second)
+    gains, onward_first, onward_second = lax.optimization_barrier((gains, onward_first, onward_second))
+    ahead_first, ahead_second = hop(onward_first, -2), hop(onward_second, -2)
+    lines = lax.axis_size("y") * lax.axis_size("z")
+    gathered = lax.all_to_all(
+        jnp.broadcast_to(gains, (lines, wide)), ("y", "z"), 0, 0, tiled=True
+    )
+    gathered, ahead_first, ahead_second = lax.optimization_barrier((gathered, ahead_first, ahead_second))
     kv_grad, kv_grad_peer = small(
         finish_kernel,
         [((ROWS, wide), bf16)] * 2,
-        "finish", k_gain, kv_mine, kv_peer, grad_own, grad_one, grad_two,
-    )
-    gains, kv_grad, kv_grad_peer = lax.optimization_barrier((gains, kv_grad, kv_grad_peer))
+        "finish", k_gain, kv_mine, kv_peer, grad_own, side_first, side_second, ahead_first, ahead_second,
+    )
     kv_grad_x = swap(kv_grad_peer)
-    gains = lax.psum(gains, ("z",))
+    gains = jnp.sum(gathered, axis=0)
     key_grad, value_grad = small(
         join_keys_kernel, [((ROWS, wide), bf16)] * 2, "join_keys", kv_grad, kv_grad_x
     )
-    return attended[None], q_grad[None], key_grad[None], value_grad[None], gains[0, :HEAD], gains[0, HEAD:]
+    return attended[None], q_grad[None], key_grad[None], value_grad[None], gains[:HEAD], gains[HEAD:]
 
 
 def solution(mesh):

time: 116 us -> 105 us (0.905)
  the two profiles are of different devices: /device:TPU:2 before, /device:TPU:1 now
where the time goes in v3:
time: 105 us; the launch traced here: 104 us
  blocking collectives  41.7 us (40%)
  starting transfers between devices  35.8 us (34%)
  Pallas kernels  11.3 us (11%)
  waiting for transfers between devices  10.9 us (10%)
  local copies, waits for them, and re-layouts  2.02 us (2%)
  other arithmetic  1.62 us (2%)
    all_to_all x1, blocking collectives, per_device(): lax.all_to_all(jnp.broadcast_to(gains, (lines, wide)), ('y', 'z'), 0, 0,...  28.8 us
    ppermute x8, starting transfers between devices, swap(): return lax.ppermute(array, axis, [(0, 1), (1, 0)])  26.4 us
    psum x1, blocking collectives, per_device(): gains = lax.psum(gains, ('dp', 'x'))  12.8 us
    ppermute x8, waiting for transfers between devices, swap(): return lax.ppermute(array, axis, [(0, 1), (1, 0)])  10.9 us
    ppermute x4, starting transfers between devices, hop(): lax.ppermute(array, SEQ, [(i, j) for i, j in pairs if 0 <= j < shards])  9.43 us
    pallas_call x1, Pallas kernels, attention(): pl.pallas_call(attention_kernel, out_shape=(shape((ROWS, 2 * HEAD), bf16)...  8.8 us
    pallas_call x3, Pallas kernels, small(): pl.pallas_call(kernel, out_shape=tuple((jax.ShapeDtypeStruct(*out) for ou...  2.49 us
  transfers between devices with their start and end apart: 12, of which 3 were waited for; matrix products, arithmetic and copies ran while one was open for 1% of the time, Pallas kernels for 1%

profile of v3, /device:TPU:1, one launch (start us, length us, event | category | flops | bytes accessed | tf_op | source)
XLA Modules:
  0.0 104.2 jit_solution(5541757292155070046)
XLA Ops:
  0.6 0.0 copy-start.4
  0.6 0.7 copy-done.4
  1.3 1.1 %broadcast_select_fusion.6 = (bf16[256,256]{1,0:T(8,128)(2,1)S(1)}, bf16[256,256]{1,0:T(8,128)(2,1)S(1)}, bf16[256,256]{1,0:T(8,128)(2,1)S(1)}, bf16[256,256]{1,0:T(8,128)(2,1)S(1)}) fusion(pred[]{:T(512)S(6)} %not.4, bf16[256,512]{1,0:T(8,128)(2,1)} %bitcast.20, pred[]{:T(512)S(6)} %eq.6, bf16[256,512]{1,0:T(8,128)(2,1)} %bitcast.21), kind=kLoop, calls=%fused_computation.15 | loop fusion | flops 262144 | bytes 1048578 | tf_op jit(solution)/shard_map/jit(_where)/select_n | solution.py:262
  2.5 0.0 copy-start.2
  2.5 0.0 copy-start.3
  2.5 5.5 %collective-permute-start.4 = (bf16[272,512]{1,0:T(8,128)(2,1)S(1)}, bf16[272,512]{1,0:T(8,128)(2,1)S(1)}, u32[]{:S(2)}, u32[]{:S(2)}) collective-permute-start(bf16[272,512]{1,0:T(8,128)(2,1)S(1)} %get-tuple-element.34), channel_id=1, source_target_pairs={{0,5},{1,4},{2,7},{3,6},{4,9},{5,8},{6,11},{7,10},{8,13},{9,12},{1... | collective-permute-start | bytes 835592 | tf_op jit(solution)/shard_map/ppermute | solution.py:250
  8.1 4.7 %collective-permute-start.1 = (bf16[272,512]{1,0:T(8,128)(2,1)S(1)}, bf16[272,512]{1,0:T(8,128)(2,1)S(1)}, u32[]{:S(2)}, u32[]{:S(2)}) collective-permute-start(bf16[272,512]{1,0:T(8,128)(2,1)S(1)} %get-tuple-element.34), channel_id=1, source_target_pairs={{0,1},{1,0},{2,3},{3,2},{4,5},{5,4},{6,7},{7,6},{8,9},{9,8},{10,11... | collective-permute-start | bytes 835592 | tf_op jit(solution)/shard_map/ppermute | solution.py:253
  12.8 1.3 %collective-permute-start.2 = (bf16[272,512]{1,0:T(8,128)(2,1)S(1)}, bf16[272,512]{1,0:T(8,128)(2,1)S(1)}, u32[]{:S(2)}, u32[]{:S(2)}) collective-permute-start(bf16[272,512]{1,0:T(8,128)(2,1)S(1)} %get-tuple-element.33.kv_own), channel_id=1, source_target_pairs={{0,4},{1,5},{2,6},{3,7},{4,8},{5,9},{6,10},{7,11},{8,12},{9,13},{1... | collective-permute-start | bytes 835592 | tf_op jit(solution)/shard_map/ppermute | solution.py:250
  14.1 0.0 copy-done.2
  14.1 0.0 copy-done.3
  14.1 0.1 broadcast_select_fusion.2
  14.2 0.1 pad_maximum_fusion.1
  14.3 2.6 %collective-permute-start = (bf16[256,1024]{1,0:T(8,128)(2,1)S(1)}, bf16[256,1024]{1,0:T(8,128)(2,1)S(1)}, u32[]{:S(2)}, u32[]{:S(2)}) collective-permute-start(bf16[256,1024]{1,0:T(8,128)(2,1)S(1)} %pad_maximum_fusion.1), channel_id=1, source_target_pairs={{0,1},{1,0},{2,3},{3,2},{4,5},{5,4},{6,7},{7,6},{8,9},{9,8},{10,11... | collective-permute-start | bytes 1572872 | tf_op jit(solution)/shard_map/ppermute | solution.py:253
  16.9 0.0 collective-permute-done.4.kv_two_x
  16.9 0.0 collective-permute-done.1.kv_peer
  16.9 3.1 %collective-permute-start.5 = (bf16[272,512]{1,0:T(8,128)(2,1)S(1)}, bf16[272,512]{1,0:T(8,128)(2,1)S(1)}, u32[]{:S(2)}, u32[]{:S(2)}) collective-permute-start(bf16[272,512]{1,0:T(8,128)(2,1)S(1)} %broadcast_select_fusion), channel_id=1, source_target_pairs={{0,2},{2,0},{1,3},{3,1},{4,6},{6,4},{5,7},{7,5},{8,10},{10,8},{9,1... | collective-permute-start | bytes 835592 | tf_op jit(solution)/shard_map/ppermute | solution.py:253
  20.1 0.0 collective-permute-done.2.kv_two
  20.1 2.5 %collective-permute-start.3 = (bf16[272,512]{1,0:T(8,128)(2,1)S(1)}, bf16[272,512]{1,0:T(8,128)(2,1)S(1)}, u32[]{:S(2)}, u32[]{:S(2)}) collective-permute-start(bf16[272,512]{1,0:T(8,128)(2,1)S(1)} %broadcast_select_fusion.1), channel_id=1, source_target_pairs={{0,2},{2,0},{1,3},{3,1},{4,6},{6,4},{5,7},{7,5},{8,10},{10,8},{9,1... | collective-permute-start | bytes 835592 | tf_op jit(solution)/shard_map/ppermute | solution.py:253
  22.7 0.0 copy-start.1
  22.7 0.1 pad_maximum_fusion.qg_own
  22.7 0.0 collective-permute-done.qg_peer
  22.7 4.4 %collective-permute-done.5.kv_one_x = bf16[272,512]{1,0:T(8,128)(2,1)S(1)} collective-permute-done((bf16[272,512]{1,0:T(8,128)(2,1)S(1)}, bf16[272,512]{1,0:T(8,128)(2,1)S(1)}, u32[]{:S(2)}, u32[]{:S(2)}) %collective-permute-start.5) | collective-permute-done | bytes 278560 | tf_op jit(solution)/shard_map/ppermute | solution.py:253
  27.1 6.0 %collective-permute-done.3.kv_one = bf16[272,512]{1,0:T(8,128)(2,1)S(1)} collective-permute-done((bf16[272,512]{1,0:T(8,128)(2,1)S(1)}, bf16[272,512]{1,0:T(8,128)(2,1)S(1)}, u32[]{:S(2)}, u32[]{:S(2)}) %collective-permute-start.3) | collective-permute-done | bytes 278560 | tf_op jit(solution)/shard_map/ppermute | solution.py:253
  33.1 0.0 copy-start
  33.1 0.0 copy-done.1
  33.1 0.7 copy-done
  33.8 8.8 %attention.1 = (bf16[256,512]{1,0:T(8,128)(2,1)S(1)}, bf16[256,512]{1,0:T(8,128)(2,1)S(1)}, bf16[272,1024]{1,0:T(8,128)(2,1)S(1)}, f32[2,256,512]{2,1,0:T(8,128)...) custom-call(f32[1,256]{1,0:T(1,128)S(1)} %bitcast.16, ...), custom_call_target="tpu_custom_call" | custom-call | flops 8589934592 | bytes 8388608 | tf_op jit(solution)/shard_map/attention/pallas_call | solution.py:196
  42.6 2.7 %collective-permute-start.6 = (bf16[272,1024]{1,0:T(8,128)(2,1)S(1)}, bf16[272,1024]{1,0:T(8,128)(2,1)S(1)}, u32[]{:S(2)}, u32[]{:S(2)}) collective-permute-start(bf16[272,1024]{1,0:T(8,128)(2,1)S(1)} %get-tuple-element.37), channel_id=1, source_target_pairs={{0,1},{1,0},{2,3},{3,2},{4,5},{5,4},{6,7},{7,6},{8,9},{9,8},{10,11... | collective-permute-start | bytes 1671176 | tf_op jit(solution)/shard_map/ppermute | solution.py:253
  45.2 3.1 %collective-permute-start.7 = (bf16[256,512]{1,0:T(8,128)(2,1)}, bf16[256,512]{1,0:T(8,128)(2,1)S(1)}, u32[]{:S(2)}, u32[]{:S(2)}) collective-permute-start(bf16[256,512]{1,0:T(8,128)(2,1)} %get-tuple-element.43), channel_id=1, source_target_pairs={{0,2},{2,0},{1,3},{3,1},{4,6},{6,4},{5,7},{7,5},{8,10},{10,8},{9,1... | collective-permute-start | bytes 786440 | tf_op jit(solution)/shard_map/ppermute | solution.py:253
  48.4 2.2 %collective-permute-start.8 = (bf16[256,512]{1,0:T(8,128)(2,1)S(1)}, bf16[256,512]{1,0:T(8,128)(2,1)S(1)}, u32[]{:S(2)}, u32[]{:S(2)}) collective-permute-start(bf16[256,512]{1,0:T(8,128)(2,1)S(1)} %get-tuple-element.44), channel_id=1, source_target_pairs={{0,2},{2,0},{1,3},{3,1},{4,6},{6,4},{5,7},{7,5},{8,10},{10,8},{9,1... | collective-permute-start | bytes 786440 | tf_op jit(solution)/shard_map/ppermute | solution.py:253
  50.5 0.0 collective-permute-done.6.from_peer
  50.6 1.1 %join_queries.1 = (bf16[256,1024]{1,0:T(8,128)(2,1)}, bf16[256,1024]{1,0:T(8,128)(2,1)}, f32[1,512]{1,0:T(1,128)S(1)}) custom-call(bf16[256,512]{1,0:T(8,128)(2,1)S(1)} %get-tuple-element.35.att_mine, bf16[256,512]{1,0:T(8,128)(2,1)S(1)} %get-tuple-element.36.grad_mine, bf16[272,1024]{1,0:T(8,128)(2,1)S(1)} %collective-permute-done.6.from_peer, ...), custom_call_target="tpu_custom_call" | custom-call | tf_op jit(solution)/shard_map/join_queries/pallas_call | solution.py:230
  51.7 12.8 %psum.7 = f32[1,512]{1,0:T(1,128)S(1)} all-reduce(f32[1,512]{1,0:T(1,128)S(1)} %get-tuple-element.42), channel_id=1, replica_groups=mesh['dp'=2,'y'=8,'z'=8,'x'=2,'core'=2] {'dp','x'}, use_global_device_ids=true, to_apply=%region_0.1 | all-reduce | flops 512 | bytes 4096 | tf_op jit(solution)/shard_map/psum | solution.py:292
  64.5 0.0 collective-permute-done.7.side_first
  64.5 0.0 collective-permute-done.8.side_second
  64.5 0.1 add_convert_fusion.1
  64.6 0.1 add_convert_fusion
  64.6 1.3 %collective-permute-start.9 = (bf16[256,512]{1,0:T(8,128)(2,1)S(1)}, bf16[256,512]{1,0:T(8,128)(2,1)S(1)}, u32[]{:S(2)}, u32[]{:S(2)}) collective-permute-start(bf16[256,512]{1,0:T(8,128)(2,1)S(1)} %add_convert_fusion.1), channel_id=1, source_target_pairs={{4,0},{5,1},{6,2},{7,3},{8,4},{9,5},{10,6},{11,7},{12,8},{13,9},{1... | collective-permute-start | bytes 786440 | tf_op jit(solution)/shard_map/ppermute | solution.py:250
  65.9 1.3 %collective-permute-start.10 = (bf16[256,512]{1,0:T(8,128)(2,1)S(1)}, bf16[256,512]{1,0:T(8,128)(2,1)S(1)}, u32[]{:S(2)}, u32[]{:S(2)}) collective-permute-start(bf16[256,512]{1,0:T(8,128)(2,1)S(1)} %add_convert_fusion), channel_id=1, source_target_pairs={{4,0},{5,1},{6,2},{7,3},{8,4},{9,5},{10,6},{11,7},{12,8},{13,9},{1... | collective-permute-start | bytes 786440 | tf_op jit(solution)/shard_map/ppermute | solution.py:250
  67.2 0.1 broadcast_in_dim.34
  67.3 28.8 %all_to_all.9 = f32[64,1,512]{2,1,0:T(1,128)S(1)} all-to-all(f32[64,1,512]{2,1,0:T(1,128)S(1)} %broadcast_in_dim.34), channel_id=1, replica_groups=mesh['dp'=2,'y'=8,'z'=8,'x'=2,'core'=2] {'y','z'}, dimensions={0} | all-to-all | bytes 262144 | tf_op jit(solution)/shard_map/all_to_all | solution.py:302
  96.2 0.0 collective-permute-done.9.ahead_first
  96.2 0.0 collective-permute-done.10.ahead_second
  96.2 0.5 finish.1
  96.7 5.5 %collective-permute-start.11 = (bf16[256,512]{1,0:T(8,128)(2,1)S(1)}, bf16[256,512]{1,0:T(8,128)(2,1)S(1)}, u32[]{:S(2)}, u32[]{:S(2)}) collective-permute-start(bf16[256,512]{1,0:T(8,128)(2,1)S(1)} %get-tuple-element.56), channel_id=1, source_target_pairs={{0,1},{1,0},{2,3},{3,2},{4,5},{5,4},{6,7},{7,6},{8,9},{9,8},{10,11... | collective-permute-start | bytes 786440 | tf_op jit(solution)/shard_map/ppermute | solution.py:253
  102.3 0.6 fusion.3
  102.8 0.5 collective-permute-done.11.other
  103.4 0.9 join_keys.1
  (6 shorter events, 0.1 us)
Async XLA Ops:
  0.6 0.7 copy-start.4
  2.5 11.6 %copy-start.2 = (bf16[1,256,1024]{2,1,0:T(8,128)(2,1)S(1)}, bf16[1,256,1024]{2,1,0:T(8,128)(2,1)}, u32[]{:S(2)}) copy-start(bf16[1,256,1024]{2,1,0:T(8,128)(2,1)} %param.10) | copy-start | bytes 1572868
  2.5 11.6 %copy-start.3 = (bf16[1,256,1024]{2,1,0:T(8,128)(2,1)S(1)}, bf16[1,256,1024]{2,1,0:T(8,128)(2,1)}, u32[]{:S(2)}) copy-start(bf16[1,256,1024]{2,1,0:T(8,128)(2,1)} %param.7) | copy-start | bytes 1572868
  2.5 14.4 %collective-permute-start.4 = (bf16[272,512]{1,0:T(8,128)(2,1)S(1)}, bf16[272,512]{1,0:T(8,128)(2,1)S(1)}, u32[]{:S(2)}, u32[]{:S(2)}) collective-permute-start(bf16[272,512]{1,0:T(8,128)(2,1)S(1)} %get-tuple-element.34), channel_id=1, source_target_pairs={{0,5},{1,4},{2,7},{3,6},{4,9},{5,8},{6,11},{7,10},{8,13},{9,12},{1... | collective-permute-start | bytes 835592 | tf_op jit(solution)/shard_map/ppermute | solution.py:250
  8.1 8.8 %collective-permute-start.1 = (bf16[272,512]{1,0:T(8,128)(2,1)S(1)}, bf16[272,512]{1,0:T(8,128)(2,1)S(1)}, u32[]{:S(2)}, u32[]{:S(2)}) collective-permute-start(bf16[272,512]{1,0:T(8,128)(2,1)S(1)} %get-tuple-element.34), channel_id=1, source_target_pairs={{0,1},{1,0},{2,3},{3,2},{4,5},{5,4},{6,7},{7,6},{8,9},{9,8},{10,11... | collective-permute-start | bytes 835592 | tf_op jit(solution)/shard_map/ppermute | solution.py:253
  12.8 7.3 %collective-permute-start.2 = (bf16[272,512]{1,0:T(8,128)(2,1)S(1)}, bf16[272,512]{1,0:T(8,128)(2,1)S(1)}, u32[]{:S(2)}, u32[]{:S(2)}) collective-permute-start(bf16[272,512]{1,0:T(8,128)(2,1)S(1)} %get-tuple-element.33.kv_own), channel_id=1, source_target_pairs={{0,4},{1,5},{2,6},{3,7},{4,8},{5,9},{6,10},{7,11},{8,12},{9,13},{1... | collective-permute-start | bytes 835592 | tf_op jit(solution)/shard_map/ppermute | solution.py:250
  14.3 8.5 %collective-permute-start = (bf16[256,1024]{1,0:T(8,128)(2,1)S(1)}, bf16[256,1024]{1,0:T(8,128)(2,1)S(1)}, u32[]{:S(2)}, u32[]{:S(2)}) collective-permute-start(bf16[256,1024]{1,0:T(8,128)(2,1)S(1)} %pad_maximum_fusion.1), channel_id=1, source_target_pairs={{0,1},{1,0},{2,3},{3,2},{4,5},{5,4},{6,7},{7,6},{8,9},{9,8},{10,11... | collective-permute-start | bytes 1572872 | tf_op jit(solution)/shard_map/ppermute | solution.py:253
  16.9 10.2 %collective-permute-start.5 = (bf16[272,512]{1,0:T(8,128)(2,1)S(1)}, bf16[272,512]{1,0:T(8,128)(2,1)S(1)}, u32[]{:S(2)}, u32[]{:S(2)}) collective-permute-start(bf16[272,512]{1,0:T(8,128)(2,1)S(1)} %broadcast_select_fusion), channel_id=1, source_target_pairs={{0,2},{2,0},{1,3},{3,1},{4,6},{6,4},{5,7},{7,5},{8,10},{10,8},{9,1... | collective-permute-start | bytes 835592 | tf_op jit(solution)/shard_map/ppermute | solution.py:253
  20.1 13.0 %collective-permute-start.3 = (bf16[272,512]{1,0:T(8,128)(2,1)S(1)}, bf16[272,512]{1,0:T(8,128)(2,1)S(1)}, u32[]{:S(2)}, u32[]{:S(2)}) collective-permute-start(bf16[272,512]{1,0:T(8,128)(2,1)S(1)} %broadcast_select_fusion.1), channel_id=1, source_target_pairs={{0,2},{2,0},{1,3},{3,1},{4,6},{6,4},{5,7},{7,5},{8,10},{10,8},{9,1... | collective-permute-start | bytes 835592 | tf_op jit(solution)/shard_map/ppermute | solution.py:253
  22.7 10.4 %copy-start.1 = (f32[256]{0:T(256)S(1)}, f32[256]{0:T(256)}, u32[]{:S(2)}) copy-start(f32[256]{0:T(256)} %param.11) | copy-start | bytes 3076
  33.1 0.7 copy-start
  42.6 8.0 %collective-permute-start.6 = (bf16[272,1024]{1,0:T(8,128)(2,1)S(1)}, bf16[272,1024]{1,0:T(8,128)(2,1)S(1)}, u32[]{:S(2)}, u32[]{:S(2)}) collective-permute-start(bf16[272,1024]{1,0:T(8,128)(2,1)S(1)} %get-tuple-element.37), channel_id=1, source_target_pairs={{0,1},{1,0},{2,3},{3,2},{4,5},{5,4},{6,7},{7,6},{8,9},{9,8},{10,11... | collective-permute-start | bytes 1671176 | tf_op jit(solution)/shard_map/ppermute | solution.py:253
  45.2 19.2 %collective-permute-start.7 = (bf16[256,512]{1,0:T(8,128)(2,1)}, bf16[256,512]{1,0:T(8,128)(2,1)S(1)}, u32[]{:S(2)}, u32[]{:S(2)}) collective-permute-start(bf16[256,512]{1,0:T(8,128)(2,1)} %get-tuple-element.43), channel_id=1, source_target_pairs={{0,2},{2,0},{1,3},{3,1},{4,6},{6,4},{5,7},{7,5},{8,10},{10,8},{9,1... | collective-permute-start | bytes 786440 | tf_op jit(solution)/shard_map/ppermute | solution.py:253
  48.4 16.1 %collective-permute-start.8 = (bf16[256,512]{1,0:T(8,128)(2,1)S(1)}, bf16[256,512]{1,0:T(8,128)(2,1)S(1)}, u32[]{:S(2)}, u32[]{:S(2)}) collective-permute-start(bf16[256,512]{1,0:T(8,128)(2,1)S(1)} %get-tuple-element.44), channel_id=1, source_target_pairs={{0,2},{2,0},{1,3},{3,1},{4,6},{6,4},{5,7},{7,5},{8,10},{10,8},{9,1... | collective-permute-start | bytes 786440 | tf_op jit(solution)/shard_map/ppermute | solution.py:253
  64.6 31.5 %collective-permute-start.9 = (bf16[256,512]{1,0:T(8,128)(2,1)S(1)}, bf16[256,512]{1,0:T(8,128)(2,1)S(1)}, u32[]{:S(2)}, u32[]{:S(2)}) collective-permute-start(bf16[256,512]{1,0:T(8,128)(2,1)S(1)} %add_convert_fusion.1), channel_id=1, source_target_pairs={{4,0},{5,1},{6,2},{7,3},{8,4},{9,5},{10,6},{11,7},{12,8},{13,9},{1... | collective-permute-start | bytes 786440 | tf_op jit(solution)/shard_map/ppermute | solution.py:250
  65.9 30.2 %collective-permute-start.10 = (bf16[256,512]{1,0:T(8,128)(2,1)S(1)}, bf16[256,512]{1,0:T(8,128)(2,1)S(1)}, u32[]{:S(2)}, u32[]{:S(2)}) collective-permute-start(bf16[256,512]{1,0:T(8,128)(2,1)S(1)} %add_convert_fusion), channel_id=1, source_target_pairs={{4,0},{5,1},{6,2},{7,3},{8,4},{9,5},{10,6},{11,7},{12,8},{13,9},{1... | collective-permute-start | bytes 786440 | tf_op jit(solution)/shard_map/ppermute | solution.py:250
  96.7 6.6 %collective-permute-start.11 = (bf16[256,512]{1,0:T(8,128)(2,1)S(1)}, bf16[256,512]{1,0:T(8,128)(2,1)S(1)}, u32[]{:S(2)}, u32[]{:S(2)}) collective-permute-start(bf16[256,512]{1,0:T(8,128)(2,1)S(1)} %get-tuple-element.56), channel_id=1, source_target_pairs={{0,1},{1,0},{2,3},{3,2},{4,5},{5,4},{6,7},{7,6},{8,9},{9,8},{10,11... | collective-permute-start | bytes 786440 | tf_op jit(solution)/shard_map/ppermute | solution.py:253

commit v4 on v3

--- a/solution.py
+++ b/solution.py
@@ -31,6 +31,20 @@
 
 def dot(a, b, dims=((1,), (0,))):
     return lax.dot_general(a, b, (dims, ((), ())), preferred_element_type=f32)
+
+
+def in_pieces(sums):
+    high = sums.astype(bf16).astype(f32)
+    middle = (sums - high).astype(bf16).astype(f32)
+    low = sums - high - middle
+    row = lax.broadcasted_iota(jnp.int32, (EXTRA, sums.shape[1]), 0)
+    pieces = jnp.where(row == 0, high, jnp.where(row == 1, middle, jnp.where(row == 2, low, 0.0)))
+    return pieces.astype(bf16)
+
+
+def from_pieces(rows):
+    rows = rows.astype(f32)
+    return rows[0:1] + (rows[1:2] + rows[2:3])
 
 
 def attention_kernel(
@@ -61,7 +75,7 @@
 
     for qg, tags, first, att_out, grad_out in (
         (qg_own, kv_own, core, attended, q_grad),
-        (qg_peer, kv_peer, 1 - core, swap.at[:ROWS, : 2 * HEAD], swap.at[:ROWS, 2 * HEAD :]),
+        (qg_peer, kv_peer, 1 - core, swap.at[:, : 2 * HEAD], swap.at[:, 2 * HEAD :]),
     ):
         for h in range(2):
             unit, _ = norm_rows(qg[:, h * HEAD : (h + 1) * HEAD])
@@ -121,26 +135,30 @@
         k_gain_grad = k_gain_grad + jnp.sum(key_grad[block] * unit, axis=0, keepdims=True)
     sums = jnp.concatenate([q_gain_grad, k_gain_grad], axis=1)
     gains[...] = sums
-    high = sums.astype(bf16).astype(f32)
-    middle = (sums - high).astype(bf16).astype(f32)
-    low = sums - high - middle
-    row = lax.broadcasted_iota(jnp.int32, (EXTRA, 2 * HEAD), 0)
-    pieces = jnp.where(row == 0, high, jnp.where(row == 1, middle, jnp.where(row == 2, low, 0.0)))
-    swap[ROWS:, : 2 * HEAD] = pieces.astype(bf16)
-    swap[ROWS:, 2 * HEAD :] = jnp.zeros((EXTRA, 2 * HEAD), bf16)
+    kv_one_first[ROWS:] = in_pieces(sums)
     outs = (kv_two_first, kv_two_second, kv_one_first, kv_one_second, kv_grad_own.at[0], kv_grad_own.at[1])
     for block, out in enumerate(outs):
-        out[:, :HEAD] = key_grad[block].astype(out.dtype)
-        out[:, HEAD:] = value_grad[block].astype(out.dtype)
+        out[:ROWS, :HEAD] = key_grad[block].astype(out.dtype)
+        out[:ROWS, HEAD:] = value_grad[block].astype(out.dtype)
+
+
+def onward_kernel(two, side, gains, onward, x_gains):
+    x = lax.axis_index("x")
+    onward[...] = (two[...].astype(f32) + jnp.where(x == 1, side[:ROWS].astype(f32), 0.0)).astype(bf16)
+    x_gains[...] = gains[...] + from_pieces(side[ROWS:])
 
 
 def finish_kernel(
-    k_gain, kv_own, kv_peer, grad_own, side_first, side_second, ahead_first, ahead_second, own, peer
+    k_gain, kv_own, kv_peer, grad_own, side_first, side_second, ahead_first, ahead_second, gathered,
+    own, peer, gains,
 ):
     core, x = lax.axis_index("core"), lax.axis_index("x")
+    sums = jnp.sum(gathered[...], axis=0, keepdims=True)
+    gains[...] = sums
+    peer[ROWS:] = in_pieces(sums)
     for block, side, ahead in ((0, side_first, ahead_first), (1, side_second, ahead_second)):
         total = grad_own[block] + ahead[...].astype(f32)
-        total = total + jnp.where(x == 0, side[...].astype(f32), 0.0)
+        total = total + jnp.where(x == 0, side[:ROWS].astype(f32), 0.0)
         raw = jnp.where(
             core == block, kv_own[:ROWS, :HEAD].astype(f32), kv_peer[:ROWS, :HEAD].astype(f32)
         )
@@ -155,8 +173,8 @@
 
         @pl.when(core != block)
         def _():
-            peer[:, :HEAD] = key_grad
-            peer[:, HEAD:] = value_grad
+            peer[:ROWS, :HEAD] = key_grad
+            peer[:ROWS, HEAD:] = value_grad
 
 
 def place(out, mine, other):
@@ -174,17 +192,18 @@
         out[:, width:] = mine
 
 
-def join_queries_kernel(att_mine, grad_mine, from_peer, gains, attended, q_grad, pair_gains):
+def join_queries_kernel(att_mine, grad_mine, from_peer, attended, q_grad):
     wide = 2 * HEAD
-    place(attended, att_mine[...], from_peer[:ROWS, :wide])
-    place(q_grad, grad_mine[...], from_peer[:ROWS, wide:])
-    pieces = from_peer[ROWS:, :wide].astype(f32)
-    pair_gains[...] = gains[...] + (pieces[0:1] + (pieces[1:2] + pieces[2:3]))
-
-
-def join_keys_kernel(mine, other, key_grad, value_grad):
-    place(key_grad, mine[:, :HEAD], other[:, :HEAD])
-    place(value_grad, mine[:, HEAD:], other[:, HEAD:])
+    place(attended, att_mine[...], from_peer[:, :wide])
+    place(q_grad, grad_mine[...], from_peer[:, wide:])
+
+
+def join_keys_kernel(mine, other, gains, key_grad, value_grad, q_gain_grad, k_gain_grad):
+    place(key_grad, mine[:, :HEAD], other[:ROWS, :HEAD])
+    place(value_grad, mine[:, HEAD:], other[:ROWS, HEAD:])
+    sums = gains[...] + from_pieces(other[ROWS:])
+    q_gain_grad[...] = sums[:, :HEAD]
+    k_gain_grad[...] = sums[:, HEAD:]
 
 
 def vmem(count):
@@ -198,9 +217,10 @@
         out_shape=(
             shape((ROWS, 2 * HEAD), bf16),
             shape((ROWS, 2 * HEAD), bf16),
-            shape((ROWS + EXTRA, 4 * HEAD), bf16),
+            shape((ROWS, 4 * HEAD), bf16),
             shape((2, ROWS, 2 * HEAD), f32),
-            *(shape((ROWS, 2 * HEAD), bf16),) * 4,
+            shape((ROWS + EXTRA, 2 * HEAD), bf16),
+            *(shape((ROWS, 2 * HEAD), bf16),) * 3,
             shape((1, 2 * HEAD), f32),
         ),
         in_specs=vmem(len(operands)),
@@ -277,43 +297,43 @@
     kv_two, kv_two_x = hop(kv_mine, 2), hop(kv_other, 2, True)
     kv_peer, qg_peer = swap(kv_other), swap(qg_other)
     kv_one = swap(jnp.where(lead, kv_mine, kv_two), "x")
-    kv_one_x = swap(jnp.where(lead, kv_peer, kv_two_x), "x")
+    pairs = [(c, 2 + (1 - c)) for c in range(2)] + [(2 + c, c) for c in range(2)]
+    kv_one_x = lax.ppermute(jnp.where(lead, kv_other, kv_two_x), ("x", "core"), pairs)
     q_gain, k_gain = query_gain[None], key_gain[None]
     attended, q_grad, to_peer, grad_own, one_first, one_second, two_first, two_second, gains = attention(
         q_gain, k_gain, qg_mine, qg_peer, kv_mine, kv_peer, kv_one, kv_one_x, kv_two, kv_two_x
     )
+    side_first, side_second = swap(one_first, "x"), swap(one_second, "x")
+    onward_first, gains = small(
+        onward_kernel,
+        [((ROWS, wide), bf16), ((1, wide), f32)],
+        "onward", two_first, side_first, gains,
+    )
+    onward_second = (two_second.astype(f32) + jnp.where(lead, 0.0, side_second.astype(f32))).astype(bf16)
+    ahead_first, ahead_second = hop(onward_first, -2), hop(onward_second, -2)
+    lines = lax.axis_size("dp") * lax.axis_size("y") * lax.axis_size("z")
+    gathered = lax.all_to_all(
+        jnp.broadcast_to(gains, (lines, wide)), ("dp", "y", "z"), 0, 0, tiled=True
+    )
+    to_peer, _ = lax.optimization_barrier((to_peer, onward_first))
     from_peer = swap(to_peer)
-    side_first, side_second = swap(one_first, "x"), swap(one_second, "x")
-    attended, q_grad, gains = small(
-        join_queries_kernel,
-        [((ROWS, 4 * HEAD), bf16), ((ROWS, 4 * HEAD), bf16), ((1, wide), f32)],
-        "join_queries", attended, q_grad, from_peer, gains,
-    )
-    gains = lax.psum(gains, ("dp", "x"))
-    gains, side_first, side_second = lax.optimization_barrier((gains, side_first, side_second))
-
-    def onward(two, side):
-        return (two.astype(f32) + jnp.where(lead, 0.0, side.astype(f32))).astype(bf16)
-
-    onward_first, onward_second = onward(two_first, side_first), onward(two_second, side_second)
-    gains, onward_first, onward_second = lax.optimization_barrier((gains, onward_first, onward_second))
-    ahead_first, ahead_second = hop(onward_first, -2), hop(onward_second, -2)
-    lines = lax.axis_size("y") * lax.axis_size("z")
-    gathered = lax.all_to_all(
-        jnp.broadcast_to(gains, (lines, wide)), ("y", "z"), 0, 0, tiled=True
+    attended, q_grad = small(
+        join_queries_kernel, [((ROWS, 4 * HEAD), bf16)] * 2, "join_queries", attended, q_grad, from_peer
     )
     gathered, ahead_first, ahead_second = lax.optimization_barrier((gathered, ahead_first, ahead_second))
-    kv_grad, kv_grad_peer = small(
+    kv_grad, kv_grad_peer, gains = small(
         finish_kernel,
-        [((ROWS, wide), bf16)] * 2,
+        [((ROWS, wide), bf16), ((ROWS + EXTRA, wide), bf16), ((1, wide), f32)],
         "finish", k_gain, kv_mine, kv_peer, grad_own, side_first, side_second, ahead_first, ahead_second,
+        gathered,
     )
     kv_grad_x = swap(kv_grad_peer)
-    gains = jnp.sum(gathered, axis=0)
-    key_grad, value_grad = small(
-        join_keys_kernel, [((ROWS, wide), bf16)] * 2, "join_keys", kv_grad, kv_grad_x
-    )
-    return attended[None], q_grad[None], key_grad[None], value_grad[None], gains[:HEAD], gains[HEAD:]
+    key_grad, value_grad, q_gain_grad, k_gain_grad = small(
+        join_keys_kernel,
+        [((ROWS, wide), bf16)] * 2 + [((1, HEAD), f32)] * 2,
+        "join_keys", kv_grad, kv_grad_x, gains,
+    )
+    return attended[None], q_grad[None], key_grad[None], value_grad[None], q_gain_grad[0], k_gain_grad[0]
 
 
 def solution(mesh):

time: 105 us -> 100 us (0.952)
  blocking collectives: 41.7 us -> 0 us
  starting transfers between devices: 35.8 us -> 56.6 us
  waiting for transfers between devices: 10.9 us -> 21.7 us
  local copies, waits for them, and re-layouts: 2.02 us -> 5.01 us
  Pallas kernels: 11.3 us -> 13.2 us
    all_to_all x1 -> x0, blocking collectives: 28.8 us -> none  [per_device(): lax.all_to_all(jnp.broadcast_to(gains, (lines, wide)), ('y', 'z'), 0, 0,...]
    all_to_all x0 -> x1, starting transfers between devices: none -> 18.5 us  [per_device(): lax.all_to_all(jnp.broadcast_to(gains, (lines, wide)), ('dp', 'y', 'z'),...]
    psum x1 -> x0, blocking collectives: 12.8 us -> none  [per_device(): gains = lax.psum(gains, ('dp', 'x'))]
    all_to_all x0 -> x1, waiting for transfers between devices: none -> 5.37 us  [per_device(): lax.all_to_all(jnp.broadcast_to(gains, (lines, wide)), ('dp', 'y', 'z'),...]
    ppermute x0 -> x1, waiting for transfers between devices: none -> 3.55 us  [per_device(): lax.ppermute(jnp.where(lead, kv_other, kv_two_x), ('x', 'core'), pairs)]
    ppermute x0 -> x1, starting transfers between devices: none -> 3.02 us  [per_device(): lax.ppermute(jnp.where(lead, kv_other, kv_two_x), ('x', 'core'), pairs)]
    unnamed x11 -> x17, local copies, waits for them, and re-layouts: 1.38 us -> 4.17 us
    ppermute x4, waiting for transfers between devices: 0.01 us -> 2.7 us  [hop(): lax.ppermute(array, SEQ, [(i, j) for i, j in pairs if 0 <= j < shards])]
  transfers between devices with their start and end apart: 12 -> 13, of which waited for: 3 -> 6; matrix products, arithmetic and copies ran while one was open for 1% -> 3% of each run, Pallas kernels for 1% -> 3%
where the time goes in v4:
time: 100 us; the launch traced here: 99.6 us
  starting transfers between devices  56.6 us (57%)
  waiting for transfers between devices  21.7 us (22%)
  Pallas kernels  13.2 us (13%)
  local copies, waits for them, and re-layouts  5.01 us (5%)
  other arithmetic  2.22 us (2%)
    ppermute x7, starting transfers between devices, swap(): return lax.ppermute(array, axis, [(0, 1), (1, 0)])  25.6 us
    all_to_all x1, starting transfers between devices, per_device(): lax.all_to_all(jnp.broadcast_to(gains, (lines, wide)), ('dp', 'y', 'z'),...  18.5 us
    ppermute x7, waiting for transfers between devices, swap(): return lax.ppermute(array, axis, [(0, 1), (1, 0)])  10.1 us
    pallas_call x1, Pallas kernels, attention(): pl.pallas_call(attention_kernel, out_shape=(shape((ROWS, 2 * HEAD), bf16)...  9.6 us
    ppermute x4, starting transfers between devices, hop(): lax.ppermute(array, SEQ, [(i, j) for i, j in pairs if 0 <= j < shards])  9.41 us
    all_to_all x1, waiting for transfers between devices, per_device(): lax.all_to_all(jnp.broadcast_to(gains, (lines, wide)), ('dp', 'y', 'z'),...  5.37 us
    unnamed x17, local copies, waits for them, and re-layouts  4.17 us
    pallas_call x4, Pallas kernels, small(): pl.pallas_call(kernel, out_shape=tuple((jax.ShapeDtypeStruct(*out) for ou...  3.59 us
  transfers between devices with their start and end apart: 13, of which 6 were waited for; matrix products, arithmetic and copies ran while one was open for 3% of the time, Pallas kernels for 3%

profile of v4, /device:TPU:1, one launch (start us, length us, event | category | flops | bytes accessed | tf_op | source)
XLA Modules:
  0.0 99.6 jit_solution(16611166169317973931)
XLA Ops:
  0.6 0.7 copy-done.7
  1.3 1.1 %broadcast_select_fusion.6 = (bf16[256,256]{1,0:T(8,128)(2,1)S(1)}, bf16[256,256]{1,0:T(8,128)(2,1)S(1)}, bf16[256,256]{1,0:T(8,128)(2,1)S(1)}, bf16[256,256]{1,0:T(8,128)(2,1)S(1)}) fusion(pred[]{:T(512)S(6)} %not.4, bf16[256,512]{1,0:T(8,128)(2,1)} %bitcast.23, pred[]{:T(512)S(6)} %eq.6, bf16[256,512]{1,0:T(8,128)(2,1)} %bitcast.24), kind=kLoop, calls=%fused_computation.14 | loop fusion | flops 262144 | bytes 1048578 | tf_op jit(solution)/shard_map/jit(_where)/select_n | solution.py:282
  2.5 0.0 copy-start.5
  2.5 0.0 copy-start.6
  2.5 5.5 %collective-permute-start.4 = (bf16[272,512]{1,0:T(8,128)(2,1)S(1)}, bf16[272,512]{1,0:T(8,128)(2,1)S(1)}, u32[]{:S(2)}, u32[]{:S(2)}) collective-permute-start(bf16[272,512]{1,0:T(8,128)(2,1)S(1)} %get-tuple-element.33), channel_id=1, source_target_pairs={{0,5},{1,4},{2,7},{3,6},{4,9},{5,8},{6,11},{7,10},{8,13},{9,12},{1... | collective-permute-start | bytes 835592 | tf_op jit(solution)/shard_map/ppermute | solution.py:270
  8.1 4.7 %collective-permute-start.1 = (bf16[272,512]{1,0:T(8,128)(2,1)S(1)}, bf16[272,512]{1,0:T(8,128)(2,1)S(1)}, u32[]{:S(2)}, u32[]{:S(2)}) collective-permute-start(bf16[272,512]{1,0:T(8,128)(2,1)S(1)} %get-tuple-element.33), channel_id=1, source_target_pairs={{0,1},{1,0},{2,3},{3,2},{4,5},{5,4},{6,7},{7,6},{8,9},{9,8},{10,11... | collective-permute-start | bytes 835592 | tf_op jit(solution)/shard_map/ppermute | solution.py:273
  12.8 1.3 %collective-permute-start.2 = (bf16[272,512]{1,0:T(8,128)(2,1)S(1)}, bf16[272,512]{1,0:T(8,128)(2,1)S(1)}, u32[]{:S(2)}, u32[]{:S(2)}) collective-permute-start(bf16[272,512]{1,0:T(8,128)(2,1)S(1)} %get-tuple-element.32.kv_own), channel_id=1, source_target_pairs={{0,4},{1,5},{2,6},{3,7},{4,8},{5,9},{6,10},{7,11},{8,12},{9,13},{1... | collective-permute-start | bytes 835592 | tf_op jit(solution)/shard_map/ppermute | solution.py:270
  14.1 0.1 broadcast_select_fusion.2
  14.2 0.1 pad_maximum_fusion.1
  14.3 2.6 %collective-permute-start = (bf16[256,1024]{1,0:T(8,128)(2,1)S(1)}, bf16[256,1024]{1,0:T(8,128)(2,1)S(1)}, u32[]{:S(2)}, u32[]{:S(2)}) collective-permute-start(bf16[256,1024]{1,0:T(8,128)(2,1)S(1)} %pad_maximum_fusion.1), channel_id=1, source_target_pairs={{0,1},{1,0},{2,3},{3,2},{4,5},{5,4},{6,7},{7,6},{8,9},{9,8},{10,11... | collective-permute-start | bytes 1572872 | tf_op jit(solution)/shard_map/ppermute | solution.py:273
  16.9 0.0 collective-permute-done.4.kv_two_x
  16.9 3.0 %collective-permute-start.5 = (bf16[272,512]{1,0:T(8,128)(2,1)S(1)}, bf16[272,512]{1,0:T(8,128)(2,1)S(1)}, u32[]{:S(2)}, u32[]{:S(2)}) collective-permute-start(bf16[272,512]{1,0:T(8,128)(2,1)S(1)} %broadcast_select_fusion), channel_id=1, source_target_pairs={{0,3},{1,2},{2,0},{3,1},{4,7},{5,6},{6,4},{7,5},{8,11},{9,10},{10,... | collective-permute-start | bytes 835592 | tf_op jit(solution)/shard_map/ppermute | solution.py:301
  20.0 0.0 collective-permute-done.2.kv_two
  20.0 2.6 %collective-permute-start.3 = (bf16[272,512]{1,0:T(8,128)(2,1)S(1)}, bf16[272,512]{1,0:T(8,128)(2,1)S(1)}, u32[]{:S(2)}, u32[]{:S(2)}) collective-permute-start(bf16[272,512]{1,0:T(8,128)(2,1)S(1)} %broadcast_select_fusion.1), channel_id=1, source_target_pairs={{0,2},{2,0},{1,3},{3,1},{4,6},{6,4},{5,7},{7,5},{8,10},{10,8},{9,1... | collective-permute-start | bytes 835592 | tf_op jit(solution)/shard_map/ppermute | solution.py:273
  22.7 0.0 copy-start.4
  22.7 0.1 pad_maximum_fusion.qg_own
  22.7 0.0 collective-permute-done.1.kv_peer
  22.7 0.0 collective-permute-done.qg_peer
  22.8 0.0 copy-start.1
  22.8 0.8 copy-done.1
  23.5 3.6 %collective-permute-done.5.kv_one_x = bf16[272,512]{1,0:T(8,128)(2,1)S(1)} collective-permute-done((bf16[272,512]{1,0:T(8,128)(2,1)S(1)}, bf16[272,512]{1,0:T(8,128)(2,1)S(1)}, u32[]{:S(2)}, u32[]{:S(2)}) %collective-permute-start.5) | collective-permute-done | bytes 278560 | tf_op jit(solution)/shard_map/ppermute | solution.py:301
  27.1 6.0 %collective-permute-done.3.kv_one = bf16[272,512]{1,0:T(8,128)(2,1)S(1)} collective-permute-done((bf16[272,512]{1,0:T(8,128)(2,1)S(1)}, bf16[272,512]{1,0:T(8,128)(2,1)S(1)}, u32[]{:S(2)}, u32[]{:S(2)}) %collective-permute-start.3) | collective-permute-done | bytes 278560 | tf_op jit(solution)/shard_map/ppermute | solution.py:273
  33.1 0.0 copy-done.4
  33.1 0.7 copy-done
  33.8 1.0 %copy-done.2 = bf16[256,1024]{1,0:T(8,128)(2,1)S(1)} copy-done((bf16[256,1024]{1,0:T(8,128)(2,1)S(1)}, bf16[256,1024]{1,0:T(8,128)(2,1)}, u32[]{:S(2)}) %copy-start.2) | copy-done | bytes 524312
  34.8 9.6 %attention.1 = (bf16[256,512]{1,0:T(8,128)(2,1)S(1)}, bf16[256,512]{1,0:T(8,128)(2,1)S(1)}, bf16[256,1024]{1,0:T(8,128)(2,1)}, f32[2,256,512]{2,1,0:T(8,128)S(1)...) custom-call(f32[1,256]{1,0:T(1,128)S(1)} %bitcast.20, ...), custom_call_target="tpu_custom_call" | custom-call | flops 8589934592 | bytes 8388608 | tf_op jit(solution)/shard_map/attention/pallas_call | solution.py:215
  44.4 2.8 %collective-permute-start.6 = (bf16[272,512]{1,0:T(8,128)(2,1)S(1)}, bf16[272,512]{1,0:T(8,128)(2,1)S(1)}, u32[]{:S(2)}, u32[]{:S(2)}) collective-permute-start(bf16[272,512]{1,0:T(8,128)(2,1)S(1)} %get-tuple-element.38), channel_id=1, source_target_pairs={{0,2},{2,0},{1,3},{3,1},{4,6},{6,4},{5,7},{7,5},{8,10},{10,8},{9,1... | collective-permute-start | bytes 835592 | tf_op jit(solution)/shard_map/ppermute | solution.py:273
  47.2 2.5 %collective-permute-start.8 = (bf16[256,512]{1,0:T(8,128)(2,1)}, bf16[256,512]{1,0:T(8,128)(2,1)S(1)}, u32[]{:S(2)}, u32[]{:S(2)}) collective-permute-start(bf16[256,512]{1,0:T(8,128)(2,1)} %get-tuple-element.45), channel_id=1, source_target_pairs={{0,2},{2,0},{1,3},{3,1},{4,6},{6,4},{5,7},{7,5},{8,10},{10,8},{9,1... | collective-permute-start | bytes 786440 | tf_op jit(solution)/shard_map/ppermute | solution.py:273
  49.7 4.0 %collective-permute-done.6.side.side_first = bf16[272,512]{1,0:T(8,128)(2,1)S(1)} collective-permute-done((bf16[272,512]{1,0:T(8,128)(2,1)S(1)}, bf16[272,512]{1,0:T(8,128)(2,1)S(1)}, u32[]{:S(2)}, u32[]{:S(2)}) %collective-permute-start.6) | collective-permute-done | bytes 278560 | tf_op jit(solution)/shard_map/ppermute | solution.py:273
  53.7 0.1 onward.1
  53.8 0.0 copy-start.3
  53.8 0.8 broadcast_in_dim.32
  54.7 18.5 %all-to-all-start = ((f32[128,1,512]{2,1,0:T(1,128)}), f32[128,1,512]{2,1,0:T(1,128)}, u32[]{:S(2)}, u32[]{:S(2)}) async-start(f32[128,1,512]{2,1,0:T(1,128)} %broadcast_in_dim.32), calls=%async_computation | async-start | bytes 524288 | tf_op jit(solution)/shard_map/all_to_all | solution.py:315
  73.2 0.0 collective-permute-done.8.side_second
  73.2 0.8 add_convert_fusion
  74.0 1.3 %collective-permute-start.10 = (bf16[256,512]{1,0:T(8,128)(2,1)}, bf16[256,512]{1,0:T(8,128)(2,1)S(1)}, u32[]{:S(2)}, u32[]{:S(2)}) collective-permute-start(bf16[256,512]{1,0:T(8,128)(2,1)} %add_convert_fusion), channel_id=1, source_target_pairs={{4,0},{5,1},{6,2},{7,3},{8,4},{9,5},{10,6},{11,7},{12,8},{13,9},{1... | collective-permute-start | bytes 786440 | tf_op jit(solution)/shard_map/ppermute | solution.py:270
  75.3 1.3 %collective-permute-start.9 = (bf16[256,512]{1,0:T(8,128)(2,1)}, bf16[256,512]{1,0:T(8,128)(2,1)}, u32[]{:S(2)}, u32[]{:S(2)}) collective-permute-start(bf16[256,512]{1,0:T(8,128)(2,1)} %copy-done.3), channel_id=1, source_target_pairs={{4,0},{5,1},{6,2},{7,3},{8,4},{9,5},{10,6},{11,7},{12,8},{13,9},{1... | collective-permute-start | bytes 786440 | tf_op jit(solution)/shard_map/ppermute | solution.py:270
  76.6 6.0 %collective-permute-start.7 = (bf16[256,1024]{1,0:T(8,128)(2,1)}, bf16[256,1024]{1,0:T(8,128)(2,1)S(1)}, u32[]{:S(2)}, u32[]{:S(2)}) collective-permute-start(bf16[256,1024]{1,0:T(8,128)(2,1)} %get-tuple-element.41), channel_id=1, source_target_pairs={{0,1},{1,0},{2,3},{3,2},{4,5},{5,4},{6,7},{7,6},{8,9},{9,8},{10,11... | collective-permute-start | bytes 1572872 | tf_op jit(solution)/shard_map/ppermute | solution.py:273
  82.6 5.4 %all-to-all-done = f32[128,1,512]{2,1,0:T(1,128)} async-done(((f32[128,1,512]{2,1,0:T(1,128)}), f32[128,1,512]{2,1,0:T(1,128)}, u32[]{:S(2)}, u32[]{:S(2)}) %all-to-all-start) | async-done | bytes 262176 | tf_op jit(solution)/shard_map/all_to_all | solution.py:315
  88.0 1.0 copy.15
  88.9 0.0 collective-permute-done.10.ahead_second
  89.0 2.7 %collective-permute-done.9.ahead_first = bf16[256,512]{1,0:T(8,128)(2,1)} collective-permute-done((bf16[256,512]{1,0:T(8,128)(2,1)}, bf16[256,512]{1,0:T(8,128)(2,1)}, u32[]{:S(2)}, u32[]{:S(2)}) %collective-permute-start.9) | collective-permute-done | bytes 262176 | tf_op jit(solution)/shard_map/ppermute | solution.py:270
  91.6 1.5 %finish.1 = (bf16[256,512]{1,0:T(8,128)(2,1)S(1)}, bf16[272,512]{1,0:T(8,128)(2,1)S(1)}, f32[1,512]{1,0:T(1,128)S(1)}) custom-call(f32[1,256]{1,0:T(1,128)S(1)} %bitcast.19, bf16[272,512]{1,0:T(8,128)(2,1)S(1)} %get-tuple-element.32.kv_own, bf16[272,512]{1,0:T(8,128)(2,1)S(1)} %collective-permute-done.1.kv_peer, ...), custom_call_target="tpu_custom_call" | custom-call | tf_op jit(solution)/shard_map/finish/pallas_call | solution.py:250
  93.2 4.4 %collective-permute-start.11 = (bf16[272,512]{1,0:T(8,128)(2,1)S(1)}, bf16[272,512]{1,0:T(8,128)(2,1)S(1)}, u32[]{:S(2)}, u32[]{:S(2)}) collective-permute-start(bf16[272,512]{1,0:T(8,128)(2,1)S(1)} %get-tuple-element.52), channel_id=1, source_target_pairs={{0,1},{1,0},{2,3},{3,2},{4,5},{5,4},{6,7},{7,6},{8,9},{9,8},{10,11... | collective-permute-start | bytes 835592 | tf_op jit(solution)/shard_map/ppermute | solution.py:273
  97.6 0.0 collective-permute-done.7.from_peer
  97.6 1.1 %join_queries.1 = (bf16[256,1024]{1,0:T(8,128)(2,1)}, bf16[256,1024]{1,0:T(8,128)(2,1)}) custom-call(bf16[256,512]{1,0:T(8,128)(2,1)S(1)} %get-tuple-element.34.att_mine, bf16[256,512]{1,0:T(8,128)(2,1)S(1)} %get-tuple-element.35.grad_mine, bf16[256,1024]{1,0:T(8,128)(2,1)S(1)} %collective-permute-done.7.from_peer), custom_call_target="tpu_custom_call" | custom-call | tf_op jit(solution)/shard_map/join_queries/pallas_call | solution.py:250
  98.7 0.1 collective-permute-done.11.other
  98.7 0.9 join_keys.1
  (10 shorter events, 0.1 us)
Async XLA Ops:
  0.6 0.7 copy-start.7
  2.5 11.6 %copy-start.5 = (bf16[1,256,1024]{2,1,0:T(8,128)(2,1)S(1)}, bf16[1,256,1024]{2,1,0:T(8,128)(2,1)}, u32[]{:S(2)}) copy-start(bf16[1,256,1024]{2,1,0:T(8,128)(2,1)} %param.10) | copy-start | bytes 1572868
  2.5 11.6 %copy-start.6 = (bf16[1,256,1024]{2,1,0:T(8,128)(2,1)S(1)}, bf16[1,256,1024]{2,1,0:T(8,128)(2,1)}, u32[]{:S(2)}) copy-start(bf16[1,256,1024]{2,1,0:T(8,128)(2,1)} %param.7) | copy-start | bytes 1572868
  2.5 14.3 %collective-permute-start.4 = (bf16[272,512]{1,0:T(8,128)(2,1)S(1)}, bf16[272,512]{1,0:T(8,128)(2,1)S(1)}, u32[]{:S(2)}, u32[]{:S(2)}) collective-permute-start(bf16[272,512]{1,0:T(8,128)(2,1)S(1)} %get-tuple-element.33), channel_id=1, source_target_pairs={{0,5},{1,4},{2,7},{3,6},{4,9},{5,8},{6,11},{7,10},{8,13},{9,12},{1... | collective-permute-start | bytes 835592 | tf_op jit(solution)/shard_map/ppermute | solution.py:270
  8.1 14.7 %collective-permute-start.1 = (bf16[272,512]{1,0:T(8,128)(2,1)S(1)}, bf16[272,512]{1,0:T(8,128)(2,1)S(1)}, u32[]{:S(2)}, u32[]{:S(2)}) collective-permute-start(bf16[272,512]{1,0:T(8,128)(2,1)S(1)} %get-tuple-element.33), channel_id=1, source_target_pairs={{0,1},{1,0},{2,3},{3,2},{4,5},{5,4},{6,7},{7,6},{8,9},{9,8},{10,11... | collective-permute-start | bytes 835592 | tf_op jit(solution)/shard_map/ppermute | solution.py:273
  12.8 7.2 %collective-permute-start.2 = (bf16[272,512]{1,0:T(8,128)(2,1)S(1)}, bf16[272,512]{1,0:T(8,128)(2,1)S(1)}, u32[]{:S(2)}, u32[]{:S(2)}) collective-permute-start(bf16[272,512]{1,0:T(8,128)(2,1)S(1)} %get-tuple-element.32.kv_own), channel_id=1, source_target_pairs={{0,4},{1,5},{2,6},{3,7},{4,8},{5,9},{6,10},{7,11},{8,12},{9,13},{1... | collective-permute-start | bytes 835592 | tf_op jit(solution)/shard_map/ppermute | solution.py:270
  14.3 8.5 %collective-permute-start = (bf16[256,1024]{1,0:T(8,128)(2,1)S(1)}, bf16[256,1024]{1,0:T(8,128)(2,1)S(1)}, u32[]{:S(2)}, u32[]{:S(2)}) collective-permute-start(bf16[256,1024]{1,0:T(8,128)(2,1)S(1)} %pad_maximum_fusion.1), channel_id=1, source_target_pairs={{0,1},{1,0},{2,3},{3,2},{4,5},{5,4},{6,7},{7,6},{8,9},{9,8},{10,11... | collective-permute-start | bytes 1572872 | tf_op jit(solution)/shard_map/ppermute | solution.py:273
  16.9 10.2 %collective-permute-start.5 = (bf16[272,512]{1,0:T(8,128)(2,1)S(1)}, bf16[272,512]{1,0:T(8,128)(2,1)S(1)}, u32[]{:S(2)}, u32[]{:S(2)}) collective-permute-start(bf16[272,512]{1,0:T(8,128)(2,1)S(1)} %broadcast_select_fusion), channel_id=1, source_target_pairs={{0,3},{1,2},{2,0},{3,1},{4,7},{5,6},{6,4},{7,5},{8,11},{9,10},{10,... | collective-permute-start | bytes 835592 | tf_op jit(solution)/shard_map/ppermute | solution.py:301
  20.0 13.1 %collective-permute-start.3 = (bf16[272,512]{1,0:T(8,128)(2,1)S(1)}, bf16[272,512]{1,0:T(8,128)(2,1)S(1)}, u32[]{:S(2)}, u32[]{:S(2)}) collective-permute-start(bf16[272,512]{1,0:T(8,128)(2,1)S(1)} %broadcast_select_fusion.1), channel_id=1, source_target_pairs={{0,2},{2,0},{1,3},{3,1},{4,6},{6,4},{5,7},{7,5},{8,10},{10,8},{9,1... | collective-permute-start | bytes 835592 | tf_op jit(solution)/shard_map/ppermute | solution.py:273
  22.7 10.4 %copy-start.4 = (f32[256]{0:T(256)S(1)}, f32[256]{0:T(256)}, u32[]{:S(2)}) copy-start(f32[256]{0:T(256)} %param.11) | copy-start | bytes 3076
  22.8 0.8 copy-start.1
  33.1 0.7 copy-start
  33.8 1.0 %copy-start.2 = (bf16[256,1024]{1,0:T(8,128)(2,1)S(1)}, bf16[256,1024]{1,0:T(8,128)(2,1)}, u32[]{:S(2)}) copy-start(bf16[256,1024]{1,0:T(8,128)(2,1)} %copy-done.1) | copy-start | bytes 1572868
  44.4 9.3 %collective-permute-start.6 = (bf16[272,512]{1,0:T(8,128)(2,1)S(1)}, bf16[272,512]{1,0:T(8,128)(2,1)S(1)}, u32[]{:S(2)}, u32[]{:S(2)}) collective-permute-start(bf16[272,512]{1,0:T(8,128)(2,1)S(1)} %get-tuple-element.38), channel_id=1, source_target_pairs={{0,2},{2,0},{1,3},{3,1},{4,6},{6,4},{5,7},{7,5},{8,10},{10,8},{9,1... | collective-permute-start | bytes 835592 | tf_op jit(solution)/shard_map/ppermute | solution.py:273
  47.2 26.0 %collective-permute-start.8 = (bf16[256,512]{1,0:T(8,128)(2,1)}, bf16[256,512]{1,0:T(8,128)(2,1)S(1)}, u32[]{:S(2)}, u32[]{:S(2)}) collective-permute-start(bf16[256,512]{1,0:T(8,128)(2,1)} %get-tuple-element.45), channel_id=1, source_target_pairs={{0,2},{2,0},{1,3},{3,1},{4,6},{6,4},{5,7},{7,5},{8,10},{10,8},{9,1... | collective-permute-start | bytes 786440 | tf_op jit(solution)/shard_map/ppermute | solution.py:273
  53.8 19.4 %copy-start.3 = (bf16[256,512]{1,0:T(8,128)(2,1)}, bf16[256,512]{1,0:T(8,128)(2,1)S(1)}, u32[]{:S(2)}) copy-start(bf16[256,512]{1,0:T(8,128)(2,1)S(1)} %get-tuple-element.40) | copy-start | bytes 786436
  54.7 33.3 %all-to-all-start = ((f32[128,1,512]{2,1,0:T(1,128)}), f32[128,1,512]{2,1,0:T(1,128)}, u32[]{:S(2)}, u32[]{:S(2)}) async-start(f32[128,1,512]{2,1,0:T(1,128)} %broadcast_in_dim.32), calls=%async_computation | async-start | bytes 524288 | tf_op jit(solution)/shard_map/all_to_all | solution.py:315
  74.0 14.9 %collective-permute-start.10 = (bf16[256,512]{1,0:T(8,128)(2,1)}, bf16[256,512]{1,0:T(8,128)(2,1)S(1)}, u32[]{:S(2)}, u32[]{:S(2)}) collective-permute-start(bf16[256,512]{1,0:T(8,128)(2,1)} %add_convert_fusion), channel_id=1, source_target_pairs={{4,0},{5,1},{6,2},{7,3},{8,4},{9,5},{10,6},{11,7},{12,8},{13,9},{1... | collective-permute-start | bytes 786440 | tf_op jit(solution)/shard_map/ppermute | solution.py:270
  75.3 16.3 %collective-permute-start.9 = (bf16[256,512]{1,0:T(8,128)(2,1)}, bf16[256,512]{1,0:T(8,128)(2,1)}, u32[]{:S(2)}, u32[]{:S(2)}) collective-permute-start(bf16[256,512]{1,0:T(8,128)(2,1)} %copy-done.3), channel_id=1, source_target_pairs={{4,0},{5,1},{6,2},{7,3},{8,4},{9,5},{10,6},{11,7},{12,8},{13,9},{1... | collective-permute-start | bytes 786440 | tf_op jit(solution)/shard_map/ppermute | solution.py:270
  76.6 21.0 %collective-permute-start.7 = (bf16[256,1024]{1,0:T(8,128)(2,1)}, bf16[256,1024]{1,0:T(8,128)(2,1)S(1)}, u32[]{:S(2)}, u32[]{:S(2)}) collective-permute-start(bf16[256,1024]{1,0:T(8,128)(2,1)} %get-tuple-element.41), channel_id=1, source_target_pairs={{0,1},{1,0},{2,3},{3,2},{4,5},{5,4},{6,7},{7,6},{8,9},{9,8},{10,11... | collective-permute-start | bytes 1572872 | tf_op jit(solution)/shard_map/ppermute | solution.py:273
  93.2 5.6 %collective-permute-start.11 = (bf16[272,512]{1,0:T(8,128)(2,1)S(1)}, bf16[272,512]{1,0:T(8,128)(2,1)S(1)}, u32[]{:S(2)}, u32[]{:S(2)}) collective-permute-start(bf16[272,512]{1,0:T(8,128)(2,1)S(1)} %get-tuple-element.52), channel_id=1, source_target_pairs={{0,1},{1,0},{2,3},{3,2},{4,5},{5,4},{6,7},{7,6},{8,9},{9,8},{10,11... | collective-permute-start | bytes 835592 | tf_op jit(solution)/shard_map/ppermute | solution.py:273

commit v5 on v4

--- a/solution.py
+++ b/solution.py
@@ -48,8 +48,8 @@
 
 
 def attention_kernel(
-    q_gain, k_gain, qg_own, qg_peer, kv_own, kv_peer, kv_one, kv_one_x, kv_two, kv_two_x,
-    attended, q_grad, swap, kv_grad_own, kv_one_first, kv_one_second, kv_two_first, kv_two_second, gains,
+    gain, qg_own, qg_peer, kv_own, kv_peer, kv_one, kv_one_x, kv_two, kv_two_x,
+    attended, q_grad, swap, kv_grad_own, kv_grad_one, kv_grad_two, gains,
     key, key_t, value, value_t, tag, key_grad, value_grad, score, query, upstream, upstream_t,
 ):
     core = lax.axis_index("core")
@@ -59,7 +59,7 @@
     )
     for part, block in parts:
         unit, _ = norm_rows(part[:ROWS, :HEAD])
-        normed = (unit * k_gain[...]).astype(bf16)
+        normed = (unit * gain[:, HEAD:]).astype(bf16)
         key[block] = normed
         key_t[block] = normed.T
         value[block] = part[:ROWS, HEAD:]
@@ -79,7 +79,7 @@
     ):
         for h in range(2):
             unit, _ = norm_rows(qg[:, h * HEAD : (h + 1) * HEAD])
-            normed = (unit * q_gain[...]).astype(bf16)
+            normed = (unit * gain[:, :HEAD]).astype(bf16)
             query[h * ROWS : (h + 1) * ROWS] = normed * jnp.asarray(SCALE, bf16)
             up = qg[:, (2 + h) * HEAD : (3 + h) * HEAD]
             upstream[h * ROWS : (h + 1) * ROWS] = up
@@ -126,7 +126,7 @@
             unit, inverse = norm_rows(qg[:, h * HEAD : (h + 1) * HEAD])
             q_gain_grad = q_gain_grad + jnp.sum(normed_grad * unit, axis=0, keepdims=True)
             grad_out[:, h * HEAD : (h + 1) * HEAD] = norm_backward(
-                normed_grad, unit, inverse, q_gain[...]
+                normed_grad, unit, inverse, gain[:, :HEAD]
             ).astype(bf16)
 
     k_gain_grad = jnp.zeros((1, HEAD), f32)
@@ -135,46 +135,24 @@
         k_gain_grad = k_gain_grad + jnp.sum(key_grad[block] * unit, axis=0, keepdims=True)
     sums = jnp.concatenate([q_gain_grad, k_gain_grad], axis=1)
     gains[...] = sums
-    kv_one_first[ROWS:] = in_pieces(sums)
-    outs = (kv_two_first, kv_two_second, kv_one_first, kv_one_second, kv_grad_own.at[0], kv_grad_own.at[1])
-    for block, out in enumerate(outs):
-        out[:ROWS, :HEAD] = key_grad[block].astype(out.dtype)
-        out[:ROWS, HEAD:] = value_grad[block].astype(out.dtype)
-
-
-def onward_kernel(two, side, gains, onward, x_gains):
-    x = lax.axis_index("x")
-    onward[...] = (two[...].astype(f32) + jnp.where(x == 1, side[:ROWS].astype(f32), 0.0)).astype(bf16)
-    x_gains[...] = gains[...] + from_pieces(side[ROWS:])
+    for i in range(2):
+        for at, out in ((0, kv_grad_two), (2, kv_grad_one), (4, kv_grad_own)):
+            out[i, :, :HEAD] = key_grad[at + i].astype(out.dtype)
+            out[i, :, HEAD:] = value_grad[at + i].astype(out.dtype)
 
 
 def finish_kernel(
-    k_gain, kv_own, kv_peer, grad_own, side_first, side_second, ahead_first, ahead_second, gathered,
-    own, peer, gains,
+    gain, kv_own, kv_peer, grad_own, grad_one, grad_two, gathered, own, peer, gains
 ):
-    core, x = lax.axis_index("core"), lax.axis_index("x")
+    core = lax.axis_index("core")
     sums = jnp.sum(gathered[...], axis=0, keepdims=True)
     gains[...] = sums
     peer[ROWS:] = in_pieces(sums)
-    for block, side, ahead in ((0, side_first, ahead_first), (1, side_second, ahead_second)):
-        total = grad_own[block] + ahead[...].astype(f32)
-        total = total + jnp.where(x == 0, side[:ROWS].astype(f32), 0.0)
-        raw = jnp.where(
-            core == block, kv_own[:ROWS, :HEAD].astype(f32), kv_peer[:ROWS, :HEAD].astype(f32)
-        )
-        unit, inverse = norm_rows(raw)
-        key_grad = norm_backward(total[:, :HEAD], unit, inverse, k_gain[...]).astype(bf16)
-        value_grad = total[:, HEAD:].astype(bf16)
-
-        @pl.when(core == block)
-        def _():
-            own[:, :HEAD] = key_grad
-            own[:, HEAD:] = value_grad
-
-        @pl.when(core != block)
-        def _():
-            peer[:ROWS, :HEAD] = key_grad
-            peer[:ROWS, HEAD:] = value_grad
+    for part, block, out in ((kv_own, core, own), (kv_peer, 1 - core, peer)):
+        total = grad_own[block] + grad_one[block].astype(f32) + grad_two[block].astype(f32)
+        unit, inverse = norm_rows(part[:ROWS, :HEAD])
+        out[:ROWS, :HEAD] = norm_backward(total[:, :HEAD], unit, inverse, gain[:, HEAD:]).astype(bf16)
+        out[:ROWS, HEAD:] = total[:, HEAD:].astype(bf16)
 
 
 def place(out, mine, other):
@@ -219,12 +197,11 @@
             shape((ROWS, 2 * HEAD), bf16),
             shape((ROWS, 4 * HEAD), bf16),
             shape((2, ROWS, 2 * HEAD), f32),
-            shape((ROWS + EXTRA, 2 * HEAD), bf16),
-            *(shape((ROWS, 2 * HEAD), bf16),) * 3,
+            *(shape((2, ROWS, 2 * HEAD), bf16),) * 2,
             shape((1, 2 * HEAD), f32),
         ),
         in_specs=vmem(len(operands)),
-        out_specs=tuple(vmem(9)),
+        out_specs=tuple(vmem(7)),
         scratch_shapes=[
             pltpu.VMEM((BLOCKS, ROWS, HEAD), bf16),
             pltpu.VMEM((BLOCKS, HEAD, ROWS), bf16),
@@ -238,7 +215,7 @@
             pltpu.VMEM((2 * ROWS, HEAD), bf16),
             pltpu.VMEM((HEAD, 2 * ROWS), bf16),
         ],
-        compiler_params=pltpu.CompilerParams(vmem_limit_bytes=40 << 20),
+        compiler_params=pltpu.CompilerParams(vmem_limit_bytes=28 << 20),
         cost_estimate=pl.CostEstimate(
             flops=8 << 30, bytes_accessed=8 << 20, transcendentals=3 << 20
         ),
@@ -275,7 +252,7 @@
     first, lead = core == 0, lax.axis_index("x") == 0
     ids = jnp.pad((document_ids[0] + 1).astype(bf16)[None], ((0, EXTRA - 1), (0, wide - ROWS)))
 
-    def pack(mine):
+    def pack(mine, keys, values):
         return jnp.concatenate(
             [
                 jnp.concatenate(
@@ -286,7 +263,14 @@
             axis=0,
         )
 
-    kv_mine, kv_other = lax.optimization_barrier((pack(first), pack(~first)))
+    gain = jnp.concatenate([query_gain, key_gain])[None]
+    kv_mine, kv_other, lead = lax.optimization_barrier(
+        (pack(first, keys, values), pack(~first, keys, values), lead)
+    )
+    kv_two, kv_two_x, kv_one_x = hop(kv_mine, 2), hop(kv_other, 2, True), hop(kv_other, 1, True)
+    kv_one = swap(jnp.where(lead, kv_mine, kv_two), "x")
+    kv_peer = swap(kv_other)
+    gain, kv_peer = lax.optimization_barrier((gain, kv_peer))
 
     def pack_queries(mine):
         return jnp.concatenate(
@@ -294,38 +278,24 @@
         )
 
     qg_mine, qg_other = pack_queries(first), pack_queries(~first)
-    kv_two, kv_two_x = hop(kv_mine, 2), hop(kv_other, 2, True)
-    kv_peer, qg_peer = swap(kv_other), swap(qg_other)
-    kv_one = swap(jnp.where(lead, kv_mine, kv_two), "x")
-    pairs = [(c, 2 + (1 - c)) for c in range(2)] + [(2 + c, c) for c in range(2)]
-    kv_one_x = lax.ppermute(jnp.where(lead, kv_other, kv_two_x), ("x", "core"), pairs)
-    q_gain, k_gain = query_gain[None], key_gain[None]
-    attended, q_grad, to_peer, grad_own, one_first, one_second, two_first, two_second, gains = attention(
-        q_gain, k_gain, qg_mine, qg_peer, kv_mine, kv_peer, kv_one, kv_one_x, kv_two, kv_two_x
-    )
-    side_first, side_second = swap(one_first, "x"), swap(one_second, "x")
-    onward_first, gains = small(
-        onward_kernel,
-        [((ROWS, wide), bf16), ((1, wide), f32)],
-        "onward", two_first, side_first, gains,
-    )
-    onward_second = (two_second.astype(f32) + jnp.where(lead, 0.0, side_second.astype(f32))).astype(bf16)
-    ahead_first, ahead_second = hop(onward_first, -2), hop(onward_second, -2)
+    qg_peer = swap(qg_other)
+    attended, q_grad, to_peer, grad_own, grad_one, grad_two, gains = attention(
+        gain, qg_mine, qg_peer, kv_mine, kv_peer, kv_one, kv_one_x, kv_two, kv_two_x
+    )
+    gains = gains + swap(gains, "x")
+    grad_two, grad_one = hop(grad_two, -2), hop(grad_one, -1)
+    from_peer = swap(to_peer)
     lines = lax.axis_size("dp") * lax.axis_size("y") * lax.axis_size("z")
     gathered = lax.all_to_all(
         jnp.broadcast_to(gains, (lines, wide)), ("dp", "y", "z"), 0, 0, tiled=True
     )
-    to_peer, _ = lax.optimization_barrier((to_peer, onward_first))
-    from_peer = swap(to_peer)
     attended, q_grad = small(
         join_queries_kernel, [((ROWS, 4 * HEAD), bf16)] * 2, "join_queries", attended, q_grad, from_peer
     )
-    gathered, ahead_first, ahead_second = lax.optimization_barrier((gathered, ahead_first, ahead_second))
     kv_grad, kv_grad_peer, gains = small(
         finish_kernel,
         [((ROWS, wide), bf16), ((ROWS + EXTRA, wide), bf16), ((1, wide), f32)],
-        "finish", k_gain, kv_mine, kv_peer, grad_own, side_first, side_second, ahead_first, ahead_second,
-        gathered,
+        "finish", gain, kv_mine, kv_peer, grad_own, grad_one, grad_two, gathered,
     )
     kv_grad_x = swap(kv_grad_peer)
     key_grad, value_grad, q_gain_grad, k_gain_grad = small(

time: 100 us -> 105 us (1.050)
  starting transfers between devices: 56.6 us -> 61 us
  waiting for transfers between devices: 21.7 us -> 25.5 us
  Pallas kernels: 13.2 us -> 11.9 us
    all_to_all x1, starting transfers between devices: 18.5 us -> 24.2 us  [per_device(): lax.all_to_all(jnp.broadcast_to(gains, (lines, wide)), ('dp', 'y', 'z'),...]
    all_to_all x1, waiting for transfers between devices: 5.37 us -> 11 us  [per_device(): lax.all_to_all(jnp.broadcast_to(gains, (lines, wide)), ('dp', 'y', 'z'),...]
    ppermute x7 -> x6, waiting for transfers between devices: 10.1 us -> 14.3 us  [swap(): return lax.ppermute(array, axis, [(0, 1), (1, 0)])]
    ppermute x1 -> x0, waiting for transfers between devices: 3.55 us -> none  [per_device(): lax.ppermute(jnp.where(lead, kv_other, kv_two_x), ('x', 'core'), pairs)]
    ppermute x4 -> x5, starting transfers between devices: 9.41 us -> 12.6 us  [hop(): lax.ppermute(array, SEQ, [(i, j) for i, j in pairs if 0 <= j < shards])]
    ppermute x1 -> x0, starting transfers between devices: 3.02 us -> none  [per_device(): lax.ppermute(jnp.where(lead, kv_other, kv_two_x), ('x', 'core'), pairs)]
    ppermute x4 -> x5, waiting for transfers between devices: 2.7 us -> 0.2 us  [hop(): lax.ppermute(array, SEQ, [(i, j) for i, j in pairs if 0 <= j < shards])]
    ppermute x7 -> x6, starting transfers between devices: 25.6 us -> 24.2 us  [swap(): return lax.ppermute(array, axis, [(0, 1), (1, 0)])]
  transfers between devices with their start and end apart: 13 -> 12, of which waited for: 6 -> 4; matrix products, arithmetic and copies ran while one was open for 3% -> 2% of each run, Pallas kernels for 3% -> 1%
where the time goes in v5:
time: 105 us
  starting transfers between devices  61 us (58%)
  waiting for transfers between devices  25.5 us (24%)
  Pallas kernels  11.9 us (11%)
  local copies, waits for them, and re-layouts  4.02 us (4%)
  other arithmetic  1.41 us (1%)
    all_to_all x1, starting transfers between devices, per_device(): lax.all_to_all(jnp.broadcast_to(gains, (lines, wide)), ('dp', 'y', 'z'),...  24.2 us
    ppermute x6, starting transfers between devices, swap(): return lax.ppermute(array, axis, [(0, 1), (1, 0)])  24.2 us
    ppermute x6, waiting for transfers between devices, swap(): return lax.ppermute(array, axis, [(0, 1), (1, 0)])  14.3 us
    ppermute x5, starting transfers between devices, hop(): lax.ppermute(array, SEQ, [(i, j) for i, j in pairs if 0 <= j < shards])  12.6 us
    all_to_all x1, waiting for transfers between devices, per_device(): lax.all_to_all(jnp.broadcast_to(gains, (lines, wide)), ('dp', 'y', 'z'),...  11 us
    pallas_call x1, Pallas kernels, attention(): pl.pallas_call(attention_kernel, out_shape=(shape((ROWS, 2 * HEAD), bf16)...  9.5 us
    unnamed x17, local copies, waits for them, and re-layouts  3.18 us
    pallas_call x3, Pallas kernels, small(): pl.pallas_call(kernel, out_shape=tuple((jax.ShapeDtypeStruct(*out) for ou...  2.37 us
  transfers between devices with their start and end apart: 12, of which 4 were waited for; matrix products, arithmetic and copies ran while one was open for 2% of the time, Pallas kernels for 1%

profile of v5, /device:TPU:1, one launch (start us, length us, event | category | flops | bytes accessed | tf_op | source)
XLA Modules:
  0.0 104.7 jit_solution(1872052546353797897)
XLA Ops:
  0.6 0.0 copy-start.5
  0.7 0.7 copy-done.5
  1.3 1.1 %broadcast_select_fusion.5 = (bf16[256,256]{1,0:T(8,128)(2,1)S(1)}, bf16[256,256]{1,0:T(8,128)(2,1)S(1)}, bf16[256,256]{1,0:T(8,128)(2,1)S(1)}, bf16[256,256]{1,0:T(8,128)(2,1)S(1)}) fusion(pred[]{:T(512)S(6)} %not.4, bf16[256,512]{1,0:T(8,128)(2,1)} %bitcast.20, pred[]{:T(512)S(6)} %eq.6, bf16[256,512]{1,0:T(8,128)(2,1)} %bitcast.21), kind=kLoop, calls=%fused_computation.12 | loop fusion | flops 262144 | bytes 1048578 | tf_op jit(solution)/shard_map/jit(_where)/select_n | solution.py:259
  2.5 0.0 copy-start.3
  2.5 0.0 copy-start.4
  2.5 5.0 %collective-permute-start.2 = (bf16[272,512]{1,0:T(8,128)(2,1)S(1)}, bf16[272,512]{1,0:T(8,128)(2,1)S(1)}, u32[]{:S(2)}, u32[]{:S(2)}) collective-permute-start(bf16[272,512]{1,0:T(8,128)(2,1)S(1)} %get-tuple-element.29.kv_own), channel_id=1, source_target_pairs={{0,4},{1,5},{2,6},{3,7},{4,8},{5,9},{6,10},{7,11},{8,12},{9,13},{1... | collective-permute-start | bytes 835592 | tf_op jit(solution)/shard_map/ppermute | solution.py:247
  7.5 0.0 copy-done.3
  7.5 0.0 copy-done.4
  7.5 0.1 broadcast_select_fusion.1
  7.6 0.1 pad_maximum_fusion.1
  7.7 0.0 copy-start.6
  7.7 0.0 copy-start.7
  7.7 5.3 %collective-permute-start.1 = (bf16[256,1024]{1,0:T(8,128)(2,1)S(1)}, bf16[256,1024]{1,0:T(8,128)(2,1)S(1)}, u32[]{:S(2)}, u32[]{:S(2)}) collective-permute-start(bf16[256,1024]{1,0:T(8,128)(2,1)S(1)} %pad_maximum_fusion.1), channel_id=1, source_target_pairs={{0,1},{1,0},{2,3},{3,2},{4,5},{5,4},{6,7},{7,6},{8,9},{9,8},{10,11... | collective-permute-start | bytes 1572872 | tf_op jit(solution)/shard_map/ppermute | solution.py:250
  13.0 1.5 %collective-permute-start.5 = (bf16[272,512]{1,0:T(8,128)(2,1)S(1)}, bf16[272,512]{1,0:T(8,128)(2,1)S(1)}, u32[]{:S(2)}, u32[]{:S(2)}) collective-permute-start(bf16[272,512]{1,0:T(8,128)(2,1)S(1)} %get-tuple-element.27), channel_id=1, source_target_pairs={{0,5},{1,4},{2,7},{3,6},{4,9},{5,8},{6,11},{7,10},{8,13},{9,12},{1... | collective-permute-start | bytes 835592 | tf_op jit(solution)/shard_map/ppermute | solution.py:247
  14.5 3.5 %collective-permute-start.4 = (bf16[272,512]{1,0:T(8,128)(2,1)S(1)}, bf16[272,512]{1,0:T(8,128)(2,1)S(1)}, u32[]{:S(2)}, u32[]{:S(2)}) collective-permute-start(bf16[272,512]{1,0:T(8,128)(2,1)S(1)} %get-tuple-element.27), channel_id=1, source_target_pairs={{0,3},{1,2},{2,5},{3,4},{4,7},{5,6},{6,9},{7,8},{8,11},{9,10},{10,... | collective-permute-start | bytes 835592 | tf_op jit(solution)/shard_map/ppermute | solution.py:247
  18.0 1.9 %collective-permute-start = (bf16[272,512]{1,0:T(8,128)(2,1)S(1)}, bf16[272,512]{1,0:T(8,128)(2,1)S(1)}, u32[]{:S(2)}, u32[]{:S(2)}) collective-permute-start(bf16[272,512]{1,0:T(8,128)(2,1)S(1)} %get-tuple-element.27), channel_id=1, source_target_pairs={{0,1},{1,0},{2,3},{3,2},{4,5},{5,4},{6,7},{7,6},{8,9},{9,8},{10,11... | collective-permute-start | bytes 835592 | tf_op jit(solution)/shard_map/ppermute | solution.py:250
  19.9 0.0 collective-permute-done.2.kv_two
  20.0 3.9 %collective-permute-start.3 = (bf16[272,512]{1,0:T(8,128)(2,1)S(1)}, bf16[272,512]{1,0:T(8,128)(2,1)S(1)}, u32[]{:S(2)}, u32[]{:S(2)}) collective-permute-start(bf16[272,512]{1,0:T(8,128)(2,1)S(1)} %broadcast_select_fusion), channel_id=1, source_target_pairs={{0,2},{2,0},{1,3},{3,1},{4,6},{6,4},{5,7},{7,5},{8,10},{10,8},{9,1... | collective-permute-start | bytes 835592 | tf_op jit(solution)/shard_map/ppermute | solution.py:250
  23.9 0.0 copy-done.6
  24.0 0.0 copy-done.7
  24.0 0.1 pad_maximum_fusion.qg_own
  24.0 0.0 collective-permute-done.kv_peer
  24.1 0.0 collective-permute-done.5.kv_two_x
  24.1 0.2 collective-permute-done.4.kv_one_x
  24.2 0.0 collective-permute-done.1.qg_peer
  24.3 6.3 %collective-permute-done.3.kv_one = bf16[272,512]{1,0:T(8,128)(2,1)S(1)} collective-permute-done((bf16[272,512]{1,0:T(8,128)(2,1)S(1)}, bf16[272,512]{1,0:T(8,128)(2,1)S(1)}, u32[]{:S(2)}, u32[]{:S(2)}) %collective-permute-start.3) | collective-permute-done | bytes 278560 | tf_op jit(solution)/shard_map/ppermute | solution.py:250
  30.5 9.5 %attention.1 = (bf16[256,512]{1,0:T(8,128)(2,1)S(1)}, bf16[256,512]{1,0:T(8,128)(2,1)S(1)}, bf16[256,1024]{1,0:T(8,128)(2,1)S(1)}, f32[2,256,512]{2,1,0:T(8,128)...) custom-call(f32[1,512]{1,0:T(1,128)S(1)} %bitcast.16, ...), custom_call_target="tpu_custom_call" | custom-call | flops 8589934592 | bytes 8388608 | tf_op jit(solution)/shard_map/attention/pallas_call | solution.py:193
  40.0 0.7 copy-done
  40.7 0.8 copy-done.2
  41.5 1.3 %collective-permute-start.7 = (bf16[2,256,512]{2,1,0:T(8,128)(2,1)}, bf16[2,256,512]{2,1,0:T(8,128)(2,1)S(1)}, u32[]{:S(2)}, u32[]{:S(2)}) collective-permute-start(bf16[2,256,512]{2,1,0:T(8,128)(2,1)} %get-tuple-element.38), channel_id=1, source_target_pairs={{2,0},{3,1},{4,2},{5,3},{6,4},{7,5},{8,6},{9,7},{10,8},{11,9},{12,... | collective-permute-start | bytes 1572872 | tf_op jit(solution)/shard_map/ppermute | solution.py:247
  42.8 1.3 %collective-permute-start.8 = (bf16[2,256,512]{2,1,0:T(8,128)(2,1)}, bf16[2,256,512]{2,1,0:T(8,128)(2,1)S(1)}, u32[]{:S(2)}, u32[]{:S(2)}) collective-permute-start(bf16[2,256,512]{2,1,0:T(8,128)(2,1)} %get-tuple-element.39), channel_id=1, source_target_pairs={{4,0},{5,1},{6,2},{7,3},{8,4},{9,5},{10,6},{11,7},{12,8},{13,9},{1... | collective-permute-start | bytes 1572872 | tf_op jit(solution)/shard_map/ppermute | solution.py:247
  44.1 4.0 %collective-permute-start.9 = (f32[1,512]{1,0:T(1,128)S(1)}, f32[1,512]{1,0:T(1,128)S(1)}, u32[]{:S(2)}, u32[]{:S(2)}) collective-permute-start(f32[1,512]{1,0:T(1,128)S(1)} %get-tuple-element.40), channel_id=1, source_target_pairs={{0,2},{2,0},{1,3},{3,1},{4,6},{6,4},{5,7},{7,5},{8,10},{10,8},{9,1... | collective-permute-start | bytes 6152 | tf_op jit(solution)/shard_map/ppermute | solution.py:250
  48.1 8.0 %collective-permute-done.9 = f32[1,512]{1,0:T(1,128)S(1)} collective-permute-done((f32[1,512]{1,0:T(1,128)S(1)}, f32[1,512]{1,0:T(1,128)S(1)}, u32[]{:S(2)}, u32[]{:S(2)}) %collective-permute-start.9) | collective-permute-done | bytes 2080 | tf_op jit(solution)/shard_map/ppermute | solution.py:250
  56.1 0.8 broadcast_in_dim.24
  56.9 24.2 %all-to-all-start = ((f32[128,1,512]{2,1,0:T(1,128)}), f32[128,1,512]{2,1,0:T(1,128)}, u32[]{:S(2)}, u32[]{:S(2)}) async-start(f32[128,1,512]{2,1,0:T(1,128)} %broadcast_in_dim.24), calls=%async_computation | async-start | bytes 524288 | tf_op jit(solution)/shard_map/all_to_all | solution.py:289
  81.2 3.5 %collective-permute-start.6 = (bf16[256,1024]{1,0:T(8,128)(2,1)}, bf16[256,1024]{1,0:T(8,128)(2,1)S(1)}, u32[]{:S(2)}, u32[]{:S(2)}) collective-permute-start(bf16[256,1024]{1,0:T(8,128)(2,1)} %copy-done.2), channel_id=1, source_target_pairs={{0,1},{1,0},{2,3},{3,2},{4,5},{5,4},{6,7},{7,6},{8,9},{9,8},{10,11... | collective-permute-start | bytes 1572872 | tf_op jit(solution)/shard_map/ppermute | solution.py:250
  84.7 11.0 %all-to-all-done = f32[128,1,512]{2,1,0:T(1,128)} async-done(((f32[128,1,512]{2,1,0:T(1,128)}), f32[128,1,512]{2,1,0:T(1,128)}, u32[]{:S(2)}, u32[]{:S(2)}) %all-to-all-start) | async-done | bytes 262176 | tf_op jit(solution)/shard_map/all_to_all | solution.py:289
  95.7 1.0 copy.15
  96.7 0.0 collective-permute-done.7.grad_one
  96.7 0.0 collective-permute-done.8.grad_two
  96.7 0.0 copy-start.1
  96.7 0.4 finish.1
  97.1 5.6 %collective-permute-start.10 = (bf16[272,512]{1,0:T(8,128)(2,1)S(1)}, bf16[272,512]{1,0:T(8,128)(2,1)S(1)}, u32[]{:S(2)}, u32[]{:S(2)}) collective-permute-start(bf16[272,512]{1,0:T(8,128)(2,1)S(1)} %get-tuple-element.42), channel_id=1, source_target_pairs={{0,1},{1,0},{2,3},{3,2},{4,5},{5,4},{6,7},{7,6},{8,9},{9,8},{10,11... | collective-permute-start | bytes 835592 | tf_op jit(solution)/shard_map/ppermute | solution.py:250
  102.7 0.0 collective-permute-done.6.from_peer
  102.7 0.0 copy-done.1
  102.7 1.1 %join_queries.1 = (bf16[256,1024]{1,0:T(8,128)(2,1)}, bf16[256,1024]{1,0:T(8,128)(2,1)}) custom-call(bf16[256,512]{1,0:T(8,128)(2,1)S(1)} %get-tuple-element.32.att_mine, bf16[256,512]{1,0:T(8,128)(2,1)S(1)} %copy-done.1, bf16[256,1024]{1,0:T(8,128)(2,1)S(1)} %collective-permute-done.6.from_peer), custom_call_target="tpu_custom_call" | custom-call | tf_op jit(solution)/shard_map/join_queries/pallas_call | solution.py:227
  103.8 0.0 collective-permute-done.10.other
  103.8 0.9 join_keys.1
  (7 shorter events, 0.1 us)
Async XLA Ops:
  0.6 0.7 copy-start.5
  2.5 5.1 %copy-start.3 = (bf16[1,256,1024]{2,1,0:T(8,128)(2,1)S(1)}, bf16[1,256,1024]{2,1,0:T(8,128)(2,1)}, u32[]{:S(2)}) copy-start(bf16[1,256,1024]{2,1,0:T(8,128)(2,1)} %param.10) | copy-start | bytes 1572868
  2.5 5.1 %copy-start.4 = (bf16[1,256,1024]{2,1,0:T(8,128)(2,1)S(1)}, bf16[1,256,1024]{2,1,0:T(8,128)(2,1)}, u32[]{:S(2)}) copy-start(bf16[1,256,1024]{2,1,0:T(8,128)(2,1)} %param.7) | copy-start | bytes 1572868
  2.5 17.4 %collective-permute-start.2 = (bf16[272,512]{1,0:T(8,128)(2,1)S(1)}, bf16[272,512]{1,0:T(8,128)(2,1)S(1)}, u32[]{:S(2)}, u32[]{:S(2)}) collective-permute-start(bf16[272,512]{1,0:T(8,128)(2,1)S(1)} %get-tuple-element.29.kv_own), channel_id=1, source_target_pairs={{0,4},{1,5},{2,6},{3,7},{4,8},{5,9},{6,10},{7,11},{8,12},{9,13},{1... | collective-permute-start | bytes 835592 | tf_op jit(solution)/shard_map/ppermute | solution.py:247
  7.7 16.3 %copy-start.6 = (f32[256]{0:T(256)S(1)}, f32[256]{0:T(256)}, u32[]{:S(2)}) copy-start(f32[256]{0:T(256)} %param.12) | copy-start | bytes 3076
  7.7 16.3 %copy-start.7 = (f32[256]{0:T(256)S(1)}, f32[256]{0:T(256)}, u32[]{:S(2)}) copy-start(f32[256]{0:T(256)} %param.11) | copy-start | bytes 3076
  7.7 16.5 %collective-permute-start.1 = (bf16[256,1024]{1,0:T(8,128)(2,1)S(1)}, bf16[256,1024]{1,0:T(8,128)(2,1)S(1)}, u32[]{:S(2)}, u32[]{:S(2)}) collective-permute-start(bf16[256,1024]{1,0:T(8,128)(2,1)S(1)} %pad_maximum_fusion.1), channel_id=1, source_target_pairs={{0,1},{1,0},{2,3},{3,2},{4,5},{5,4},{6,7},{7,6},{8,9},{9,8},{10,11... | collective-permute-start | bytes 1572872 | tf_op jit(solution)/shard_map/ppermute | solution.py:250
  13.0 11.1 %collective-permute-start.5 = (bf16[272,512]{1,0:T(8,128)(2,1)S(1)}, bf16[272,512]{1,0:T(8,128)(2,1)S(1)}, u32[]{:S(2)}, u32[]{:S(2)}) collective-permute-start(bf16[272,512]{1,0:T(8,128)(2,1)S(1)} %get-tuple-element.27), channel_id=1, source_target_pairs={{0,5},{1,4},{2,7},{3,6},{4,9},{5,8},{6,11},{7,10},{8,13},{9,12},{1... | collective-permute-start | bytes 835592 | tf_op jit(solution)/shard_map/ppermute | solution.py:247
  14.5 9.8 %collective-permute-start.4 = (bf16[272,512]{1,0:T(8,128)(2,1)S(1)}, bf16[272,512]{1,0:T(8,128)(2,1)S(1)}, u32[]{:S(2)}, u32[]{:S(2)}) collective-permute-start(bf16[272,512]{1,0:T(8,128)(2,1)S(1)} %get-tuple-element.27), channel_id=1, source_target_pairs={{0,3},{1,2},{2,5},{3,4},{4,7},{5,6},{6,9},{7,8},{8,11},{9,10},{10,... | collective-permute-start | bytes 835592 | tf_op jit(solution)/shard_map/ppermute | solution.py:247
  18.0 6.0 %collective-permute-start = (bf16[272,512]{1,0:T(8,128)(2,1)S(1)}, bf16[272,512]{1,0:T(8,128)(2,1)S(1)}, u32[]{:S(2)}, u32[]{:S(2)}) collective-permute-start(bf16[272,512]{1,0:T(8,128)(2,1)S(1)} %get-tuple-element.27), channel_id=1, source_target_pairs={{0,1},{1,0},{2,3},{3,2},{4,5},{5,4},{6,7},{7,6},{8,9},{9,8},{10,11... | collective-permute-start | bytes 835592 | tf_op jit(solution)/shard_map/ppermute | solution.py:250
  20.0 10.5 %collective-permute-start.3 = (bf16[272,512]{1,0:T(8,128)(2,1)S(1)}, bf16[272,512]{1,0:T(8,128)(2,1)S(1)}, u32[]{:S(2)}, u32[]{:S(2)}) collective-permute-start(bf16[272,512]{1,0:T(8,128)(2,1)S(1)} %broadcast_select_fusion), channel_id=1, source_target_pairs={{0,2},{2,0},{1,3},{3,1},{4,6},{6,4},{5,7},{7,5},{8,10},{10,8},{9,1... | collective-permute-start | bytes 835592 | tf_op jit(solution)/shard_map/ppermute | solution.py:250
  40.0 0.7 copy-start
  40.7 0.8 copy-start.2
  41.5 55.1 %collective-permute-start.7 = (bf16[2,256,512]{2,1,0:T(8,128)(2,1)}, bf16[2,256,512]{2,1,0:T(8,128)(2,1)S(1)}, u32[]{:S(2)}, u32[]{:S(2)}) collective-permute-start(bf16[2,256,512]{2,1,0:T(8,128)(2,1)} %get-tuple-element.38), channel_id=1, source_target_pairs={{2,0},{3,1},{4,2},{5,3},{6,4},{7,5},{8,6},{9,7},{10,8},{11,9},{12,... | collective-permute-start | bytes 1572872 | tf_op jit(solution)/shard_map/ppermute | solution.py:247
  42.8 53.9 %collective-permute-start.8 = (bf16[2,256,512]{2,1,0:T(8,128)(2,1)}, bf16[2,256,512]{2,1,0:T(8,128)(2,1)S(1)}, u32[]{:S(2)}, u32[]{:S(2)}) collective-permute-start(bf16[2,256,512]{2,1,0:T(8,128)(2,1)} %get-tuple-element.39), channel_id=1, source_target_pairs={{4,0},{5,1},{6,2},{7,3},{8,4},{9,5},{10,6},{11,7},{12,8},{13,9},{1... | collective-permute-start | bytes 1572872 | tf_op jit(solution)/shard_map/ppermute | solution.py:247
  44.1 12.0 %collective-permute-start.9 = (f32[1,512]{1,0:T(1,128)S(1)}, f32[1,512]{1,0:T(1,128)S(1)}, u32[]{:S(2)}, u32[]{:S(2)}) collective-permute-start(f32[1,512]{1,0:T(1,128)S(1)} %get-tuple-element.40), channel_id=1, source_target_pairs={{0,2},{2,0},{1,3},{3,1},{4,6},{6,4},{5,7},{7,5},{8,10},{10,8},{9,1... | collective-permute-start | bytes 6152 | tf_op jit(solution)/shard_map/ppermute | solution.py:250
  56.9 38.8 %all-to-all-start = ((f32[128,1,512]{2,1,0:T(1,128)}), f32[128,1,512]{2,1,0:T(1,128)}, u32[]{:S(2)}, u32[]{:S(2)}) async-start(f32[128,1,512]{2,1,0:T(1,128)} %broadcast_in_dim.24), calls=%async_computation | async-start | bytes 524288 | tf_op jit(solution)/shard_map/all_to_all | solution.py:289
  81.2 21.5 %collective-permute-start.6 = (bf16[256,1024]{1,0:T(8,128)(2,1)}, bf16[256,1024]{1,0:T(8,128)(2,1)S(1)}, u32[]{:S(2)}, u32[]{:S(2)}) collective-permute-start(bf16[256,1024]{1,0:T(8,128)(2,1)} %copy-done.2), channel_id=1, source_target_pairs={{0,1},{1,0},{2,3},{3,2},{4,5},{5,4},{6,7},{7,6},{8,9},{9,8},{10,11... | collective-permute-start | bytes 1572872 | tf_op jit(solution)/shard_map/ppermute | solution.py:250
  96.7 6.0 %copy-start.1 = (bf16[256,512]{1,0:T(8,128)(2,1)S(1)}, bf16[256,512]{1,0:T(8,128)(2,1)}, u32[]{:S(2)}) copy-start(bf16[256,512]{1,0:T(8,128)(2,1)} %copy-done) | copy-start | bytes 786436
  97.1 6.7 %collective-permute-start.10 = (bf16[272,512]{1,0:T(8,128)(2,1)S(1)}, bf16[272,512]{1,0:T(8,128)(2,1)S(1)}, u32[]{:S(2)}, u32[]{:S(2)}) collective-permute-start(bf16[272,512]{1,0:T(8,128)(2,1)S(1)} %get-tuple-element.42), channel_id=1, source_target_pairs={{0,1},{1,0},{2,3},{3,2},{4,5},{5,4},{6,7},{7,6},{8,9},{9,8},{10,11... | collective-permute-start | bytes 835592 | tf_op jit(solution)/shard_map/ppermute | solution.py:250

commit v6 on v5

--- a/solution.py
+++ b/solution.py
@@ -48,7 +48,7 @@
 
 
 def attention_kernel(
-    gain, qg_own, qg_peer, kv_own, kv_peer, kv_one, kv_one_x, kv_two, kv_two_x,
+    gain, q_own, g_own, q_peer, g_peer, kv_own, kv_peer, kv_one, kv_one_x, kv_two, kv_two_x,
     attended, q_grad, swap, kv_grad_own, kv_grad_one, kv_grad_two, gains,
     key, key_t, value, value_t, tag, key_grad, value_grad, score, query, upstream, upstream_t,
 ):
@@ -73,15 +73,15 @@
     query_at = lax.broadcasted_iota(jnp.int32, (ROWS, 2 * ROWS), 1) % ROWS
     q_gain_grad = jnp.zeros((1, HEAD), f32)
 
-    for qg, tags, first, att_out, grad_out in (
-        (qg_own, kv_own, core, attended, q_grad),
-        (qg_peer, kv_peer, 1 - core, swap.at[:, : 2 * HEAD], swap.at[:, 2 * HEAD :]),
+    for raw, up_raw, tags, first, att_out, grad_out in (
+        (q_own, g_own, kv_own, core, attended, q_grad),
+        (q_peer, g_peer, kv_peer, 1 - core, swap.at[:, : 2 * HEAD], swap.at[:, 2 * HEAD :]),
     ):
         for h in range(2):
-            unit, _ = norm_rows(qg[:, h * HEAD : (h + 1) * HEAD])
+            unit, _ = norm_rows(raw[:, h * HEAD : (h + 1) * HEAD])
             normed = (unit * gain[:, :HEAD]).astype(bf16)
             query[h * ROWS : (h + 1) * ROWS] = normed * jnp.asarray(SCALE, bf16)
-            up = qg[:, (2 + h) * HEAD : (3 + h) * HEAD]
+            up = up_raw[:, h * HEAD : (h + 1) * HEAD]
             upstream[h * ROWS : (h + 1) * ROWS] = up
             upstream_t[:, h * ROWS : (h + 1) * ROWS] = up.T
         ids = tags[ROWS : ROWS + EXTRA, :ROWS].astype(f32)[:1]
@@ -123,7 +123,7 @@
         for h in range(2):
             att_out[:, h * HEAD : (h + 1) * HEAD] = att_t[:, h * ROWS : (h + 1) * ROWS].T.astype(bf16)
             normed_grad = grad_t[:, h * ROWS : (h + 1) * ROWS].T * SCALE
-            unit, inverse = norm_rows(qg[:, h * HEAD : (h + 1) * HEAD])
+            unit, inverse = norm_rows(raw[:, h * HEAD : (h + 1) * HEAD])
             q_gain_grad = q_gain_grad + jnp.sum(normed_grad * unit, axis=0, keepdims=True)
             grad_out[:, h * HEAD : (h + 1) * HEAD] = norm_backward(
                 normed_grad, unit, inverse, gain[:, :HEAD]
@@ -141,15 +141,19 @@
             out[i, :, HEAD:] = value_grad[at + i].astype(out.dtype)
 
 
-def finish_kernel(
-    gain, kv_own, kv_peer, grad_own, grad_one, grad_two, gathered, own, peer, gains
-):
-    core = lax.axis_index("core")
+def onward_kernel(two, side, onward):
+    x = lax.axis_index("x")
+    onward[...] = (two[...].astype(f32) + jnp.where(x == 1, side[...].astype(f32), 0.0)).astype(bf16)
+
+
+def finish_kernel(gain, kv_own, kv_peer, grad_own, side, ahead, gathered, own, peer, gains):
+    core, x = lax.axis_index("core"), lax.axis_index("x")
     sums = jnp.sum(gathered[...], axis=0, keepdims=True)
     gains[...] = sums
     peer[ROWS:] = in_pieces(sums)
     for part, block, out in ((kv_own, core, own), (kv_peer, 1 - core, peer)):
-        total = grad_own[block] + grad_one[block].astype(f32) + grad_two[block].astype(f32)
+        total = grad_own[block] + ahead[block].astype(f32)
+        total = total + jnp.where(x == 0, side[block].astype(f32), 0.0)
         unit, inverse = norm_rows(part[:ROWS, :HEAD])
         out[:ROWS, :HEAD] = norm_backward(total[:, :HEAD], unit, inverse, gain[:, HEAD:]).astype(bf16)
         out[:ROWS, HEAD:] = total[:, HEAD:].astype(bf16)
@@ -272,30 +276,32 @@
     kv_peer = swap(kv_other)
     gain, kv_peer = lax.optimization_barrier((gain, kv_peer))
 
-    def pack_queries(mine):
-        return jnp.concatenate(
-            [jnp.where(mine, a[:, :wide], a[:, wide:]) for a in (queries, upstream)], axis=1
-        )
-
-    qg_mine, qg_other = pack_queries(first), pack_queries(~first)
-    qg_peer = swap(qg_other)
+    def halves(array):
+        return jnp.where(first, array[:, :wide], array[:, wide:]), jnp.where(first, array[:, wide:], array[:, :wide])
+
+    (q_mine, q_other), (g_mine, g_other) = halves(queries), halves(upstream)
+    q_peer, g_peer = swap(q_other), swap(g_other)
     attended, q_grad, to_peer, grad_own, grad_one, grad_two, gains = attention(
-        gain, qg_mine, qg_peer, kv_mine, kv_peer, kv_one, kv_one_x, kv_two, kv_two_x
+        gain, q_mine, g_mine, q_peer, g_peer, kv_mine, kv_peer, kv_one, kv_one_x, kv_two, kv_two_x
     )
     gains = gains + swap(gains, "x")
-    grad_two, grad_one = hop(grad_two, -2), hop(grad_one, -1)
+    gains, grad_one = lax.optimization_barrier((gains, grad_one))
+    side = swap(grad_one, "x")
     from_peer = swap(to_peer)
+    attended, q_grad = small(
+        join_queries_kernel, [((ROWS, 4 * HEAD), bf16)] * 2, "join_queries", attended, q_grad, from_peer
+    )
+    gains, attended, q_grad = lax.optimization_barrier((gains, attended, q_grad))
     lines = lax.axis_size("dp") * lax.axis_size("y") * lax.axis_size("z")
     gathered = lax.all_to_all(
         jnp.broadcast_to(gains, (lines, wide)), ("dp", "y", "z"), 0, 0, tiled=True
     )
-    attended, q_grad = small(
-        join_queries_kernel, [((ROWS, 4 * HEAD), bf16)] * 2, "join_queries", attended, q_grad, from_peer
-    )
+    (onward,) = small(onward_kernel, [((2, ROWS, wide), bf16)], "onward", grad_two, side)
+    ahead = hop(onward, -2)
     kv_grad, kv_grad_peer, gains = small(
         finish_kernel,
         [((ROWS, wide), bf16), ((ROWS + EXTRA, wide), bf16), ((1, wide), f32)],
-        "finish", gain, kv_mine, kv_peer, grad_own, grad_one, grad_two, gathered,
+        "finish", gain, kv_mine, kv_peer, grad_own, side, ahead, gathered,
     )
     kv_grad_x = swap(kv_grad_peer)
     key_grad, value_grad, q_gain_grad, k_gain_grad = small(

time: 105 us -> 108 us (1.029)
  blocking collectives: 0 us -> 38.7 us
  starting transfers between devices: 61 us -> 42.3 us
  waiting for transfers between devices: 25.5 us -> 11.6 us
  local copies, waits for them, and re-layouts: 4.02 us -> 0.85 us
    all_to_all x0 -> x1, blocking collectives: none -> 38.7 us  [per_device(): lax.all_to_all(jnp.broadcast_to(gains, (lines, wide)), ('dp', 'y', 'z'),...]
    all_to_all x1 -> x0, starting transfers between devices: 24.2 us -> none  [per_device(): lax.all_to_all(jnp.broadcast_to(gains, (lines, wide)), ('dp', 'y', 'z'),...]
    all_to_all x1 -> x0, waiting for transfers between devices: 11 us -> none  [per_device(): lax.all_to_all(jnp.broadcast_to(gains, (lines, wide)), ('dp', 'y', 'z'),...]
    ppermute x6 -> x8, starting transfers between devices: 24.2 us -> 28.6 us  [swap(): return lax.ppermute(array, axis, [(0, 1), (1, 0)])]
    ppermute x6 -> x8, waiting for transfers between devices: 14.3 us -> 11.6 us  [swap(): return lax.ppermute(array, axis, [(0, 1), (1, 0)])]
    unnamed x17 -> x11, local copies, waits for them, and re-layouts: 3.18 us -> 0.71 us
    ppermute x5 -> x4, starting transfers between devices: 12.6 us -> 13.7 us  [hop(): lax.ppermute(array, SEQ, [(i, j) for i, j in pairs if 0 <= j < shards])]
    pallas_call x3 -> x4, Pallas kernels: 2.37 us -> 2.6 us  [small(): pl.pallas_call(kernel, out_shape=tuple((jax.ShapeDtypeStruct(*out) for ou...]
  transfers between devices with their start and end apart: 12 -> 12, of which waited for: 4 -> 5; matrix products, arithmetic and copies ran while one was open for 2% -> 0% of each run, Pallas kernels for 1% -> 1%
where the time goes in v6:
time: 108 us; the launch traced here: 107 us
  starting transfers between devices  42.3 us (39%)
  blocking collectives  38.7 us (36%)
  waiting for transfers between devices  11.6 us (11%)
  Pallas kernels  11.5 us (11%)
  other arithmetic  1.31 us (1%)
    all_to_all x1, blocking collectives, per_device(): lax.all_to_all(jnp.broadcast_to(gains, (lines, wide)), ('dp', 'y', 'z'),...  38.7 us
    ppermute x8, starting transfers between devices, swap(): return lax.ppermute(array, axis, [(0, 1), (1, 0)])  28.6 us
    ppermute x4, starting transfers between devices, hop(): lax.ppermute(array, SEQ, [(i, j) for i, j in pairs if 0 <= j < shards])  13.7 us
    ppermute x8, waiting for transfers between devices, swap(): return lax.ppermute(array, axis, [(0, 1), (1, 0)])  11.6 us
    pallas_call x1, Pallas kernels, attention(): pl.pallas_call(attention_kernel, out_shape=(shape((ROWS, 2 * HEAD), bf16)...  8.88 us
    pallas_call x4, Pallas kernels, small(): pl.pallas_call(kernel, out_shape=tuple((jax.ShapeDtypeStruct(*out) for ou...  2.6 us
  transfers between devices with their start and end apart: 12, of which 5 were waited for; matrix products, arithmetic and copies ran while one was open for 0% of the time, Pallas kernels for 1%

profile of v6, /device:TPU:1, one launch (start us, length us, event | category | flops | bytes accessed | tf_op | source)
XLA Modules:
  0.0 107.2 jit_solution(10969702915045145736)
XLA Ops:
  0.6 0.0 copy-start.2
  0.7 0.7 copy-done.2
  1.3 1.1 %broadcast_select_fusion.5 = (bf16[256,256]{1,0:T(8,128)(2,1)S(1)}, bf16[256,256]{1,0:T(8,128)(2,1)S(1)}, bf16[256,256]{1,0:T(8,128)(2,1)S(1)}, bf16[256,256]{1,0:T(8,128)(2,1)S(1)}) fusion(pred[]{:T(512)S(6)} %not.3, bf16[256,512]{1,0:T(8,128)(2,1)} %bitcast.20, pred[]{:T(512)S(6)} %eq.6, bf16[256,512]{1,0:T(8,128)(2,1)} %bitcast.21), kind=kLoop, calls=%fused_computation.10 | loop fusion | flops 262144 | bytes 1048578 | tf_op jit(solution)/shard_map/jit(_where)/select_n | solution.py:263
  2.5 0.0 copy-start
  2.5 5.0 %collective-permute-start.3 = (bf16[272,512]{1,0:T(8,128)(2,1)S(1)}, bf16[272,512]{1,0:T(8,128)(2,1)S(1)}, u32[]{:S(2)}, u32[]{:S(2)}) collective-permute-start(bf16[272,512]{1,0:T(8,128)(2,1)S(1)} %get-tuple-element.34.kv_own), channel_id=1, source_target_pairs={{0,4},{1,5},{2,6},{3,7},{4,8},{5,9},{6,10},{7,11},{8,12},{9,13},{1... | collective-permute-start | bytes 835592 | tf_op jit(solution)/shard_map/ppermute | solution.py:251
  7.5 4.8 %collective-permute-start.6 = (bf16[272,512]{1,0:T(8,128)(2,1)S(1)}, bf16[272,512]{1,0:T(8,128)(2,1)S(1)}, u32[]{:S(2)}, u32[]{:S(2)}) collective-permute-start(bf16[272,512]{1,0:T(8,128)(2,1)S(1)} %get-tuple-element.32), channel_id=1, source_target_pairs={{0,5},{1,4},{2,7},{3,6},{4,9},{5,8},{6,11},{7,10},{8,13},{9,12},{1... | collective-permute-start | bytes 835592 | tf_op jit(solution)/shard_map/ppermute | solution.py:251
  12.4 2.6 %collective-permute-start.5 = (bf16[272,512]{1,0:T(8,128)(2,1)S(1)}, bf16[272,512]{1,0:T(8,128)(2,1)S(1)}, u32[]{:S(2)}, u32[]{:S(2)}) collective-permute-start(bf16[272,512]{1,0:T(8,128)(2,1)S(1)} %get-tuple-element.32), channel_id=1, source_target_pairs={{0,3},{1,2},{2,5},{3,4},{4,7},{5,6},{6,9},{7,8},{8,11},{9,10},{10,... | collective-permute-start | bytes 835592 | tf_op jit(solution)/shard_map/ppermute | solution.py:251
  14.9 2.9 %collective-permute-start = (bf16[272,512]{1,0:T(8,128)(2,1)S(1)}, bf16[272,512]{1,0:T(8,128)(2,1)S(1)}, u32[]{:S(2)}, u32[]{:S(2)}) collective-permute-start(bf16[272,512]{1,0:T(8,128)(2,1)S(1)} %get-tuple-element.32), channel_id=1, source_target_pairs={{0,1},{1,0},{2,3},{3,2},{4,5},{5,4},{6,7},{7,6},{8,9},{9,8},{10,11... | collective-permute-start | bytes 835592 | tf_op jit(solution)/shard_map/ppermute | solution.py:254
  17.8 0.0 copy-done
  17.9 0.0 copy-start.1
  17.9 2.1 %collective-permute-start.1 = (bf16[256,512]{1,0:T(8,128)(2,1)S(1)}, bf16[256,512]{1,0:T(8,128)(2,1)S(1)}, u32[]{:S(2)}, u32[]{:S(2)}) collective-permute-start(bf16[256,512]{1,0:T(8,128)(2,1)S(1)} %get-tuple-element.60), channel_id=1, source_target_pairs={{0,1},{1,0},{2,3},{3,2},{4,5},{5,4},{6,7},{7,6},{8,9},{9,8},{10,11... | collective-permute-start | bytes 786440 | tf_op jit(solution)/shard_map/ppermute | solution.py:254
  19.9 0.0 collective-permute-done.3.kv_two
  20.0 3.9 %collective-permute-start.4 = (bf16[272,512]{1,0:T(8,128)(2,1)S(1)}, bf16[272,512]{1,0:T(8,128)(2,1)S(1)}, u32[]{:S(2)}, u32[]{:S(2)}) collective-permute-start(bf16[272,512]{1,0:T(8,128)(2,1)S(1)} %broadcast_select_fusion), channel_id=1, source_target_pairs={{0,2},{2,0},{1,3},{3,1},{4,6},{6,4},{5,7},{7,5},{8,10},{10,8},{9,1... | collective-permute-start | bytes 835592 | tf_op jit(solution)/shard_map/ppermute | solution.py:254
  23.9 0.0 copy-done.1
  24.0 0.0 copy-start.4
  24.0 0.0 copy-start.3
  24.0 0.0 collective-permute-done.kv_peer
  24.0 2.7 %collective-permute-start.2 = (bf16[256,512]{1,0:T(8,128)(2,1)S(1)}, bf16[256,512]{1,0:T(8,128)(2,1)S(1)}, u32[]{:S(2)}, u32[]{:S(2)}) collective-permute-start(bf16[256,512]{1,0:T(8,128)(2,1)S(1)} %get-tuple-element.58), channel_id=1, source_target_pairs={{0,1},{1,0},{2,3},{3,2},{4,5},{5,4},{6,7},{7,6},{8,9},{9,8},{10,11... | collective-permute-start | bytes 786440 | tf_op jit(solution)/shard_map/ppermute | solution.py:254
  26.7 0.0 copy-done.4
  26.7 0.0 copy-done.3
  26.8 0.0 collective-permute-done.1.q_peer
  26.8 1.1 %collective-permute-done.2.g_peer = bf16[256,512]{1,0:T(8,128)(2,1)S(1)} collective-permute-done((bf16[256,512]{1,0:T(8,128)(2,1)S(1)}, bf16[256,512]{1,0:T(8,128)(2,1)S(1)}, u32[]{:S(2)}, u32[]{:S(2)}) %collective-permute-start.2) | collective-permute-done | bytes 262176 | tf_op jit(solution)/shard_map/ppermute | solution.py:254
  27.9 0.0 collective-permute-done.6.kv_two_x
  27.9 0.0 collective-permute-done.5.kv_one_x
  27.9 2.6 %collective-permute-done.4.kv_one = bf16[272,512]{1,0:T(8,128)(2,1)S(1)} collective-permute-done((bf16[272,512]{1,0:T(8,128)(2,1)S(1)}, bf16[272,512]{1,0:T(8,128)(2,1)S(1)}, u32[]{:S(2)}, u32[]{:S(2)}) %collective-permute-start.4) | collective-permute-done | bytes 278560 | tf_op jit(solution)/shard_map/ppermute | solution.py:254
  30.5 8.9 %attention.1 = (bf16[256,512]{1,0:T(8,128)(2,1)S(1)}, bf16[256,512]{1,0:T(8,128)(2,1)S(1)}, bf16[256,1024]{1,0:T(8,128)(2,1)S(1)}, f32[2,256,512]{2,1,0:T(8,128)...) custom-call(f32[1,512]{1,0:T(1,128)S(1)} %bitcast.16, ...), custom_call_target="tpu_custom_call" | custom-call | flops 8589934592 | bytes 8388608 | tf_op jit(solution)/shard_map/attention/pallas_call | solution.py:197
  39.4 3.0 %collective-permute-start.7 = (f32[1,512]{1,0:T(1,128)S(1)}, f32[1,512]{1,0:T(1,128)S(1)}, u32[]{:S(2)}, u32[]{:S(2)}) collective-permute-start(f32[1,512]{1,0:T(1,128)S(1)} %get-tuple-element.37), channel_id=1, source_target_pairs={{0,2},{2,0},{1,3},{3,1},{4,6},{6,4},{5,7},{7,5},{8,10},{10,8},{9,1... | collective-permute-start | bytes 6152 | tf_op jit(solution)/shard_map/ppermute | solution.py:254
  42.4 1.3 %collective-permute-done.7 = f32[1,512]{1,0:T(1,128)S(1)} collective-permute-done((f32[1,512]{1,0:T(1,128)S(1)}, f32[1,512]{1,0:T(1,128)S(1)}, u32[]{:S(2)}, u32[]{:S(2)}) %collective-permute-start.7) | collective-permute-done | bytes 2080 | tf_op jit(solution)/shard_map/ppermute | solution.py:254
  43.7 3.0 %collective-permute-start.9 = (bf16[2,256,512]{2,1,0:T(8,128)(2,1)S(1)}, bf16[2,256,512]{2,1,0:T(8,128)(2,1)S(1)}, u32[]{:S(2)}, u32[]{:S(2)}) collective-permute-start(bf16[2,256,512]{2,1,0:T(8,128)(2,1)S(1)} %get-tuple-element.48), channel_id=1, source_target_pairs={{0,2},{2,0},{1,3},{3,1},{4,6},{6,4},{5,7},{7,5},{8,10},{10,8},{9,1... | collective-permute-start | bytes 1572872 | tf_op jit(solution)/shard_map/ppermute | solution.py:254
  46.8 4.7 %collective-permute-start.8 = (bf16[256,1024]{1,0:T(8,128)(2,1)S(1)}, bf16[256,1024]{1,0:T(8,128)(2,1)S(1)}, u32[]{:S(2)}, u32[]{:S(2)}) collective-permute-start(bf16[256,1024]{1,0:T(8,128)(2,1)S(1)} %get-tuple-element.42), channel_id=1, source_target_pairs={{0,1},{1,0},{2,3},{3,2},{4,5},{5,4},{6,7},{7,6},{8,9},{9,8},{10,11... | collective-permute-start | bytes 1572872 | tf_op jit(solution)/shard_map/ppermute | solution.py:254
  51.4 5.4 %collective-permute-done.9.side = bf16[2,256,512]{2,1,0:T(8,128)(2,1)S(1)} collective-permute-done((bf16[2,256,512]{2,1,0:T(8,128)(2,1)S(1)}, bf16[2,256,512]{2,1,0:T(8,128)(2,1)S(1)}, u32[]{:S(2)}, u32[]{:S(2)}) %collective-permute-start.9) | collective-permute-done | bytes 524320 | tf_op jit(solution)/shard_map/ppermute | solution.py:254
  56.9 0.2 onward.1
  57.1 1.3 %collective-permute-start.10 = (bf16[2,256,512]{2,1,0:T(8,128)(2,1)S(1)}, bf16[2,256,512]{2,1,0:T(8,128)(2,1)S(1)}, u32[]{:S(2)}, u32[]{:S(2)}) collective-permute-start(bf16[2,256,512]{2,1,0:T(8,128)(2,1)S(1)} %onward.1), channel_id=1, source_target_pairs={{4,0},{5,1},{6,2},{7,3},{8,4},{9,5},{10,6},{11,7},{12,8},{13,9},{1... | collective-permute-start | bytes 1572872 | tf_op jit(solution)/shard_map/ppermute | solution.py:251
  58.4 0.0 collective-permute-done.8.from_peer
  58.4 1.1 %join_queries.1 = (bf16[256,1024]{1,0:T(8,128)(2,1)}, bf16[256,1024]{1,0:T(8,128)(2,1)}) custom-call(bf16[256,512]{1,0:T(8,128)(2,1)S(1)} %get-tuple-element.40.att_mine, bf16[256,512]{1,0:T(8,128)(2,1)S(1)} %get-tuple-element.41.grad_mine, bf16[256,1024]{1,0:T(8,128)(2,1)S(1)} %collective-permute-done.8.from_peer), custom_call_target="tpu_custom_call" | custom-call | tf_op jit(solution)/shard_map/join_queries/pallas_call | solution.py:231
  59.5 0.1 broadcast_in_dim.24
  59.6 38.7 %all_to_all.8 = f32[128,1,512]{2,1,0:T(1,128)S(1)} all-to-all(f32[128,1,512]{2,1,0:T(1,128)S(1)} %broadcast_in_dim.24), channel_id=1, replica_groups=mesh['dp'=2,'y'=8,'z'=8,'x'=2,'core'=2] {'dp','y','z'}, dimensions={0} | all-to-all | bytes 524288 | tf_op jit(solution)/shard_map/all_to_all | solution.py:296
  98.3 0.0 collective-permute-done.10.ahead
  98.4 0.5 finish.1
  98.8 6.4 %collective-permute-start.11 = (bf16[272,512]{1,0:T(8,128)(2,1)S(1)}, bf16[272,512]{1,0:T(8,128)(2,1)S(1)}, u32[]{:S(2)}, u32[]{:S(2)}) collective-permute-start(bf16[272,512]{1,0:T(8,128)(2,1)S(1)} %get-tuple-element.52), channel_id=1, source_target_pairs={{0,1},{1,0},{2,3},{3,2},{4,5},{5,4},{6,7},{7,6},{8,9},{9,8},{10,11... | collective-permute-start | bytes 835592 | tf_op jit(solution)/shard_map/ppermute | solution.py:254
  105.2 1.2 %collective-permute-done.11.other = bf16[272,512]{1,0:T(8,128)(2,1)S(1)} collective-permute-done((bf16[272,512]{1,0:T(8,128)(2,1)S(1)}, bf16[272,512]{1,0:T(8,128)(2,1)S(1)}, u32[]{:S(2)}, u32[]{:S(2)}) %collective-permute-start.11) | collective-permute-done | bytes 278560 | tf_op jit(solution)/shard_map/ppermute | solution.py:254
  106.3 0.9 join_keys.1
  (8 shorter events, 0.2 us)
Async XLA Ops:
  0.6 0.7 copy-start.2
  2.5 15.3 %copy-start = (bf16[1,256,1024]{2,1,0:T(8,128)(2,1)S(1)}, bf16[1,256,1024]{2,1,0:T(8,128)(2,1)}, u32[]{:S(2)}) copy-start(bf16[1,256,1024]{2,1,0:T(8,128)(2,1)} %param.7) | copy-start | bytes 1572868
  2.5 17.4 %collective-permute-start.3 = (bf16[272,512]{1,0:T(8,128)(2,1)S(1)}, bf16[272,512]{1,0:T(8,128)(2,1)S(1)}, u32[]{:S(2)}, u32[]{:S(2)}) collective-permute-start(bf16[272,512]{1,0:T(8,128)(2,1)S(1)} %get-tuple-element.34.kv_own), channel_id=1, source_target_pairs={{0,4},{1,5},{2,6},{3,7},{4,8},{5,9},{6,10},{7,11},{8,12},{9,13},{1... | collective-permute-start | bytes 835592 | tf_op jit(solution)/shard_map/ppermute | solution.py:251
  7.5 20.4 %collective-permute-start.6 = (bf16[272,512]{1,0:T(8,128)(2,1)S(1)}, bf16[272,512]{1,0:T(8,128)(2,1)S(1)}, u32[]{:S(2)}, u32[]{:S(2)}) collective-permute-start(bf16[272,512]{1,0:T(8,128)(2,1)S(1)} %get-tuple-element.32), channel_id=1, source_target_pairs={{0,5},{1,4},{2,7},{3,6},{4,9},{5,8},{6,11},{7,10},{8,13},{9,12},{1... | collective-permute-start | bytes 835592 | tf_op jit(solution)/shard_map/ppermute | solution.py:251
  12.4 15.5 %collective-permute-start.5 = (bf16[272,512]{1,0:T(8,128)(2,1)S(1)}, bf16[272,512]{1,0:T(8,128)(2,1)S(1)}, u32[]{:S(2)}, u32[]{:S(2)}) collective-permute-start(bf16[272,512]{1,0:T(8,128)(2,1)S(1)} %get-tuple-element.32), channel_id=1, source_target_pairs={{0,3},{1,2},{2,5},{3,4},{4,7},{5,6},{6,9},{7,8},{8,11},{9,10},{10,... | collective-permute-start | bytes 835592 | tf_op jit(solution)/shard_map/ppermute | solution.py:251
  14.9 9.1 %collective-permute-start = (bf16[272,512]{1,0:T(8,128)(2,1)S(1)}, bf16[272,512]{1,0:T(8,128)(2,1)S(1)}, u32[]{:S(2)}, u32[]{:S(2)}) collective-permute-start(bf16[272,512]{1,0:T(8,128)(2,1)S(1)} %get-tuple-element.32), channel_id=1, source_target_pairs={{0,1},{1,0},{2,3},{3,2},{4,5},{5,4},{6,7},{7,6},{8,9},{9,8},{10,11... | collective-permute-start | bytes 835592 | tf_op jit(solution)/shard_map/ppermute | solution.py:254
  17.9 6.1 %copy-start.1 = (bf16[1,256,1024]{2,1,0:T(8,128)(2,1)S(1)}, bf16[1,256,1024]{2,1,0:T(8,128)(2,1)}, u32[]{:S(2)}) copy-start(bf16[1,256,1024]{2,1,0:T(8,128)(2,1)} %param.10) | copy-start | bytes 1572868
  17.9 8.9 %collective-permute-start.1 = (bf16[256,512]{1,0:T(8,128)(2,1)S(1)}, bf16[256,512]{1,0:T(8,128)(2,1)S(1)}, u32[]{:S(2)}, u32[]{:S(2)}) collective-permute-start(bf16[256,512]{1,0:T(8,128)(2,1)S(1)} %get-tuple-element.60), channel_id=1, source_target_pairs={{0,1},{1,0},{2,3},{3,2},{4,5},{5,4},{6,7},{7,6},{8,9},{9,8},{10,11... | collective-permute-start | bytes 786440 | tf_op jit(solution)/shard_map/ppermute | solution.py:254
  20.0 10.5 %collective-permute-start.4 = (bf16[272,512]{1,0:T(8,128)(2,1)S(1)}, bf16[272,512]{1,0:T(8,128)(2,1)S(1)}, u32[]{:S(2)}, u32[]{:S(2)}) collective-permute-start(bf16[272,512]{1,0:T(8,128)(2,1)S(1)} %broadcast_select_fusion), channel_id=1, source_target_pairs={{0,2},{2,0},{1,3},{3,1},{4,6},{6,4},{5,7},{7,5},{8,10},{10,8},{9,1... | collective-permute-start | bytes 835592 | tf_op jit(solution)/shard_map/ppermute | solution.py:254
  24.0 2.8 %copy-start.4 = (f32[256]{0:T(256)S(1)}, f32[256]{0:T(256)}, u32[]{:S(2)}) copy-start(f32[256]{0:T(256)} %param.11) | copy-start | bytes 3076
  24.0 2.7 %copy-start.3 = (f32[256]{0:T(256)S(1)}, f32[256]{0:T(256)}, u32[]{:S(2)}) copy-start(f32[256]{0:T(256)} %param.12) | copy-start | bytes 3076
  24.0 3.8 %collective-permute-start.2 = (bf16[256,512]{1,0:T(8,128)(2,1)S(1)}, bf16[256,512]{1,0:T(8,128)(2,1)S(1)}, u32[]{:S(2)}, u32[]{:S(2)}) collective-permute-start(bf16[256,512]{1,0:T(8,128)(2,1)S(1)} %get-tuple-element.58), channel_id=1, source_target_pairs={{0,1},{1,0},{2,3},{3,2},{4,5},{5,4},{6,7},{7,6},{8,9},{9,8},{10,11... | collective-permute-start | bytes 786440 | tf_op jit(solution)/shard_map/ppermute | solution.py:254
  39.4 4.3 %collective-permute-start.7 = (f32[1,512]{1,0:T(1,128)S(1)}, f32[1,512]{1,0:T(1,128)S(1)}, u32[]{:S(2)}, u32[]{:S(2)}) collective-permute-start(f32[1,512]{1,0:T(1,128)S(1)} %get-tuple-element.37), channel_id=1, source_target_pairs={{0,2},{2,0},{1,3},{3,1},{4,6},{6,4},{5,7},{7,5},{8,10},{10,8},{9,1... | collective-permute-start | bytes 6152 | tf_op jit(solution)/shard_map/ppermute | solution.py:254
  43.7 13.1 %collective-permute-start.9 = (bf16[2,256,512]{2,1,0:T(8,128)(2,1)S(1)}, bf16[2,256,512]{2,1,0:T(8,128)(2,1)S(1)}, u32[]{:S(2)}, u32[]{:S(2)}) collective-permute-start(bf16[2,256,512]{2,1,0:T(8,128)(2,1)S(1)} %get-tuple-element.48), channel_id=1, source_target_pairs={{0,2},{2,0},{1,3},{3,1},{4,6},{6,4},{5,7},{7,5},{8,10},{10,8},{9,1... | collective-permute-start | bytes 1572872 | tf_op jit(solution)/shard_map/ppermute | solution.py:254
  46.8 11.6 %collective-permute-start.8 = (bf16[256,1024]{1,0:T(8,128)(2,1)S(1)}, bf16[256,1024]{1,0:T(8,128)(2,1)S(1)}, u32[]{:S(2)}, u32[]{:S(2)}) collective-permute-start(bf16[256,1024]{1,0:T(8,128)(2,1)S(1)} %get-tuple-element.42), channel_id=1, source_target_pairs={{0,1},{1,0},{2,3},{3,2},{4,5},{5,4},{6,7},{7,6},{8,9},{9,8},{10,11... | collective-permute-start | bytes 1572872 | tf_op jit(solution)/shard_map/ppermute | solution.py:254
  57.1 41.3 %collective-permute-start.10 = (bf16[2,256,512]{2,1,0:T(8,128)(2,1)S(1)}, bf16[2,256,512]{2,1,0:T(8,128)(2,1)S(1)}, u32[]{:S(2)}, u32[]{:S(2)}) collective-permute-start(bf16[2,256,512]{2,1,0:T(8,128)(2,1)S(1)} %onward.1), channel_id=1, source_target_pairs={{4,0},{5,1},{6,2},{7,3},{8,4},{9,5},{10,6},{11,7},{12,8},{13,9},{1... | collective-permute-start | bytes 1572872 | tf_op jit(solution)/shard_map/ppermute | solution.py:251
  98.8 7.5 %collective-permute-start.11 = (bf16[272,512]{1,0:T(8,128)(2,1)S(1)}, bf16[272,512]{1,0:T(8,128)(2,1)S(1)}, u32[]{:S(2)}, u32[]{:S(2)}) collective-permute-start(bf16[272,512]{1,0:T(8,128)(2,1)S(1)} %get-tuple-element.52), channel_id=1, source_target_pairs={{0,1},{1,0},{2,3},{3,2},{4,5},{5,4},{6,7},{7,6},{8,9},{9,8},{10,11... | collective-permute-start | bytes 835592 | tf_op jit(solution)/shard_map/ppermute | solution.py:254

commit v7 on v6

--- a/solution.py
+++ b/solution.py
@@ -31,20 +31,6 @@
 
 def dot(a, b, dims=((1,), (0,))):
     return lax.dot_general(a, b, (dims, ((), ())), preferred_element_type=f32)
-
-
-def in_pieces(sums):
-    high = sums.astype(bf16).astype(f32)
-    middle = (sums - high).astype(bf16).astype(f32)
-    low = sums - high - middle
-    row = lax.broadcasted_iota(jnp.int32, (EXTRA, sums.shape[1]), 0)
-    pieces = jnp.where(row == 0, high, jnp.where(row == 1, middle, jnp.where(row == 2, low, 0.0)))
-    return pieces.astype(bf16)
-
-
-def from_pieces(rows):
-    rows = rows.astype(f32)
-    return rows[0:1] + (rows[1:2] + rows[2:3])
 
 
 def attention_kernel(
@@ -146,17 +132,14 @@
     onward[...] = (two[...].astype(f32) + jnp.where(x == 1, side[...].astype(f32), 0.0)).astype(bf16)
 
 
-def finish_kernel(gain, kv_own, kv_peer, grad_own, side, ahead, gathered, own, peer, gains):
+def finish_kernel(gain, kv_own, kv_peer, grad_own, side, ahead, own, peer):
     core, x = lax.axis_index("core"), lax.axis_index("x")
-    sums = jnp.sum(gathered[...], axis=0, keepdims=True)
-    gains[...] = sums
-    peer[ROWS:] = in_pieces(sums)
     for part, block, out in ((kv_own, core, own), (kv_peer, 1 - core, peer)):
         total = grad_own[block] + ahead[block].astype(f32)
         total = total + jnp.where(x == 0, side[block].astype(f32), 0.0)
         unit, inverse = norm_rows(part[:ROWS, :HEAD])
-        out[:ROWS, :HEAD] = norm_backward(total[:, :HEAD], unit, inverse, gain[:, HEAD:]).astype(bf16)
-        out[:ROWS, HEAD:] = total[:, HEAD:].astype(bf16)
+        out[:, :HEAD] = norm_backward(total[:, :HEAD], unit, inverse, gain[:, HEAD:]).astype(bf16)
+        out[:, HEAD:] = total[:, HEAD:].astype(bf16)
 
 
 def place(out, mine, other):
@@ -181,11 +164,10 @@
 
 
 def join_keys_kernel(mine, other, gains, key_grad, value_grad, q_gain_grad, k_gain_grad):
-    place(key_grad, mine[:, :HEAD], other[:ROWS, :HEAD])
-    place(value_grad, mine[:, HEAD:], other[:ROWS, HEAD:])
-    sums = gains[...] + from_pieces(other[ROWS:])
-    q_gain_grad[...] = sums[:, :HEAD]
-    k_gain_grad[...] = sums[:, HEAD:]
+    place(key_grad, mine[:, :HEAD], other[:, :HEAD])
+    place(value_grad, mine[:, HEAD:], other[:, HEAD:])
+    q_gain_grad[...] = gains[:, :HEAD]
+    k_gain_grad[...] = gains[:, HEAD:]
 
 
 def vmem(count):
@@ -271,8 +253,10 @@
     kv_mine, kv_other, lead = lax.optimization_barrier(
         (pack(first, keys, values), pack(~first, keys, values), lead)
     )
-    kv_two, kv_two_x, kv_one_x = hop(kv_mine, 2), hop(kv_other, 2, True), hop(kv_other, 1, True)
+    kv_two, kv_two_x = hop(kv_mine, 2), hop(kv_other, 2, True)
     kv_one = swap(jnp.where(lead, kv_mine, kv_two), "x")
+    pairs = [(c, 2 + (1 - c)) for c in range(2)] + [(2 + c, c) for c in range(2)]
+    kv_one_x = lax.ppermute(jnp.where(lead, kv_other, kv_two_x), ("x", "core"), pairs)
     kv_peer = swap(kv_other)
     gain, kv_peer = lax.optimization_barrier((gain, kv_peer))
 
@@ -284,24 +268,25 @@
     attended, q_grad, to_peer, grad_own, grad_one, grad_two, gains = attention(
         gain, q_mine, g_mine, q_peer, g_peer, kv_mine, kv_peer, kv_one, kv_one_x, kv_two, kv_two_x
     )
-    gains = gains + swap(gains, "x")
-    gains, grad_one = lax.optimization_barrier((gains, grad_one))
     side = swap(grad_one, "x")
     from_peer = swap(to_peer)
+    lines = lax.axis_size("y") * lax.axis_size("z")
+    gathered = lax.all_to_all(
+        jnp.broadcast_to(gains, (lines, wide)), ("y", "z"), 0, 0, tiled=True
+    )
+    gathered, side = lax.optimization_barrier((gathered, side))
+    (onward,) = small(onward_kernel, [((2, ROWS, wide), bf16)], "onward", grad_two, side)
+    gathered, onward = lax.optimization_barrier((gathered, onward))
+    ahead = hop(onward, -2)
+    gains = lax.psum(jnp.sum(gathered, axis=0, keepdims=True), ("dp", "x", "core"))
     attended, q_grad = small(
         join_queries_kernel, [((ROWS, 4 * HEAD), bf16)] * 2, "join_queries", attended, q_grad, from_peer
     )
-    gains, attended, q_grad = lax.optimization_barrier((gains, attended, q_grad))
-    lines = lax.axis_size("dp") * lax.axis_size("y") * lax.axis_size("z")
-    gathered = lax.all_to_all(
-        jnp.broadcast_to(gains, (lines, wide)), ("dp", "y", "z"), 0, 0, tiled=True
-    )
-    (onward,) = small(onward_kernel, [((2, ROWS, wide), bf16)], "onward", grad_two, side)
-    ahead = hop(onward, -2)
-    kv_grad, kv_grad_peer, gains = small(
+    gains, ahead, attended, q_grad = lax.optimization_barrier((gains, ahead, attended, q_grad))
+    kv_grad, kv_grad_peer = small(
         finish_kernel,
-        [((ROWS, wide), bf16), ((ROWS + EXTRA, wide), bf16), ((1, wide), f32)],
-        "finish", gain, kv_mine, kv_peer, grad_own, side, ahead, gathered,
+        [((ROWS, wide), bf16)] * 2,
+        "finish", gain, kv_mine, kv_peer, grad_own, side, ahead,
     )
     kv_grad_x = swap(kv_grad_peer)
     key_grad, value_grad, q_gain_grad, k_gain_grad = small(

time: 108 us -> 103 us (0.954)
  blocking collectives: 38.7 us -> 14.3 us
  starting transfers between devices: 42.3 us -> 49.5 us
  local copies, waits for them, and re-layouts: 0.85 us -> 7.25 us
  waiting for transfers between devices: 11.6 us -> 15.8 us
    all_to_all x1 -> x0, blocking collectives: 38.7 us -> none  [per_device(): lax.all_to_all(jnp.broadcast_to(gains, (lines, wide)), ('dp', 'y', 'z'),...]
    all_to_all x0 -> x1, starting transfers between devices: none -> 16.1 us  [per_device(): lax.all_to_all(jnp.broadcast_to(gains, (lines, wide)), ('y', 'z'), 0, 0,...]
    psum x0 -> x1, blocking collectives: none -> 14.3 us  [per_device(): lax.psum(jnp.sum(gathered, axis=0, keepdims=True), ('dp', 'x', 'core'))]
    all_to_all x0 -> x1, waiting for transfers between devices: none -> 7.98 us  [per_device(): lax.all_to_all(jnp.broadcast_to(gains, (lines, wide)), ('y', 'z'), 0, 0,...]
    ppermute x8 -> x7, starting transfers between devices: 28.6 us -> 22.2 us  [swap(): return lax.ppermute(array, axis, [(0, 1), (1, 0)])]
    unnamed x11 -> x23, local copies, waits for them, and re-layouts: 0.71 us -> 6.52 us
    ppermute x4 -> x3, starting transfers between devices: 13.7 us -> 8.13 us  [hop(): lax.ppermute(array, SEQ, [(i, j) for i, j in pairs if 0 <= j < shards])]
    ppermute x8 -> x7, waiting for transfers between devices: 11.6 us -> 7.85 us  [swap(): return lax.ppermute(array, axis, [(0, 1), (1, 0)])]
  transfers between devices with their start and end apart: 12 -> 12, of which waited for: 5 -> 4; matrix products, arithmetic and copies ran while one was open for 0% -> 3% of each run, Pallas kernels for 1% -> 1%
where the time goes in v7:
time: 103 us; the launch traced here: 102 us
  starting transfers between devices  49.5 us (48%)
  waiting for transfers between devices  15.8 us (15%)
  blocking collectives  14.3 us (14%)
  Pallas kernels  12.2 us (12%)
  local copies, waits for them, and re-layouts  7.25 us (7%)
  other arithmetic  2.28 us (2%)
    ppermute x7, starting transfers between devices, swap(): return lax.ppermute(array, axis, [(0, 1), (1, 0)])  22.2 us
    all_to_all x1, starting transfers between devices, per_device(): lax.all_to_all(jnp.broadcast_to(gains, (lines, wide)), ('y', 'z'), 0, 0,...  16.1 us
    psum x1, blocking collectives, per_device(): lax.psum(jnp.sum(gathered, axis=0, keepdims=True), ('dp', 'x', 'core'))  14.3 us
    pallas_call x1, Pallas kernels, attention(): pl.pallas_call(attention_kernel, out_shape=(shape((ROWS, 2 * HEAD), bf16)...  9.65 us
    ppermute x3, starting transfers between devices, hop(): lax.ppermute(array, SEQ, [(i, j) for i, j in pairs if 0 <= j < shards])  8.13 us
    all_to_all x1, waiting for transfers between devices, per_device(): lax.all_to_all(jnp.broadcast_to(gains, (lines, wide)), ('y', 'z'), 0, 0,...  7.98 us
    ppermute x7, waiting for transfers between devices, swap(): return lax.ppermute(array, axis, [(0, 1), (1, 0)])  7.85 us
    unnamed x23, local copies, waits for them, and re-layouts  6.52 us
  transfers between devices with their start and end apart: 12, of which 4 were waited for; matrix products, arithmetic and copies ran while one was open for 3% of the time, Pallas kernels for 1%

profile of v7, /device:TPU:1, one launch (start us, length us, event | category | flops | bytes accessed | tf_op | source)
XLA Modules:
  0.0 102.3 jit_solution(8976634324398170041)
XLA Ops:
  0.7 0.7 copy-done.8
  1.3 1.1 %broadcast_select_fusion.6 = (bf16[256,256]{1,0:T(8,128)(2,1)S(1)}, bf16[256,256]{1,0:T(8,128)(2,1)S(1)}, bf16[256,256]{1,0:T(8,128)(2,1)S(1)}, bf16[256,256]{1,0:T(8,128)(2,1)S(1)}) fusion(pred[]{:T(512)S(6)} %not.3, bf16[256,512]{1,0:T(8,128)(2,1)} %bitcast.22, pred[]{:T(512)S(6)} %eq.6, bf16[256,512]{1,0:T(8,128)(2,1)} %bitcast.23), kind=kLoop, calls=%fused_computation.11 | loop fusion | flops 262144 | bytes 1048578 | tf_op jit(solution)/shard_map/jit(_where)/select_n | solution.py:245
  2.5 0.0 copy-start.6
  2.5 5.5 %collective-permute-start.5 = (bf16[272,512]{1,0:T(8,128)(2,1)S(1)}, bf16[272,512]{1,0:T(8,128)(2,1)S(1)}, u32[]{:S(2)}, u32[]{:S(2)}) collective-permute-start(bf16[272,512]{1,0:T(8,128)(2,1)S(1)} %get-tuple-element.34), channel_id=1, source_target_pairs={{0,5},{1,4},{2,7},{3,6},{4,9},{5,8},{6,11},{7,10},{8,13},{9,12},{1... | collective-permute-start | bytes 835592 | tf_op jit(solution)/shard_map/ppermute | solution.py:233
  8.1 4.7 %collective-permute-start = (bf16[272,512]{1,0:T(8,128)(2,1)S(1)}, bf16[272,512]{1,0:T(8,128)(2,1)S(1)}, u32[]{:S(2)}, u32[]{:S(2)}) collective-permute-start(bf16[272,512]{1,0:T(8,128)(2,1)S(1)} %get-tuple-element.34), channel_id=1, source_target_pairs={{0,1},{1,0},{2,3},{3,2},{4,5},{5,4},{6,7},{7,6},{8,9},{9,8},{10,11... | collective-permute-start | bytes 835592 | tf_op jit(solution)/shard_map/ppermute | solution.py:236
  12.8 1.3 %collective-permute-start.3 = (bf16[272,512]{1,0:T(8,128)(2,1)S(1)}, bf16[272,512]{1,0:T(8,128)(2,1)S(1)}, u32[]{:S(2)}, u32[]{:S(2)}) collective-permute-start(bf16[272,512]{1,0:T(8,128)(2,1)S(1)} %get-tuple-element.36.kv_own), channel_id=1, source_target_pairs={{0,4},{1,5},{2,6},{3,7},{4,8},{5,9},{6,10},{7,11},{8,12},{9,13},{1... | collective-permute-start | bytes 835592 | tf_op jit(solution)/shard_map/ppermute | solution.py:233
  14.1 2.6 %collective-permute-start.1 = (bf16[256,512]{1,0:T(8,128)(2,1)S(1)}, bf16[256,512]{1,0:T(8,128)(2,1)S(1)}, u32[]{:S(2)}, u32[]{:S(2)}) collective-permute-start(bf16[256,512]{1,0:T(8,128)(2,1)S(1)} %get-tuple-element.64), channel_id=1, source_target_pairs={{0,1},{1,0},{2,3},{3,2},{4,5},{5,4},{6,7},{7,6},{8,9},{9,8},{10,11... | collective-permute-start | bytes 786440 | tf_op jit(solution)/shard_map/ppermute | solution.py:236
  16.8 0.0 collective-permute-done.5.kv_two_x
  16.8 0.0 copy-start.7
  16.8 3.1 %collective-permute-start.6 = (bf16[272,512]{1,0:T(8,128)(2,1)S(1)}, bf16[272,512]{1,0:T(8,128)(2,1)S(1)}, u32[]{:S(2)}, u32[]{:S(2)}) collective-permute-start(bf16[272,512]{1,0:T(8,128)(2,1)S(1)} %broadcast_select_fusion), channel_id=1, source_target_pairs={{0,3},{1,2},{2,0},{3,1},{4,7},{5,6},{6,4},{7,5},{8,11},{9,10},{10,... | collective-permute-start | bytes 835592 | tf_op jit(solution)/shard_map/ppermute | solution.py:259
  20.0 0.0 collective-permute-done.3.kv_two
  20.0 2.6 %collective-permute-start.4 = (bf16[272,512]{1,0:T(8,128)(2,1)S(1)}, bf16[272,512]{1,0:T(8,128)(2,1)S(1)}, u32[]{:S(2)}, u32[]{:S(2)}) collective-permute-start(bf16[272,512]{1,0:T(8,128)(2,1)S(1)} %broadcast_select_fusion.1), channel_id=1, source_target_pairs={{0,2},{2,0},{1,3},{3,1},{4,6},{6,4},{5,7},{7,5},{8,10},{10,8},{9,1... | collective-permute-start | bytes 835592 | tf_op jit(solution)/shard_map/ppermute | solution.py:236
  22.7 0.0 copy-start.10
  22.7 0.0 copy-start.9
  22.7 3.6 %collective-permute-start.2 = (bf16[256,512]{1,0:T(8,128)(2,1)S(1)}, bf16[256,512]{1,0:T(8,128)(2,1)S(1)}, u32[]{:S(2)}, u32[]{:S(2)}) collective-permute-start(bf16[256,512]{1,0:T(8,128)(2,1)S(1)} %get-tuple-element.62), channel_id=1, source_target_pairs={{0,1},{1,0},{2,3},{3,2},{4,5},{5,4},{6,7},{7,6},{8,9},{9,8},{10,11... | collective-permute-start | bytes 786440 | tf_op jit(solution)/shard_map/ppermute | solution.py:236
  26.3 0.0 copy-done.10
  26.3 0.0 copy-done.9
  26.4 0.0 collective-permute-done.kv_peer
  26.4 0.0 copy-start
  26.4 0.0 collective-permute-done.1.q_peer
  26.4 1.1 %collective-permute-done.2.g_peer = bf16[256,512]{1,0:T(8,128)(2,1)S(1)} collective-permute-done((bf16[256,512]{1,0:T(8,128)(2,1)S(1)}, bf16[256,512]{1,0:T(8,128)(2,1)S(1)}, u32[]{:S(2)}, u32[]{:S(2)}) %collective-permute-start.2) | collective-permute-done | bytes 262176 | tf_op jit(solution)/shard_map/ppermute | solution.py:236
  27.5 0.0 collective-permute-done.6.kv_one_x
  27.5 5.6 %collective-permute-done.4.kv_one = bf16[272,512]{1,0:T(8,128)(2,1)S(1)} collective-permute-done((bf16[272,512]{1,0:T(8,128)(2,1)S(1)}, bf16[272,512]{1,0:T(8,128)(2,1)S(1)}, u32[]{:S(2)}, u32[]{:S(2)}) %collective-permute-start.4) | collective-permute-done | bytes 278560 | tf_op jit(solution)/shard_map/ppermute | solution.py:236
  33.1 9.6 %attention.1 = (bf16[256,512]{1,0:T(8,128)(2,1)S(1)}, bf16[256,512]{1,0:T(8,128)(2,1)S(1)}, bf16[256,1024]{1,0:T(8,128)(2,1)}, f32[2,256,512]{2,1,0:T(8,128)S(1)...) custom-call(f32[1,512]{1,0:T(1,128)S(1)} %bitcast.16, ...), custom_call_target="tpu_custom_call" | custom-call | flops 8589934592 | bytes 8388608 | tf_op jit(solution)/shard_map/attention/pallas_call | solution.py:179
  42.7 0.7 copy-done.2
  43.4 0.7 copy-done.4
  44.1 2.8 %collective-permute-start.7 = (bf16[2,256,512]{2,1,0:T(8,128)(2,1)S(1)}, bf16[2,256,512]{2,1,0:T(8,128)(2,1)S(1)}, u32[]{:S(2)}, u32[]{:S(2)}) collective-permute-start(bf16[2,256,512]{2,1,0:T(8,128)(2,1)S(1)} %get-tuple-element.40), channel_id=1, source_target_pairs={{0,2},{2,0},{1,3},{3,1},{4,6},{6,4},{5,7},{7,5},{8,10},{10,8},{9,1... | collective-permute-start | bytes 1572872 | tf_op jit(solution)/shard_map/ppermute | solution.py:236
  46.9 0.7 broadcast_in_dim.25
  47.6 16.1 %all-to-all-start = ((f32[64,1,512]{2,1,0:T(1,128)}), f32[64,1,512]{2,1,0:T(1,128)}, u32[]{:S(2)}, u32[]{:S(2)}) async-start(f32[64,1,512]{2,1,0:T(1,128)} %broadcast_in_dim.25), calls=%async_computation | async-start | bytes 262144 | tf_op jit(solution)/shard_map/all_to_all | solution.py:274
  63.7 3.3 %collective-permute-start.9 = (bf16[256,1024]{1,0:T(8,128)(2,1)}, bf16[256,1024]{1,0:T(8,128)(2,1)S(1)}, u32[]{:S(2)}, u32[]{:S(2)}) collective-permute-start(bf16[256,1024]{1,0:T(8,128)(2,1)} %get-tuple-element.48), channel_id=1, source_target_pairs={{0,1},{1,0},{2,3},{3,2},{4,5},{5,4},{6,7},{7,6},{8,9},{9,8},{10,11... | collective-permute-start | bytes 1572872 | tf_op jit(solution)/shard_map/ppermute | solution.py:236
  67.1 8.0 %all-to-all-done = f32[64,1,512]{2,1,0:T(1,128)} async-done(((f32[64,1,512]{2,1,0:T(1,128)}), f32[64,1,512]{2,1,0:T(1,128)}, u32[]{:S(2)}, u32[]{:S(2)}) %all-to-all-start) | async-done | bytes 131104 | tf_op jit(solution)/shard_map/all_to_all | solution.py:274
  75.1 1.6 %copy.15 = f32[64,1,512]{2,0,1:T(8,128)} copy(f32[64,1,512]{2,1,0:T(1,128)} %all-to-all-done) | data formatting | bytes 262144
  76.7 0.0 collective-permute-done.7.side
  76.7 0.2 onward.1
  76.8 1.3 %collective-permute-start.8 = (bf16[2,256,512]{2,1,0:T(8,128)(2,1)S(1)}, bf16[2,256,512]{2,1,0:T(8,128)(2,1)S(1)}, u32[]{:S(2)}, u32[]{:S(2)}) collective-permute-start(bf16[2,256,512]{2,1,0:T(8,128)(2,1)S(1)} %onward.1), channel_id=1, source_target_pairs={{4,0},{5,1},{6,2},{7,3},{8,4},{9,5},{10,6},{11,7},{12,8},{13,9},{1... | collective-permute-start | bytes 1572872 | tf_op jit(solution)/shard_map/ppermute | solution.py:233
  78.1 0.9 reduce_sum.9
  79.1 0.0 collective-permute-done.9.from_peer
  79.1 0.0 copy-start.3
  79.1 0.9 copy-done.3
  80.0 0.9 copy-done.5
  81.0 1.1 %join_queries.1 = (bf16[256,1024]{1,0:T(8,128)(2,1)}, bf16[256,1024]{1,0:T(8,128)(2,1)}) custom-call(bf16[256,512]{1,0:T(8,128)(2,1)S(1)} %copy-done.3, bf16[256,512]{1,0:T(8,128)(2,1)S(1)} %copy-done.5, bf16[256,1024]{1,0:T(8,128)(2,1)S(1)} %collective-permute-done.9.from_peer), custom_call_target="tpu_custom_call" | custom-call | tf_op jit(solution)/shard_map/join_queries/pallas_call | solution.py:213
  82.1 14.3 %psum.7.gains = f32[1,512]{1,0:T(1,128)S(1)} all-reduce(f32[1,512]{1,0:T(1,128)S(1)} %bitcast.24), channel_id=1, replica_groups=mesh['dp'=2,'y'=8,'z'=8,'x'=2,'core'=2] {'dp','x','core'}, use_global_device_ids=true, to_apply=%region_1.2 | all-reduce | flops 512 | bytes 4096 | tf_op jit(solution)/shard_map/psum | solution.py:281
  96.4 0.0 collective-permute-done.8.ahead
  96.4 1.0 copy-done.1
  97.3 0.4 finish.1
  97.8 2.6 %collective-permute-start.10 = (bf16[256,512]{1,0:T(8,128)(2,1)S(1)}, bf16[256,512]{1,0:T(8,128)(2,1)S(1)}, u32[]{:S(2)}, u32[]{:S(2)}) collective-permute-start(bf16[256,512]{1,0:T(8,128)(2,1)S(1)} %get-tuple-element.56), channel_id=1, source_target_pairs={{0,1},{1,0},{2,3},{3,2},{4,5},{5,4},{6,7},{7,6},{8,9},{9,8},{10,11... | collective-permute-start | bytes 786440 | tf_op jit(solution)/shard_map/ppermute | solution.py:236
  100.3 1.1 %collective-permute-done.10.other = bf16[256,512]{1,0:T(8,128)(2,1)S(1)} collective-permute-done((bf16[256,512]{1,0:T(8,128)(2,1)S(1)}, bf16[256,512]{1,0:T(8,128)(2,1)S(1)}, u32[]{:S(2)}, u32[]{:S(2)}) %collective-permute-start.10) | collective-permute-done | bytes 262176 | tf_op jit(solution)/shard_map/ppermute | solution.py:236
  101.5 0.9 join_keys.1
  (15 shorter events, 0.2 us)
Async XLA Ops:
  0.6 0.7 copy-start.8
  2.5 11.6 %copy-start.6 = (bf16[1,256,1024]{2,1,0:T(8,128)(2,1)S(1)}, bf16[1,256,1024]{2,1,0:T(8,128)(2,1)}, u32[]{:S(2)}) copy-start(bf16[1,256,1024]{2,1,0:T(8,128)(2,1)} %param.7) | copy-start | bytes 1572868
  2.5 14.2 %collective-permute-start.5 = (bf16[272,512]{1,0:T(8,128)(2,1)S(1)}, bf16[272,512]{1,0:T(8,128)(2,1)S(1)}, u32[]{:S(2)}, u32[]{:S(2)}) collective-permute-start(bf16[272,512]{1,0:T(8,128)(2,1)S(1)} %get-tuple-element.34), channel_id=1, source_target_pairs={{0,5},{1,4},{2,7},{3,6},{4,9},{5,8},{6,11},{7,10},{8,13},{9,12},{1... | collective-permute-start | bytes 835592 | tf_op jit(solution)/shard_map/ppermute | solution.py:233
  8.1 18.3 %collective-permute-start = (bf16[272,512]{1,0:T(8,128)(2,1)S(1)}, bf16[272,512]{1,0:T(8,128)(2,1)S(1)}, u32[]{:S(2)}, u32[]{:S(2)}) collective-permute-start(bf16[272,512]{1,0:T(8,128)(2,1)S(1)} %get-tuple-element.34), channel_id=1, source_target_pairs={{0,1},{1,0},{2,3},{3,2},{4,5},{5,4},{6,7},{7,6},{8,9},{9,8},{10,11... | collective-permute-start | bytes 835592 | tf_op jit(solution)/shard_map/ppermute | solution.py:236
  12.8 7.2 %collective-permute-start.3 = (bf16[272,512]{1,0:T(8,128)(2,1)S(1)}, bf16[272,512]{1,0:T(8,128)(2,1)S(1)}, u32[]{:S(2)}, u32[]{:S(2)}) collective-permute-start(bf16[272,512]{1,0:T(8,128)(2,1)S(1)} %get-tuple-element.36.kv_own), channel_id=1, source_target_pairs={{0,4},{1,5},{2,6},{3,7},{4,8},{5,9},{6,10},{7,11},{8,12},{9,13},{1... | collective-permute-start | bytes 835592 | tf_op jit(solution)/shard_map/ppermute | solution.py:233
  14.1 12.2 %collective-permute-start.1 = (bf16[256,512]{1,0:T(8,128)(2,1)S(1)}, bf16[256,512]{1,0:T(8,128)(2,1)S(1)}, u32[]{:S(2)}, u32[]{:S(2)}) collective-permute-start(bf16[256,512]{1,0:T(8,128)(2,1)S(1)} %get-tuple-element.64), channel_id=1, source_target_pairs={{0,1},{1,0},{2,3},{3,2},{4,5},{5,4},{6,7},{7,6},{8,9},{9,8},{10,11... | collective-permute-start | bytes 786440 | tf_op jit(solution)/shard_map/ppermute | solution.py:236
  16.8 5.8 %copy-start.7 = (bf16[1,256,1024]{2,1,0:T(8,128)(2,1)S(1)}, bf16[1,256,1024]{2,1,0:T(8,128)(2,1)}, u32[]{:S(2)}) copy-start(bf16[1,256,1024]{2,1,0:T(8,128)(2,1)} %param.10) | copy-start | bytes 1572868
  16.8 10.6 %collective-permute-start.6 = (bf16[272,512]{1,0:T(8,128)(2,1)S(1)}, bf16[272,512]{1,0:T(8,128)(2,1)S(1)}, u32[]{:S(2)}, u32[]{:S(2)}) collective-permute-start(bf16[272,512]{1,0:T(8,128)(2,1)S(1)} %broadcast_select_fusion), channel_id=1, source_target_pairs={{0,3},{1,2},{2,0},{3,1},{4,7},{5,6},{6,4},{7,5},{8,11},{9,10},{10,... | collective-permute-start | bytes 835592 | tf_op jit(solution)/shard_map/ppermute | solution.py:259
  20.0 13.1 %collective-permute-start.4 = (bf16[272,512]{1,0:T(8,128)(2,1)S(1)}, bf16[272,512]{1,0:T(8,128)(2,1)S(1)}, u32[]{:S(2)}, u32[]{:S(2)}) collective-permute-start(bf16[272,512]{1,0:T(8,128)(2,1)S(1)} %broadcast_select_fusion.1), channel_id=1, source_target_pairs={{0,2},{2,0},{1,3},{3,1},{4,6},{6,4},{5,7},{7,5},{8,10},{10,8},{9,1... | collective-permute-start | bytes 835592 | tf_op jit(solution)/shard_map/ppermute | solution.py:236
  22.7 3.7 %copy-start.10 = (f32[256]{0:T(256)S(1)}, f32[256]{0:T(256)}, u32[]{:S(2)}) copy-start(f32[256]{0:T(256)} %param.11) | copy-start | bytes 3076
  22.7 3.6 %copy-start.9 = (f32[256]{0:T(256)S(1)}, f32[256]{0:T(256)}, u32[]{:S(2)}) copy-start(f32[256]{0:T(256)} %param.12) | copy-start | bytes 3076
  22.7 4.7 %collective-permute-start.2 = (bf16[256,512]{1,0:T(8,128)(2,1)S(1)}, bf16[256,512]{1,0:T(8,128)(2,1)S(1)}, u32[]{:S(2)}, u32[]{:S(2)}) collective-permute-start(bf16[256,512]{1,0:T(8,128)(2,1)S(1)} %get-tuple-element.62), channel_id=1, source_target_pairs={{0,1},{1,0},{2,3},{3,2},{4,5},{5,4},{6,7},{7,6},{8,9},{9,8},{10,11... | collective-permute-start | bytes 786440 | tf_op jit(solution)/shard_map/ppermute | solution.py:236
  26.4 16.4 %copy-start = (bf16[272,512]{1,0:T(8,128)(2,1)}, bf16[272,512]{1,0:T(8,128)(2,1)S(1)}, u32[]{:S(2)}) copy-start(bf16[272,512]{1,0:T(8,128)(2,1)S(1)} %collective-permute-done.kv_peer) | copy-start | bytes 835588
  42.7 0.7 copy-start.2
  43.4 0.7 copy-start.4
  44.1 32.5 %collective-permute-start.7 = (bf16[2,256,512]{2,1,0:T(8,128)(2,1)S(1)}, bf16[2,256,512]{2,1,0:T(8,128)(2,1)S(1)}, u32[]{:S(2)}, u32[]{:S(2)}) collective-permute-start(bf16[2,256,512]{2,1,0:T(8,128)(2,1)S(1)} %get-tuple-element.40), channel_id=1, source_target_pairs={{0,2},{2,0},{1,3},{3,1},{4,6},{6,4},{5,7},{7,5},{8,10},{10,8},{9,1... | collective-permute-start | bytes 1572872 | tf_op jit(solution)/shard_map/ppermute | solution.py:236
  47.6 27.4 %all-to-all-start = ((f32[64,1,512]{2,1,0:T(1,128)}), f32[64,1,512]{2,1,0:T(1,128)}, u32[]{:S(2)}, u32[]{:S(2)}) async-start(f32[64,1,512]{2,1,0:T(1,128)} %broadcast_in_dim.25), calls=%async_computation | async-start | bytes 262144 | tf_op jit(solution)/shard_map/all_to_all | solution.py:274
  63.7 15.3 %collective-permute-start.9 = (bf16[256,1024]{1,0:T(8,128)(2,1)}, bf16[256,1024]{1,0:T(8,128)(2,1)S(1)}, u32[]{:S(2)}, u32[]{:S(2)}) collective-permute-start(bf16[256,1024]{1,0:T(8,128)(2,1)} %get-tuple-element.48), channel_id=1, source_target_pairs={{0,1},{1,0},{2,3},{3,2},{4,5},{5,4},{6,7},{7,6},{8,9},{9,8},{10,11... | collective-permute-start | bytes 1572872 | tf_op jit(solution)/shard_map/ppermute | solution.py:236
  76.8 19.6 %collective-permute-start.8 = (bf16[2,256,512]{2,1,0:T(8,128)(2,1)S(1)}, bf16[2,256,512]{2,1,0:T(8,128)(2,1)S(1)}, u32[]{:S(2)}, u32[]{:S(2)}) collective-permute-start(bf16[2,256,512]{2,1,0:T(8,128)(2,1)S(1)} %onward.1), channel_id=1, source_target_pairs={{4,0},{5,1},{6,2},{7,3},{8,4},{9,5},{10,6},{11,7},{12,8},{13,9},{1... | collective-permute-start | bytes 1572872 | tf_op jit(solution)/shard_map/ppermute | solution.py:233
  79.1 1.0 copy-start.3
  80.0 0.9 copy-start.5
  96.4 1.0 copy-start.1
  97.8 3.7 %collective-permute-start.10 = (bf16[256,512]{1,0:T(8,128)(2,1)S(1)}, bf16[256,512]{1,0:T(8,128)(2,1)S(1)}, u32[]{:S(2)}, u32[]{:S(2)}) collective-permute-start(bf16[256,512]{1,0:T(8,128)(2,1)S(1)} %get-tuple-element.56), channel_id=1, source_target_pairs={{0,1},{1,0},{2,3},{3,2},{4,5},{5,4},{6,7},{7,6},{8,9},{9,8},{10,11... | collective-permute-start | bytes 786440 | tf_op jit(solution)/shard_map/ppermute | solution.py:236

commit v8 on v7

--- a/solution.py
+++ b/solution.py
@@ -270,6 +270,10 @@
     )
     side = swap(grad_one, "x")
     from_peer = swap(to_peer)
+    attended, q_grad = small(
+        join_queries_kernel, [((ROWS, 4 * HEAD), bf16)] * 2, "join_queries", attended, q_grad, from_peer
+    )
+    gains, attended, q_grad = lax.optimization_barrier((gains, attended, q_grad))
     lines = lax.axis_size("y") * lax.axis_size("z")
     gathered = lax.all_to_all(
         jnp.broadcast_to(gains, (lines, wide)), ("y", "z"), 0, 0, tiled=True
@@ -279,10 +283,7 @@
     gathered, onward = lax.optimization_barrier((gathered, onward))
     ahead = hop(onward, -2)
     gains = lax.psum(jnp.sum(gathered, axis=0, keepdims=True), ("dp", "x", "core"))
-    attended, q_grad = small(
-        join_queries_kernel, [((ROWS, 4 * HEAD), bf16)] * 2, "join_queries", attended, q_grad, from_peer
-    )
-    gains, ahead, attended, q_grad = lax.optimization_barrier((gains, ahead, attended, q_grad))
+    gains, ahead = lax.optimization_barrier((gains, ahead))
     kv_grad, kv_grad_peer = small(
         finish_kernel,
         [((ROWS, wide), bf16)] * 2,

time: 103 us -> 97.1 us (0.943)
  blocking collectives: 14.3 us -> 40.8 us
  starting transfers between devices: 49.5 us -> 33.4 us
  waiting for transfers between devices: 15.8 us -> 7.87 us
  local copies, waits for them, and re-layouts: 7.25 us -> 0.77 us
    all_to_all x0 -> x1, blocking collectives: none -> 27 us  [per_device(): lax.all_to_all(jnp.broadcast_to(gains, (lines, wide)), ('y', 'z'), 0, 0,...]
    all_to_all x1 -> x0, starting transfers between devices: 16.1 us -> none  [per_device(): lax.all_to_all(jnp.broadcast_to(gains, (lines, wide)), ('y', 'z'), 0, 0,...]
    all_to_all x1 -> x0, waiting for transfers between devices: 7.98 us -> none  [per_device(): lax.all_to_all(jnp.broadcast_to(gains, (lines, wide)), ('y', 'z'), 0, 0,...]
    unnamed x23 -> x11, local copies, waits for them, and re-layouts: 6.52 us -> 0.71 us
  transfers between devices with their start and end apart: 12 -> 11, of which waited for: 4 -> 3; matrix products, arithmetic and copies ran while one was open for 3% -> 0% of each run, Pallas kernels for 1% -> 1%
where the time goes in v8:
time: 97.1 us; the launch traced here: 96.6 us
  blocking collectives  40.8 us (42%)
  starting transfers between devices  33.4 us (34%)
  Pallas kernels  11.4 us (12%)
  waiting for transfers between devices  7.87 us (8%)
  other arithmetic  1.37 us (1%)
    all_to_all x1, blocking collectives, per_device(): lax.all_to_all(jnp.broadcast_to(gains, (lines, wide)), ('y', 'z'), 0, 0,...  27 us
    ppermute x7, starting transfers between devices, swap(): return lax.ppermute(array, axis, [(0, 1), (1, 0)])  22.2 us
    psum x1, blocking collectives, per_device(): lax.psum(jnp.sum(gathered, axis=0, keepdims=True), ('dp', 'x', 'core'))  13.8 us
    pallas_call x1, Pallas kernels, attention(): pl.pallas_call(attention_kernel, out_shape=(shape((ROWS, 2 * HEAD), bf16)...  8.85 us
    ppermute x3, starting transfers between devices, hop(): lax.ppermute(array, SEQ, [(i, j) for i, j in pairs if 0 <= j < shards])  8.13 us
    ppermute x7, waiting for transfers between devices, swap(): return lax.ppermute(array, axis, [(0, 1), (1, 0)])  7.86 us
    ppermute x1, starting transfers between devices, per_device(): lax.ppermute(jnp.where(lead, kv_other, kv_two_x), ('x', 'core'), pairs)  3.15 us
    pallas_call x4, Pallas kernels, small(): pl.pallas_call(kernel, out_shape=tuple((jax.ShapeDtypeStruct(*out) for ou...  2.54 us
  transfers between devices with their start and end apart: 11, of which 3 were waited for; matrix products, arithmetic and copies ran while one was open for 0% of the time, Pallas kernels for 1%

profile of v8, /device:TPU:1, one launch (start us, length us, event | category | flops | bytes accessed | tf_op | source)
XLA Modules:
  0.0 96.6 jit_solution(11243463192223969927)
XLA Ops:
  0.6 0.0 copy-start.2
  0.7 0.7 copy-done.2
  1.3 1.1 %broadcast_select_fusion.6 = (bf16[256,256]{1,0:T(8,128)(2,1)S(1)}, bf16[256,256]{1,0:T(8,128)(2,1)S(1)}, bf16[256,256]{1,0:T(8,128)(2,1)S(1)}, bf16[256,256]{1,0:T(8,128)(2,1)S(1)}) fusion(pred[]{:T(512)S(6)} %not.3, bf16[256,512]{1,0:T(8,128)(2,1)} %bitcast.22, pred[]{:T(512)S(6)} %eq.6, bf16[256,512]{1,0:T(8,128)(2,1)} %bitcast.23), kind=kLoop, calls=%fused_computation.11 | loop fusion | flops 262144 | bytes 1048578 | tf_op jit(solution)/shard_map/jit(_where)/select_n | solution.py:245
  2.5 0.0 copy-start
  2.5 5.5 %collective-permute-start.5 = (bf16[272,512]{1,0:T(8,128)(2,1)S(1)}, bf16[272,512]{1,0:T(8,128)(2,1)S(1)}, u32[]{:S(2)}, u32[]{:S(2)}) collective-permute-start(bf16[272,512]{1,0:T(8,128)(2,1)S(1)} %get-tuple-element.35), channel_id=1, source_target_pairs={{0,5},{1,4},{2,7},{3,6},{4,9},{5,8},{6,11},{7,10},{8,13},{9,12},{1... | collective-permute-start | bytes 835592 | tf_op jit(solution)/shard_map/ppermute | solution.py:233
  8.1 4.7 %collective-permute-start = (bf16[272,512]{1,0:T(8,128)(2,1)S(1)}, bf16[272,512]{1,0:T(8,128)(2,1)S(1)}, u32[]{:S(2)}, u32[]{:S(2)}) collective-permute-start(bf16[272,512]{1,0:T(8,128)(2,1)S(1)} %get-tuple-element.35), channel_id=1, source_target_pairs={{0,1},{1,0},{2,3},{3,2},{4,5},{5,4},{6,7},{7,6},{8,9},{9,8},{10,11... | collective-permute-start | bytes 835592 | tf_op jit(solution)/shard_map/ppermute | solution.py:236
  12.8 1.3 %collective-permute-start.3 = (bf16[272,512]{1,0:T(8,128)(2,1)S(1)}, bf16[272,512]{1,0:T(8,128)(2,1)S(1)}, u32[]{:S(2)}, u32[]{:S(2)}) collective-permute-start(bf16[272,512]{1,0:T(8,128)(2,1)S(1)} %get-tuple-element.37.kv_own), channel_id=1, source_target_pairs={{0,4},{1,5},{2,6},{3,7},{4,8},{5,9},{6,10},{7,11},{8,12},{9,13},{1... | collective-permute-start | bytes 835592 | tf_op jit(solution)/shard_map/ppermute | solution.py:233
  14.1 0.0 copy-done
  14.1 2.6 %collective-permute-start.1 = (bf16[256,512]{1,0:T(8,128)(2,1)S(1)}, bf16[256,512]{1,0:T(8,128)(2,1)S(1)}, u32[]{:S(2)}, u32[]{:S(2)}) collective-permute-start(bf16[256,512]{1,0:T(8,128)(2,1)S(1)} %get-tuple-element.66), channel_id=1, source_target_pairs={{0,1},{1,0},{2,3},{3,2},{4,5},{5,4},{6,7},{7,6},{8,9},{9,8},{10,11... | collective-permute-start | bytes 786440 | tf_op jit(solution)/shard_map/ppermute | solution.py:236
  16.8 0.0 collective-permute-done.5.kv_two_x
  16.8 0.0 copy-start.1
  16.8 3.1 %collective-permute-start.6 = (bf16[272,512]{1,0:T(8,128)(2,1)S(1)}, bf16[272,512]{1,0:T(8,128)(2,1)S(1)}, u32[]{:S(2)}, u32[]{:S(2)}) collective-permute-start(bf16[272,512]{1,0:T(8,128)(2,1)S(1)} %broadcast_select_fusion), channel_id=1, source_target_pairs={{0,3},{1,2},{2,0},{3,1},{4,7},{5,6},{6,4},{7,5},{8,11},{9,10},{10,... | collective-permute-start | bytes 835592 | tf_op jit(solution)/shard_map/ppermute | solution.py:259
  20.0 0.0 collective-permute-done.3.kv_two
  20.0 2.6 %collective-permute-start.4 = (bf16[272,512]{1,0:T(8,128)(2,1)S(1)}, bf16[272,512]{1,0:T(8,128)(2,1)S(1)}, u32[]{:S(2)}, u32[]{:S(2)}) collective-permute-start(bf16[272,512]{1,0:T(8,128)(2,1)S(1)} %broadcast_select_fusion.1), channel_id=1, source_target_pairs={{0,2},{2,0},{1,3},{3,1},{4,6},{6,4},{5,7},{7,5},{8,10},{10,8},{9,1... | collective-permute-start | bytes 835592 | tf_op jit(solution)/shard_map/ppermute | solution.py:236
  22.7 0.0 copy-done.1
  22.7 0.0 copy-start.4
  22.7 0.0 copy-start.3
  22.7 3.6 %collective-permute-start.2 = (bf16[256,512]{1,0:T(8,128)(2,1)S(1)}, bf16[256,512]{1,0:T(8,128)(2,1)S(1)}, u32[]{:S(2)}, u32[]{:S(2)}) collective-permute-start(bf16[256,512]{1,0:T(8,128)(2,1)S(1)} %get-tuple-element.64), channel_id=1, source_target_pairs={{0,1},{1,0},{2,3},{3,2},{4,5},{5,4},{6,7},{7,6},{8,9},{9,8},{10,11... | collective-permute-start | bytes 786440 | tf_op jit(solution)/shard_map/ppermute | solution.py:236
  26.3 0.0 copy-done.4
  26.3 0.0 copy-done.3
  26.4 0.0 collective-permute-done.kv_peer
  26.4 0.0 collective-permute-done.1.q_peer
  26.4 1.1 %collective-permute-done.2.g_peer = bf16[256,512]{1,0:T(8,128)(2,1)S(1)} collective-permute-done((bf16[256,512]{1,0:T(8,128)(2,1)S(1)}, bf16[256,512]{1,0:T(8,128)(2,1)S(1)}, u32[]{:S(2)}, u32[]{:S(2)}) %collective-permute-start.2) | collective-permute-done | bytes 262176 | tf_op jit(solution)/shard_map/ppermute | solution.py:236
  27.5 0.0 collective-permute-done.6.kv_one_x
  27.5 5.6 %collective-permute-done.4.kv_one = bf16[272,512]{1,0:T(8,128)(2,1)S(1)} collective-permute-done((bf16[272,512]{1,0:T(8,128)(2,1)S(1)}, bf16[272,512]{1,0:T(8,128)(2,1)S(1)}, u32[]{:S(2)}, u32[]{:S(2)}) %collective-permute-start.4) | collective-permute-done | bytes 278560 | tf_op jit(solution)/shard_map/ppermute | solution.py:236
  33.1 8.8 %attention.1 = (bf16[256,512]{1,0:T(8,128)(2,1)S(1)}, bf16[256,512]{1,0:T(8,128)(2,1)S(1)}, bf16[256,1024]{1,0:T(8,128)(2,1)S(1)}, f32[2,256,512]{2,1,0:T(8,128)...) custom-call(f32[1,512]{1,0:T(1,128)S(1)} %bitcast.16, ...), custom_call_target="tpu_custom_call" | custom-call | flops 8589934592 | bytes 8388608 | tf_op jit(solution)/shard_map/attention/pallas_call | solution.py:179
  41.9 2.7 %collective-permute-start.7 = (bf16[256,1024]{1,0:T(8,128)(2,1)S(1)}, bf16[256,1024]{1,0:T(8,128)(2,1)S(1)}, u32[]{:S(2)}, u32[]{:S(2)}) collective-permute-start(bf16[256,1024]{1,0:T(8,128)(2,1)S(1)} %get-tuple-element.43), channel_id=1, source_target_pairs={{0,1},{1,0},{2,3},{3,2},{4,5},{5,4},{6,7},{7,6},{8,9},{9,8},{10,11... | collective-permute-start | bytes 1572872 | tf_op jit(solution)/shard_map/ppermute | solution.py:236
  44.6 3.0 %collective-permute-start.8 = (bf16[2,256,512]{2,1,0:T(8,128)(2,1)S(1)}, bf16[2,256,512]{2,1,0:T(8,128)(2,1)S(1)}, u32[]{:S(2)}, u32[]{:S(2)}) collective-permute-start(bf16[2,256,512]{2,1,0:T(8,128)(2,1)S(1)} %get-tuple-element.50), channel_id=1, source_target_pairs={{0,2},{2,0},{1,3},{3,1},{4,6},{6,4},{5,7},{7,5},{8,10},{10,8},{9,1... | collective-permute-start | bytes 1572872 | tf_op jit(solution)/shard_map/ppermute | solution.py:236
  47.7 0.0 collective-permute-done.7.from_peer
  47.7 1.1 %join_queries.1 = (bf16[256,1024]{1,0:T(8,128)(2,1)}, bf16[256,1024]{1,0:T(8,128)(2,1)}) custom-call(bf16[256,512]{1,0:T(8,128)(2,1)S(1)} %get-tuple-element.41.att_mine, bf16[256,512]{1,0:T(8,128)(2,1)S(1)} %get-tuple-element.42.grad_mine, bf16[256,1024]{1,0:T(8,128)(2,1)S(1)} %collective-permute-done.7.from_peer), custom_call_target="tpu_custom_call" | custom-call | tf_op jit(solution)/shard_map/join_queries/pallas_call | solution.py:213
  48.8 0.1 broadcast_in_dim.27
  48.8 27.0 %all_to_all.9 = f32[64,1,512]{2,1,0:T(1,128)S(1)} all-to-all(f32[64,1,512]{2,1,0:T(1,128)S(1)} %broadcast_in_dim.27), channel_id=1, replica_groups=mesh['dp'=2,'y'=8,'z'=8,'x'=2,'core'=2] {'y','z'}, dimensions={0} | all-to-all | bytes 262144 | tf_op jit(solution)/shard_map/all_to_all | solution.py:278
  75.9 0.0 collective-permute-done.8.side
  75.9 0.2 onward.1
  76.0 1.3 %collective-permute-start.9 = (bf16[2,256,512]{2,1,0:T(8,128)(2,1)S(1)}, bf16[2,256,512]{2,1,0:T(8,128)(2,1)S(1)}, u32[]{:S(2)}, u32[]{:S(2)}) collective-permute-start(bf16[2,256,512]{2,1,0:T(8,128)(2,1)S(1)} %onward.1), channel_id=1, source_target_pairs={{4,0},{5,1},{6,2},{7,3},{8,4},{9,5},{10,6},{11,7},{12,8},{13,9},{1... | collective-permute-start | bytes 1572872 | tf_op jit(solution)/shard_map/ppermute | solution.py:233
  77.4 13.8 %psum.7.gains = f32[1,512]{1,0:T(1,128)S(1)} all-reduce(f32[1,512]{1,0:T(1,128)S(1)} %bitcast.24), channel_id=1, replica_groups=mesh['dp'=2,'y'=8,'z'=8,'x'=2,'core'=2] {'dp','x','core'}, use_global_device_ids=true, to_apply=%region_1.2 | all-reduce | flops 512 | bytes 4096 | tf_op jit(solution)/shard_map/psum | solution.py:285
  91.2 0.0 collective-permute-done.9.ahead
  91.2 0.4 finish.1
  91.6 3.0 %collective-permute-start.10 = (bf16[256,512]{1,0:T(8,128)(2,1)S(1)}, bf16[256,512]{1,0:T(8,128)(2,1)S(1)}, u32[]{:S(2)}, u32[]{:S(2)}) collective-permute-start(bf16[256,512]{1,0:T(8,128)(2,1)S(1)} %get-tuple-element.58), channel_id=1, source_target_pairs={{0,1},{1,0},{2,3},{3,2},{4,5},{5,4},{6,7},{7,6},{8,9},{9,8},{10,11... | collective-permute-start | bytes 786440 | tf_op jit(solution)/shard_map/ppermute | solution.py:236
  94.6 1.1 %collective-permute-done.10.other = bf16[256,512]{1,0:T(8,128)(2,1)S(1)} collective-permute-done((bf16[256,512]{1,0:T(8,128)(2,1)S(1)}, bf16[256,512]{1,0:T(8,128)(2,1)S(1)}, u32[]{:S(2)}, u32[]{:S(2)}) %collective-permute-start.10) | collective-permute-done | bytes 262176 | tf_op jit(solution)/shard_map/ppermute | solution.py:236
  95.7 0.9 join_keys.1
  (9 shorter events, 0.2 us)
Async XLA Ops:
  0.6 0.7 copy-start.2
  2.5 11.6 %copy-start = (bf16[1,256,1024]{2,1,0:T(8,128)(2,1)S(1)}, bf16[1,256,1024]{2,1,0:T(8,128)(2,1)}, u32[]{:S(2)}) copy-start(bf16[1,256,1024]{2,1,0:T(8,128)(2,1)} %param.7) | copy-start | bytes 1572868
  2.5 14.2 %collective-permute-start.5 = (bf16[272,512]{1,0:T(8,128)(2,1)S(1)}, bf16[272,512]{1,0:T(8,128)(2,1)S(1)}, u32[]{:S(2)}, u32[]{:S(2)}) collective-permute-start(bf16[272,512]{1,0:T(8,128)(2,1)S(1)} %get-tuple-element.35), channel_id=1, source_target_pairs={{0,5},{1,4},{2,7},{3,6},{4,9},{5,8},{6,11},{7,10},{8,13},{9,12},{1... | collective-permute-start | bytes 835592 | tf_op jit(solution)/shard_map/ppermute | solution.py:233
  8.1 18.3 %collective-permute-start = (bf16[272,512]{1,0:T(8,128)(2,1)S(1)}, bf16[272,512]{1,0:T(8,128)(2,1)S(1)}, u32[]{:S(2)}, u32[]{:S(2)}) collective-permute-start(bf16[272,512]{1,0:T(8,128)(2,1)S(1)} %get-tuple-element.35), channel_id=1, source_target_pairs={{0,1},{1,0},{2,3},{3,2},{4,5},{5,4},{6,7},{7,6},{8,9},{9,8},{10,11... | collective-permute-start | bytes 835592 | tf_op jit(solution)/shard_map/ppermute | solution.py:236
  12.8 7.2 %collective-permute-start.3 = (bf16[272,512]{1,0:T(8,128)(2,1)S(1)}, bf16[272,512]{1,0:T(8,128)(2,1)S(1)}, u32[]{:S(2)}, u32[]{:S(2)}) collective-permute-start(bf16[272,512]{1,0:T(8,128)(2,1)S(1)} %get-tuple-element.37.kv_own), channel_id=1, source_target_pairs={{0,4},{1,5},{2,6},{3,7},{4,8},{5,9},{6,10},{7,11},{8,12},{9,13},{1... | collective-permute-start | bytes 835592 | tf_op jit(solution)/shard_map/ppermute | solution.py:233
  14.1 12.2 %collective-permute-start.1 = (bf16[256,512]{1,0:T(8,128)(2,1)S(1)}, bf16[256,512]{1,0:T(8,128)(2,1)S(1)}, u32[]{:S(2)}, u32[]{:S(2)}) collective-permute-start(bf16[256,512]{1,0:T(8,128)(2,1)S(1)} %get-tuple-element.66), channel_id=1, source_target_pairs={{0,1},{1,0},{2,3},{3,2},{4,5},{5,4},{6,7},{7,6},{8,9},{9,8},{10,11... | collective-permute-start | bytes 786440 | tf_op jit(solution)/shard_map/ppermute | solution.py:236
  16.8 5.9 %copy-start.1 = (bf16[1,256,1024]{2,1,0:T(8,128)(2,1)S(1)}, bf16[1,256,1024]{2,1,0:T(8,128)(2,1)}, u32[]{:S(2)}) copy-start(bf16[1,256,1024]{2,1,0:T(8,128)(2,1)} %param.10) | copy-start | bytes 1572868
  16.8 10.6 %collective-permute-start.6 = (bf16[272,512]{1,0:T(8,128)(2,1)S(1)}, bf16[272,512]{1,0:T(8,128)(2,1)S(1)}, u32[]{:S(2)}, u32[]{:S(2)}) collective-permute-start(bf16[272,512]{1,0:T(8,128)(2,1)S(1)} %broadcast_select_fusion), channel_id=1, source_target_pairs={{0,3},{1,2},{2,0},{3,1},{4,7},{5,6},{6,4},{7,5},{8,11},{9,10},{10,... | collective-permute-start | bytes 835592 | tf_op jit(solution)/shard_map/ppermute | solution.py:259
  20.0 13.1 %collective-permute-start.4 = (bf16[272,512]{1,0:T(8,128)(2,1)S(1)}, bf16[272,512]{1,0:T(8,128)(2,1)S(1)}, u32[]{:S(2)}, u32[]{:S(2)}) collective-permute-start(bf16[272,512]{1,0:T(8,128)(2,1)S(1)} %broadcast_select_fusion.1), channel_id=1, source_target_pairs={{0,2},{2,0},{1,3},{3,1},{4,6},{6,4},{5,7},{7,5},{8,10},{10,8},{9,1... | collective-permute-start | bytes 835592 | tf_op jit(solution)/shard_map/ppermute | solution.py:236
  22.7 3.7 %copy-start.4 = (f32[256]{0:T(256)S(1)}, f32[256]{0:T(256)}, u32[]{:S(2)}) copy-start(f32[256]{0:T(256)} %param.11) | copy-start | bytes 3076
  22.7 3.6 %copy-start.3 = (f32[256]{0:T(256)S(1)}, f32[256]{0:T(256)}, u32[]{:S(2)}) copy-start(f32[256]{0:T(256)} %param.12) | copy-start | bytes 3076
  22.7 4.7 %collective-permute-start.2 = (bf16[256,512]{1,0:T(8,128)(2,1)S(1)}, bf16[256,512]{1,0:T(8,128)(2,1)S(1)}, u32[]{:S(2)}, u32[]{:S(2)}) collective-permute-start(bf16[256,512]{1,0:T(8,128)(2,1)S(1)} %get-tuple-element.64), channel_id=1, source_target_pairs={{0,1},{1,0},{2,3},{3,2},{4,5},{5,4},{6,7},{7,6},{8,9},{9,8},{10,11... | collective-permute-start | bytes 786440 | tf_op jit(solution)/shard_map/ppermute | solution.py:236
  41.9 5.7 %collective-permute-start.7 = (bf16[256,1024]{1,0:T(8,128)(2,1)S(1)}, bf16[256,1024]{1,0:T(8,128)(2,1)S(1)}, u32[]{:S(2)}, u32[]{:S(2)}) collective-permute-start(bf16[256,1024]{1,0:T(8,128)(2,1)S(1)} %get-tuple-element.43), channel_id=1, source_target_pairs={{0,1},{1,0},{2,3},{3,2},{4,5},{5,4},{6,7},{7,6},{8,9},{9,8},{10,11... | collective-permute-start | bytes 1572872 | tf_op jit(solution)/shard_map/ppermute | solution.py:236
  44.6 31.2 %collective-permute-start.8 = (bf16[2,256,512]{2,1,0:T(8,128)(2,1)S(1)}, bf16[2,256,512]{2,1,0:T(8,128)(2,1)S(1)}, u32[]{:S(2)}, u32[]{:S(2)}) collective-permute-start(bf16[2,256,512]{2,1,0:T(8,128)(2,1)S(1)} %get-tuple-element.50), channel_id=1, source_target_pairs={{0,2},{2,0},{1,3},{3,1},{4,6},{6,4},{5,7},{7,5},{8,10},{10,8},{9,1... | collective-permute-start | bytes 1572872 | tf_op jit(solution)/shard_map/ppermute | solution.py:236
  76.0 15.2 %collective-permute-start.9 = (bf16[2,256,512]{2,1,0:T(8,128)(2,1)S(1)}, bf16[2,256,512]{2,1,0:T(8,128)(2,1)S(1)}, u32[]{:S(2)}, u32[]{:S(2)}) collective-permute-start(bf16[2,256,512]{2,1,0:T(8,128)(2,1)S(1)} %onward.1), channel_id=1, source_target_pairs={{4,0},{5,1},{6,2},{7,3},{8,4},{9,5},{10,6},{11,7},{12,8},{13,9},{1... | collective-permute-start | bytes 1572872 | tf_op jit(solution)/shard_map/ppermute | solution.py:233
  91.6 4.1 %collective-permute-start.10 = (bf16[256,512]{1,0:T(8,128)(2,1)S(1)}, bf16[256,512]{1,0:T(8,128)(2,1)S(1)}, u32[]{:S(2)}, u32[]{:S(2)}) collective-permute-start(bf16[256,512]{1,0:T(8,128)(2,1)S(1)} %get-tuple-element.58), channel_id=1, source_target_pairs={{0,1},{1,0},{2,3},{3,2},{4,5},{5,4},{6,7},{7,6},{8,9},{9,8},{10,11... | collective-permute-start | bytes 786440 | tf_op jit(solution)/shard_map/ppermute | solution.py:236

commit v9 on v8

--- a/solution.py
+++ b/solution.py
@@ -31,6 +31,20 @@
 
 def dot(a, b, dims=((1,), (0,))):
     return lax.dot_general(a, b, (dims, ((), ())), preferred_element_type=f32)
+
+
+def in_pieces(sums):
+    high = sums.astype(bf16).astype(f32)
+    middle = (sums - high).astype(bf16).astype(f32)
+    low = sums - high - middle
+    row = lax.broadcasted_iota(jnp.int32, (EXTRA, sums.shape[1]), 0)
+    pieces = jnp.where(row == 0, high, jnp.where(row == 1, middle, jnp.where(row == 2, low, 0.0)))
+    return pieces.astype(bf16)
+
+
+def from_pieces(rows):
+    rows = rows.astype(f32)
+    return rows[0:1] + (rows[1:2] + rows[2:3])
 
 
 def attention_kernel(
@@ -61,7 +75,7 @@
 
     for raw, up_raw, tags, first, att_out, grad_out in (
         (q_own, g_own, kv_own, core, attended, q_grad),
-        (q_peer, g_peer, kv_peer, 1 - core, swap.at[:, : 2 * HEAD], swap.at[:, 2 * HEAD :]),
+        (q_peer, g_peer, kv_peer, 1 - core, swap.at[:ROWS, : 2 * HEAD], swap.at[:ROWS, 2 * HEAD :]),
     ):
         for h in range(2):
             unit, _ = norm_rows(raw[:, h * HEAD : (h + 1) * HEAD])
@@ -121,6 +135,8 @@
         k_gain_grad = k_gain_grad + jnp.sum(key_grad[block] * unit, axis=0, keepdims=True)
     sums = jnp.concatenate([q_gain_grad, k_gain_grad], axis=1)
     gains[...] = sums
+    swap[ROWS:, : 2 * HEAD] = in_pieces(sums)
+    swap[ROWS:, 2 * HEAD :] = jnp.zeros((EXTRA, 2 * HEAD), bf16)
     for i in range(2):
         for at, out in ((0, kv_grad_two), (2, kv_grad_one), (4, kv_grad_own)):
             out[i, :, :HEAD] = key_grad[at + i].astype(out.dtype)
@@ -157,10 +173,11 @@
         out[:, width:] = mine
 
 
-def join_queries_kernel(att_mine, grad_mine, from_peer, attended, q_grad):
+def join_queries_kernel(att_mine, grad_mine, from_peer, gains, attended, q_grad, chip_gains):
     wide = 2 * HEAD
-    place(attended, att_mine[...], from_peer[:, :wide])
-    place(q_grad, grad_mine[...], from_peer[:, wide:])
+    place(attended, att_mine[...], from_peer[:ROWS, :wide])
+    place(q_grad, grad_mine[...], from_peer[:ROWS, wide:])
+    chip_gains[...] = gains[...] + from_pieces(from_peer[ROWS:, :wide])
 
 
 def join_keys_kernel(mine, other, gains, key_grad, value_grad, q_gain_grad, k_gain_grad):
@@ -181,7 +198,7 @@
         out_shape=(
             shape((ROWS, 2 * HEAD), bf16),
             shape((ROWS, 2 * HEAD), bf16),
-            shape((ROWS, 4 * HEAD), bf16),
+            shape((ROWS + EXTRA, 4 * HEAD), bf16),
             shape((2, ROWS, 2 * HEAD), f32),
             *(shape((2, ROWS, 2 * HEAD), bf16),) * 2,
             shape((1, 2 * HEAD), f32),
@@ -256,7 +273,8 @@
     kv_two, kv_two_x = hop(kv_mine, 2), hop(kv_other, 2, True)
     kv_one = swap(jnp.where(lead, kv_mine, kv_two), "x")
     pairs = [(c, 2 + (1 - c)) for c in range(2)] + [(2 + c, c) for c in range(2)]
-    kv_one_x = lax.ppermute(jnp.where(lead, kv_other, kv_two_x), ("x", "core"), pairs)
+    relayed, kv_other = lax.optimization_barrier((jnp.where(lead, kv_other, kv_two_x), kv_other))
+    kv_one_x = lax.ppermute(relayed, ("x", "core"), pairs)
     kv_peer = swap(kv_other)
     gain, kv_peer = lax.optimization_barrier((gain, kv_peer))
 
@@ -270,8 +288,10 @@
     )
     side = swap(grad_one, "x")
     from_peer = swap(to_peer)
-    attended, q_grad = small(
-        join_queries_kernel, [((ROWS, 4 * HEAD), bf16)] * 2, "join_queries", attended, q_grad, from_peer
+    attended, q_grad, gains = small(
+        join_queries_kernel,
+        [((ROWS, 4 * HEAD), bf16)] * 2 + [((1, wide), f32)],
+        "join_queries", attended, q_grad, from_peer, gains,
     )
     gains, attended, q_grad = lax.optimization_barrier((gains, attended, q_grad))
     lines = lax.axis_size("y") * lax.axis_size("z")
@@ -282,7 +302,7 @@
     (onward,) = small(onward_kernel, [((2, ROWS, wide), bf16)], "onward", grad_two, side)
     gathered, onward = lax.optimization_barrier((gathered, onward))
     ahead = hop(onward, -2)
-    gains = lax.psum(jnp.sum(gathered, axis=0, keepdims=True), ("dp", "x", "core"))
+    gains = lax.psum(jnp.sum(gathered, axis=0, keepdims=True), ("dp", "x"))
     gains, ahead = lax.optimization_barrier((gains, ahead))
     kv_grad, kv_grad_peer = small(
         finish_kernel,

time: 97.1 us -> 99.1 us (1.021)
  waiting for transfers between devices: 7.87 us -> 13.3 us
  blocking collectives: 40.8 us -> 36 us
  starting transfers between devices: 33.4 us -> 34.9 us
    psum x1, blocking collectives: 13.8 us -> 7.89 us  [per_device(): gains = lax.psum(jnp.sum(gathered, axis=0, keepdims=True), ('dp', 'x'))]
    ppermute x3, waiting for transfers between devices: 0.01 us -> 4.02 us  [hop(): lax.ppermute(array, SEQ, [(i, j) for i, j in pairs if 0 <= j < shards])]
    ppermute x3, starting transfers between devices: 8.13 us -> 10.8 us  [hop(): lax.ppermute(array, SEQ, [(i, j) for i, j in pairs if 0 <= j < shards])]
    ppermute x1, starting transfers between devices: 3.15 us -> 1.92 us  [per_device(): kv_one_x = lax.ppermute(relayed, ('x', 'core'), pairs)]
    all_to_all x1, blocking collectives: 27 us -> 28.2 us  [per_device(): lax.all_to_all(jnp.broadcast_to(gains, (lines, wide)), ('y', 'z'), 0, 0,...]
    ppermute x1, waiting for transfers between devices: 0.01 us -> 1.11 us  [per_device(): kv_one_x = lax.ppermute(relayed, ('x', 'core'), pairs)]
  transfers between devices with their start and end apart: 11 -> 11, of which waited for: 3 -> 5; matrix products, arithmetic and copies ran while one was open for 0% -> 0% of each run, Pallas kernels for 1% -> 1%
where the time goes in v9:
time: 99.1 us; the launch traced here: 98.7 us
  blocking collectives  36 us (36%)
  starting transfers between devices  34.9 us (35%)
  waiting for transfers between devices  13.3 us (13%)
  Pallas kernels  11.4 us (12%)
  other arithmetic  1.37 us (1%)
    all_to_all x1, blocking collectives, per_device(): lax.all_to_all(jnp.broadcast_to(gains, (lines, wide)), ('y', 'z'), 0, 0,...  28.2 us
    ppermute x7, starting transfers between devices, swap(): return lax.ppermute(array, axis, [(0, 1), (1, 0)])  22.1 us
    ppermute x3, starting transfers between devices, hop(): lax.ppermute(array, SEQ, [(i, j) for i, j in pairs if 0 <= j < shards])  10.8 us
    pallas_call x1, Pallas kernels, attention(): pl.pallas_call(attention_kernel, out_shape=(shape((ROWS, 2 * HEAD), bf16)...  8.84 us
    ppermute x7, waiting for transfers between devices, swap(): return lax.ppermute(array, axis, [(0, 1), (1, 0)])  8.2 us
    psum x1, blocking collectives, per_device(): gains = lax.psum(jnp.sum(gathered, axis=0, keepdims=True), ('dp', 'x'))  7.89 us
    ppermute x3, waiting for transfers between devices, hop(): lax.ppermute(array, SEQ, [(i, j) for i, j in pairs if 0 <= j < shards])  4.02 us
    pallas_call x4, Pallas kernels, small(): pl.pallas_call(kernel, out_shape=tuple((jax.ShapeDtypeStruct(*out) for ou...  2.54 us
  transfers between devices with their start and end apart: 11, of which 5 were waited for; matrix products, arithmetic and copies ran while one was open for 0% of the time, Pallas kernels for 1%

profile of v9, /device:TPU:1, one launch (start us, length us, event | category | flops | bytes accessed | tf_op | source)
XLA Modules:
  0.0 98.7 jit_solution(13069674163622229481)
XLA Ops:
  0.6 0.0 copy-start.2
  0.7 0.7 copy-done.2
  1.3 1.1 %broadcast_select_fusion.6 = (bf16[256,256]{1,0:T(8,128)(2,1)S(1)}, bf16[256,256]{1,0:T(8,128)(2,1)S(1)}, bf16[256,256]{1,0:T(8,128)(2,1)S(1)}, bf16[256,256]{1,0:T(8,128)(2,1)S(1)}) fusion(pred[]{:T(512)S(6)} %not.3, bf16[256,512]{1,0:T(8,128)(2,1)} %bitcast.22, pred[]{:T(512)S(6)} %eq.6, bf16[256,512]{1,0:T(8,128)(2,1)} %bitcast.23), kind=kLoop, calls=%fused_computation.11 | loop fusion | flops 262144 | bytes 1048578 | tf_op jit(solution)/shard_map/jit(_where)/select_n | solution.py:262
  2.5 0.0 copy-start
  2.5 5.5 %collective-permute-start = (bf16[272,512]{1,0:T(8,128)(2,1)S(1)}, bf16[272,512]{1,0:T(8,128)(2,1)S(1)}, u32[]{:S(2)}, u32[]{:S(2)}) collective-permute-start(bf16[272,512]{1,0:T(8,128)(2,1)S(1)} %get-tuple-element.40), channel_id=1, source_target_pairs={{0,5},{1,4},{2,7},{3,6},{4,9},{5,8},{6,11},{7,10},{8,13},{9,12},{1... | collective-permute-start | bytes 835592 | tf_op jit(solution)/shard_map/ppermute | solution.py:250
  8.1 4.0 %collective-permute-start.4 = (bf16[272,512]{1,0:T(8,128)(2,1)S(1)}, bf16[272,512]{1,0:T(8,128)(2,1)S(1)}, u32[]{:S(2)}, u32[]{:S(2)}) collective-permute-start(bf16[272,512]{1,0:T(8,128)(2,1)S(1)} %get-tuple-element.42.kv_own), channel_id=1, source_target_pairs={{0,4},{1,5},{2,6},{3,7},{4,8},{5,9},{6,10},{7,11},{8,12},{9,13},{1... | collective-permute-start | bytes 835592 | tf_op jit(solution)/shard_map/ppermute | solution.py:250
  12.1 0.0 copy-done
  12.1 2.0 %collective-permute-start.2 = (bf16[256,512]{1,0:T(8,128)(2,1)S(1)}, bf16[256,512]{1,0:T(8,128)(2,1)S(1)}, u32[]{:S(2)}, u32[]{:S(2)}) collective-permute-start(bf16[256,512]{1,0:T(8,128)(2,1)S(1)} %get-tuple-element.72), channel_id=1, source_target_pairs={{0,1},{1,0},{2,3},{3,2},{4,5},{5,4},{6,7},{7,6},{8,9},{9,8},{10,11... | collective-permute-start | bytes 786440 | tf_op jit(solution)/shard_map/ppermute | solution.py:253
  14.2 0.0 collective-permute-done.kv_two_x
  14.2 0.0 copy-start.1
  14.2 4.7 %collective-permute-start.1 = (bf16[272,512]{1,0:T(8,128)(2,1)S(1)}, bf16[272,512]{1,0:T(8,128)(2,1)S(1)}, u32[]{:S(2)}, u32[]{:S(2)}) collective-permute-start(bf16[272,512]{1,0:T(8,128)(2,1)S(1)} %get-tuple-element.40), channel_id=1, source_target_pairs={{0,1},{1,0},{2,3},{3,2},{4,5},{5,4},{6,7},{7,6},{8,9},{9,8},{10,11... | collective-permute-start | bytes 835592 | tf_op jit(solution)/shard_map/ppermute | solution.py:253
  18.9 1.9 %collective-permute-start.6 = (bf16[272,512]{1,0:T(8,128)(2,1)S(1)}, bf16[272,512]{1,0:T(8,128)(2,1)S(1)}, u32[]{:S(2)}, u32[]{:S(2)}) collective-permute-start(bf16[272,512]{1,0:T(8,128)(2,1)S(1)} %broadcast_select_fusion.1), channel_id=1, source_target_pairs={{0,3},{1,2},{2,0},{3,1},{4,7},{5,6},{6,4},{7,5},{8,11},{9,10},{10,... | collective-permute-start | bytes 835592 | tf_op jit(solution)/shard_map/ppermute | solution.py:277
  20.9 0.0 collective-permute-done.4.kv_two
  20.9 3.4 %collective-permute-start.5 = (bf16[272,512]{1,0:T(8,128)(2,1)S(1)}, bf16[272,512]{1,0:T(8,128)(2,1)S(1)}, u32[]{:S(2)}, u32[]{:S(2)}) collective-permute-start(bf16[272,512]{1,0:T(8,128)(2,1)S(1)} %broadcast_select_fusion), channel_id=1, source_target_pairs={{0,2},{2,0},{1,3},{3,1},{4,6},{6,4},{5,7},{7,5},{8,10},{10,8},{9,1... | collective-permute-start | bytes 835592 | tf_op jit(solution)/shard_map/ppermute | solution.py:253
  24.3 0.0 copy-done.1
  24.3 0.0 copy-start.4
  24.4 0.0 copy-start.3
  24.4 2.5 %collective-permute-start.3 = (bf16[256,512]{1,0:T(8,128)(2,1)S(1)}, bf16[256,512]{1,0:T(8,128)(2,1)S(1)}, u32[]{:S(2)}, u32[]{:S(2)}) collective-permute-start(bf16[256,512]{1,0:T(8,128)(2,1)S(1)} %get-tuple-element.70), channel_id=1, source_target_pairs={{0,1},{1,0},{2,3},{3,2},{4,5},{5,4},{6,7},{7,6},{8,9},{9,8},{10,11... | collective-permute-start | bytes 786440 | tf_op jit(solution)/shard_map/ppermute | solution.py:253
  26.9 0.0 copy-done.4
  26.9 0.0 copy-done.3
  26.9 0.0 collective-permute-done.1.kv_peer
  26.9 0.0 collective-permute-done.2.q_peer
  26.9 1.1 %collective-permute-done.3.g_peer = bf16[256,512]{1,0:T(8,128)(2,1)S(1)} collective-permute-done((bf16[256,512]{1,0:T(8,128)(2,1)S(1)}, bf16[256,512]{1,0:T(8,128)(2,1)S(1)}, u32[]{:S(2)}, u32[]{:S(2)}) %collective-permute-start.3) | collective-permute-done | bytes 262176 | tf_op jit(solution)/shard_map/ppermute | solution.py:253
  28.0 1.1 %collective-permute-done.6.kv_one_x = bf16[272,512]{1,0:T(8,128)(2,1)S(1)} collective-permute-done((bf16[272,512]{1,0:T(8,128)(2,1)S(1)}, bf16[272,512]{1,0:T(8,128)(2,1)S(1)}, u32[]{:S(2)}, u32[]{:S(2)}) %collective-permute-start.6) | collective-permute-done | bytes 278560 | tf_op jit(solution)/shard_map/ppermute | solution.py:277
  29.1 6.0 %collective-permute-done.5.kv_one = bf16[272,512]{1,0:T(8,128)(2,1)S(1)} collective-permute-done((bf16[272,512]{1,0:T(8,128)(2,1)S(1)}, bf16[272,512]{1,0:T(8,128)(2,1)S(1)}, u32[]{:S(2)}, u32[]{:S(2)}) %collective-permute-start.5) | collective-permute-done | bytes 278560 | tf_op jit(solution)/shard_map/ppermute | solution.py:253
  35.1 8.8 %attention.1 = (bf16[256,512]{1,0:T(8,128)(2,1)S(1)}, bf16[256,512]{1,0:T(8,128)(2,1)S(1)}, bf16[272,1024]{1,0:T(8,128)(2,1)S(1)}, f32[2,256,512]{2,1,0:T(8,128)...) custom-call(f32[1,512]{1,0:T(1,128)S(1)} %bitcast.16, ...), custom_call_target="tpu_custom_call" | custom-call | flops 8589934592 | bytes 8388608 | tf_op jit(solution)/shard_map/attention/pallas_call | solution.py:196
  43.9 2.7 %collective-permute-start.7 = (bf16[272,1024]{1,0:T(8,128)(2,1)S(1)}, bf16[272,1024]{1,0:T(8,128)(2,1)S(1)}, u32[]{:S(2)}, u32[]{:S(2)}) collective-permute-start(bf16[272,1024]{1,0:T(8,128)(2,1)S(1)} %get-tuple-element.47), channel_id=1, source_target_pairs={{0,1},{1,0},{2,3},{3,2},{4,5},{5,4},{6,7},{7,6},{8,9},{9,8},{10,11... | collective-permute-start | bytes 1671176 | tf_op jit(solution)/shard_map/ppermute | solution.py:253
  46.6 1.9 %collective-permute-start.8 = (bf16[2,256,512]{2,1,0:T(8,128)(2,1)S(1)}, bf16[2,256,512]{2,1,0:T(8,128)(2,1)S(1)}, u32[]{:S(2)}, u32[]{:S(2)}) collective-permute-start(bf16[2,256,512]{2,1,0:T(8,128)(2,1)S(1)} %get-tuple-element.56), channel_id=1, source_target_pairs={{0,2},{2,0},{1,3},{3,1},{4,6},{6,4},{5,7},{7,5},{8,10},{10,8},{9,1... | collective-permute-start | bytes 1572872 | tf_op jit(solution)/shard_map/ppermute | solution.py:253
  48.6 0.0 collective-permute-done.7.from_peer
  48.6 1.1 %join_queries.1 = (bf16[256,1024]{1,0:T(8,128)(2,1)}, bf16[256,1024]{1,0:T(8,128)(2,1)}, f32[1,512]{1,0:T(1,128)S(1)}) custom-call(bf16[256,512]{1,0:T(8,128)(2,1)S(1)} %get-tuple-element.45.att_mine, bf16[256,512]{1,0:T(8,128)(2,1)S(1)} %get-tuple-element.46.grad_mine, bf16[272,1024]{1,0:T(8,128)(2,1)S(1)} %collective-permute-done.7.from_peer, ...), custom_call_target="tpu_custom_call" | custom-call | tf_op jit(solution)/shard_map/join_queries/pallas_call | solution.py:230
  49.7 0.1 broadcast_in_dim.27
  49.7 28.2 %all_to_all.9 = f32[64,1,512]{2,1,0:T(1,128)S(1)} all-to-all(f32[64,1,512]{2,1,0:T(1,128)S(1)} %broadcast_in_dim.27), channel_id=1, replica_groups=mesh['dp'=2,'y'=8,'z'=8,'x'=2,'core'=2] {'y','z'}, dimensions={0} | all-to-all | bytes 262144 | tf_op jit(solution)/shard_map/all_to_all | solution.py:298
  77.9 0.0 collective-permute-done.8.side
  77.9 0.2 onward.1
  78.1 1.3 %collective-permute-start.9 = (bf16[2,256,512]{2,1,0:T(8,128)(2,1)S(1)}, bf16[2,256,512]{2,1,0:T(8,128)(2,1)S(1)}, u32[]{:S(2)}, u32[]{:S(2)}) collective-permute-start(bf16[2,256,512]{2,1,0:T(8,128)(2,1)S(1)} %onward.1), channel_id=1, source_target_pairs={{4,0},{5,1},{6,2},{7,3},{8,4},{9,5},{10,6},{11,7},{12,8},{13,9},{1... | collective-permute-start | bytes 1572872 | tf_op jit(solution)/shard_map/ppermute | solution.py:250
  79.4 7.9 %psum.7.gains = f32[1,512]{1,0:T(1,128)S(1)} all-reduce(f32[1,512]{1,0:T(1,128)S(1)} %bitcast.24), channel_id=1, replica_groups=mesh['dp'=2,'y'=8,'z'=8,'x'=2,'core'=2] {'dp','x'}, use_global_device_ids=true, to_apply=%region_1.2 | all-reduce | flops 512 | bytes 4096 | tf_op jit(solution)/shard_map/psum | solution.py:305
  87.3 4.0 %collective-permute-done.9.ahead = bf16[2,256,512]{2,1,0:T(8,128)(2,1)S(1)} collective-permute-done((bf16[2,256,512]{2,1,0:T(8,128)(2,1)S(1)}, bf16[2,256,512]{2,1,0:T(8,128)(2,1)S(1)}, u32[]{:S(2)}, u32[]{:S(2)}) %collective-permute-start.9) | collective-permute-done | bytes 524320 | tf_op jit(solution)/shard_map/ppermute | solution.py:250
  91.3 0.4 finish.1
  91.7 4.9 %collective-permute-start.10 = (bf16[256,512]{1,0:T(8,128)(2,1)S(1)}, bf16[256,512]{1,0:T(8,128)(2,1)S(1)}, u32[]{:S(2)}, u32[]{:S(2)}) collective-permute-start(bf16[256,512]{1,0:T(8,128)(2,1)S(1)} %get-tuple-element.64), channel_id=1, source_target_pairs={{0,1},{1,0},{2,3},{3,2},{4,5},{5,4},{6,7},{7,6},{8,9},{9,8},{10,11... | collective-permute-start | bytes 786440 | tf_op jit(solution)/shard_map/ppermute | solution.py:253
  96.7 1.1 %collective-permute-done.10.other = bf16[256,512]{1,0:T(8,128)(2,1)S(1)} collective-permute-done((bf16[256,512]{1,0:T(8,128)(2,1)S(1)}, bf16[256,512]{1,0:T(8,128)(2,1)S(1)}, u32[]{:S(2)}, u32[]{:S(2)}) %collective-permute-start.10) | collective-permute-done | bytes 262176 | tf_op jit(solution)/shard_map/ppermute | solution.py:253
  97.8 0.9 join_keys.1
  (9 shorter events, 0.2 us)
Async XLA Ops:
  0.6 0.7 copy-start.2
  2.5 9.6 %copy-start = (bf16[1,256,1024]{2,1,0:T(8,128)(2,1)S(1)}, bf16[1,256,1024]{2,1,0:T(8,128)(2,1)}, u32[]{:S(2)}) copy-start(bf16[1,256,1024]{2,1,0:T(8,128)(2,1)} %param.7) | copy-start | bytes 1572868
  2.5 11.6 %collective-permute-start = (bf16[272,512]{1,0:T(8,128)(2,1)S(1)}, bf16[272,512]{1,0:T(8,128)(2,1)S(1)}, u32[]{:S(2)}, u32[]{:S(2)}) collective-permute-start(bf16[272,512]{1,0:T(8,128)(2,1)S(1)} %get-tuple-element.40), channel_id=1, source_target_pairs={{0,5},{1,4},{2,7},{3,6},{4,9},{5,8},{6,11},{7,10},{8,13},{9,12},{1... | collective-permute-start | bytes 835592 | tf_op jit(solution)/shard_map/ppermute | solution.py:250
  8.1 12.8 %collective-permute-start.4 = (bf16[272,512]{1,0:T(8,128)(2,1)S(1)}, bf16[272,512]{1,0:T(8,128)(2,1)S(1)}, u32[]{:S(2)}, u32[]{:S(2)}) collective-permute-start(bf16[272,512]{1,0:T(8,128)(2,1)S(1)} %get-tuple-element.42.kv_own), channel_id=1, source_target_pairs={{0,4},{1,5},{2,6},{3,7},{4,8},{5,9},{6,10},{7,11},{8,12},{9,13},{1... | collective-permute-start | bytes 835592 | tf_op jit(solution)/shard_map/ppermute | solution.py:250
  12.1 14.8 %collective-permute-start.2 = (bf16[256,512]{1,0:T(8,128)(2,1)S(1)}, bf16[256,512]{1,0:T(8,128)(2,1)S(1)}, u32[]{:S(2)}, u32[]{:S(2)}) collective-permute-start(bf16[256,512]{1,0:T(8,128)(2,1)S(1)} %get-tuple-element.72), channel_id=1, source_target_pairs={{0,1},{1,0},{2,3},{3,2},{4,5},{5,4},{6,7},{7,6},{8,9},{9,8},{10,11... | collective-permute-start | bytes 786440 | tf_op jit(solution)/shard_map/ppermute | solution.py:253
  14.2 10.1 %copy-start.1 = (bf16[1,256,1024]{2,1,0:T(8,128)(2,1)S(1)}, bf16[1,256,1024]{2,1,0:T(8,128)(2,1)}, u32[]{:S(2)}) copy-start(bf16[1,256,1024]{2,1,0:T(8,128)(2,1)} %param.10) | copy-start | bytes 1572868
  14.2 12.7 %collective-permute-start.1 = (bf16[272,512]{1,0:T(8,128)(2,1)S(1)}, bf16[272,512]{1,0:T(8,128)(2,1)S(1)}, u32[]{:S(2)}, u32[]{:S(2)}) collective-permute-start(bf16[272,512]{1,0:T(8,128)(2,1)S(1)} %get-tuple-element.40), channel_id=1, source_target_pairs={{0,1},{1,0},{2,3},{3,2},{4,5},{5,4},{6,7},{7,6},{8,9},{9,8},{10,11... | collective-permute-start | bytes 835592 | tf_op jit(solution)/shard_map/ppermute | solution.py:253
  18.9 10.2 %collective-permute-start.6 = (bf16[272,512]{1,0:T(8,128)(2,1)S(1)}, bf16[272,512]{1,0:T(8,128)(2,1)S(1)}, u32[]{:S(2)}, u32[]{:S(2)}) collective-permute-start(bf16[272,512]{1,0:T(8,128)(2,1)S(1)} %broadcast_select_fusion.1), channel_id=1, source_target_pairs={{0,3},{1,2},{2,0},{3,1},{4,7},{5,6},{6,4},{7,5},{8,11},{9,10},{10,... | collective-permute-start | bytes 835592 | tf_op jit(solution)/shard_map/ppermute | solution.py:277
  20.9 14.2 %collective-permute-start.5 = (bf16[272,512]{1,0:T(8,128)(2,1)S(1)}, bf16[272,512]{1,0:T(8,128)(2,1)S(1)}, u32[]{:S(2)}, u32[]{:S(2)}) collective-permute-start(bf16[272,512]{1,0:T(8,128)(2,1)S(1)} %broadcast_select_fusion), channel_id=1, source_target_pairs={{0,2},{2,0},{1,3},{3,1},{4,6},{6,4},{5,7},{7,5},{8,10},{10,8},{9,1... | collective-permute-start | bytes 835592 | tf_op jit(solution)/shard_map/ppermute | solution.py:253
  24.3 2.6 %copy-start.4 = (f32[256]{0:T(256)S(1)}, f32[256]{0:T(256)}, u32[]{:S(2)}) copy-start(f32[256]{0:T(256)} %param.11) | copy-start | bytes 3076
  24.4 2.5 %copy-start.3 = (f32[256]{0:T(256)S(1)}, f32[256]{0:T(256)}, u32[]{:S(2)}) copy-start(f32[256]{0:T(256)} %param.12) | copy-start | bytes 3076
  24.4 3.6 %collective-permute-start.3 = (bf16[256,512]{1,0:T(8,128)(2,1)S(1)}, bf16[256,512]{1,0:T(8,128)(2,1)S(1)}, u32[]{:S(2)}, u32[]{:S(2)}) collective-permute-start(bf16[256,512]{1,0:T(8,128)(2,1)S(1)} %get-tuple-element.70), channel_id=1, source_target_pairs={{0,1},{1,0},{2,3},{3,2},{4,5},{5,4},{6,7},{7,6},{8,9},{9,8},{10,11... | collective-permute-start | bytes 786440 | tf_op jit(solution)/shard_map/ppermute | solution.py:253
  43.9 4.6 %collective-permute-start.7 = (bf16[272,1024]{1,0:T(8,128)(2,1)S(1)}, bf16[272,1024]{1,0:T(8,128)(2,1)S(1)}, u32[]{:S(2)}, u32[]{:S(2)}) collective-permute-start(bf16[272,1024]{1,0:T(8,128)(2,1)S(1)} %get-tuple-element.47), channel_id=1, source_target_pairs={{0,1},{1,0},{2,3},{3,2},{4,5},{5,4},{6,7},{7,6},{8,9},{9,8},{10,11... | collective-permute-start | bytes 1671176 | tf_op jit(solution)/shard_map/ppermute | solution.py:253
  46.6 31.3 %collective-permute-start.8 = (bf16[2,256,512]{2,1,0:T(8,128)(2,1)S(1)}, bf16[2,256,512]{2,1,0:T(8,128)(2,1)S(1)}, u32[]{:S(2)}, u32[]{:S(2)}) collective-permute-start(bf16[2,256,512]{2,1,0:T(8,128)(2,1)S(1)} %get-tuple-element.56), channel_id=1, source_target_pairs={{0,2},{2,0},{1,3},{3,1},{4,6},{6,4},{5,7},{7,5},{8,10},{10,8},{9,1... | collective-permute-start | bytes 1572872 | tf_op jit(solution)/shard_map/ppermute | solution.py:253
  78.1 13.2 %collective-permute-start.9 = (bf16[2,256,512]{2,1,0:T(8,128)(2,1)S(1)}, bf16[2,256,512]{2,1,0:T(8,128)(2,1)S(1)}, u32[]{:S(2)}, u32[]{:S(2)}) collective-permute-start(bf16[2,256,512]{2,1,0:T(8,128)(2,1)S(1)} %onward.1), channel_id=1, source_target_pairs={{4,0},{5,1},{6,2},{7,3},{8,4},{9,5},{10,6},{11,7},{12,8},{13,9},{1... | collective-permute-start | bytes 1572872 | tf_op jit(solution)/shard_map/ppermute | solution.py:250
  91.7 6.1 %collective-permute-start.10 = (bf16[256,512]{1,0:T(8,128)(2,1)S(1)}, bf16[256,512]{1,0:T(8,128)(2,1)S(1)}, u32[]{:S(2)}, u32[]{:S(2)}) collective-permute-start(bf16[256,512]{1,0:T(8,128)(2,1)S(1)} %get-tuple-element.64), channel_id=1, source_target_pairs={{0,1},{1,0},{2,3},{3,2},{4,5},{5,4},{6,7},{7,6},{8,9},{9,8},{10,11... | collective-permute-start | bytes 786440 | tf_op jit(solution)/shard_map/ppermute | solution.py:253

commit v10 on v7

--- a/solution.py
+++ b/solution.py
@@ -269,20 +269,20 @@
         gain, q_mine, g_mine, q_peer, g_peer, kv_mine, kv_peer, kv_one, kv_one_x, kv_two, kv_two_x
     )
     side = swap(grad_one, "x")
-    from_peer = swap(to_peer)
     lines = lax.axis_size("y") * lax.axis_size("z")
     gathered = lax.all_to_all(
         jnp.broadcast_to(gains, (lines, wide)), ("y", "z"), 0, 0, tiled=True
     )
     gathered, side = lax.optimization_barrier((gathered, side))
     (onward,) = small(onward_kernel, [((2, ROWS, wide), bf16)], "onward", grad_two, side)
-    gathered, onward = lax.optimization_barrier((gathered, onward))
+    gathered, onward, to_peer = lax.optimization_barrier((gathered, onward, to_peer))
     ahead = hop(onward, -2)
-    gains = lax.psum(jnp.sum(gathered, axis=0, keepdims=True), ("dp", "x", "core"))
+    from_peer = swap(to_peer)
     attended, q_grad = small(
         join_queries_kernel, [((ROWS, 4 * HEAD), bf16)] * 2, "join_queries", attended, q_grad, from_peer
     )
-    gains, ahead, attended, q_grad = lax.optimization_barrier((gains, ahead, attended, q_grad))
+    gains = lax.psum(jnp.sum(gathered, axis=0, keepdims=True), ("dp", "x", "core"))
+    gains, ahead = lax.optimization_barrier((gains, ahead))
     kv_grad, kv_grad_peer = small(
         finish_kernel,
         [((ROWS, wide), bf16)] * 2,

time: 103 us -> 101 us (0.981)
  blocking collectives: 14.3 us -> 38.9 us
  starting transfers between devices: 49.5 us -> 36.5 us
  waiting for transfers between devices: 15.8 us -> 6.73 us
  local copies, waits for them, and re-layouts: 7.25 us -> 2.39 us
    all_to_all x0 -> x1, blocking collectives: none -> 27.1 us  [per_device(): lax.all_to_all(jnp.broadcast_to(gains, (lines, wide)), ('y', 'z'), 0, 0,...]
    all_to_all x1 -> x0, starting transfers between devices: 16.1 us -> none  [per_device(): lax.all_to_all(jnp.broadcast_to(gains, (lines, wide)), ('y', 'z'), 0, 0,...]
    all_to_all x1 -> x0, waiting for transfers between devices: 7.98 us -> none  [per_device(): lax.all_to_all(jnp.broadcast_to(gains, (lines, wide)), ('y', 'z'), 0, 0,...]
    unnamed x23, local copies, waits for them, and re-layouts: 6.52 us -> 2.32 us
    ppermute x7, starting transfers between devices: 22.2 us -> 25.2 us  [swap(): return lax.ppermute(array, axis, [(0, 1), (1, 0)])]
    psum x1, blocking collectives: 14.3 us -> 11.8 us  [per_device(): lax.psum(jnp.sum(gathered, axis=0, keepdims=True), ('dp', 'x', 'core'))]
    ppermute x7, waiting for transfers between devices: 7.85 us -> 6.72 us  [swap(): return lax.ppermute(array, axis, [(0, 1), (1, 0)])]
  transfers between devices with their start and end apart: 12 -> 11, of which waited for: 4 -> 2; matrix products, arithmetic and copies ran while one was open for 3% -> 2% of each run, Pallas kernels for 1% -> 2%
where the time goes in v10:
time: 101 us; the launch traced here: 100 us
  blocking collectives  38.9 us (39%)
  starting transfers between devices  36.5 us (36%)
  Pallas kernels  12.4 us (12%)
  waiting for transfers between devices  6.73 us (7%)
  local copies, waits for them, and re-layouts  2.39 us (2%)
  other arithmetic  2.27 us (2%)
    all_to_all x1, blocking collectives, per_device(): lax.all_to_all(jnp.broadcast_to(gains, (lines, wide)), ('y', 'z'), 0, 0,...  27.1 us
    ppermute x7, starting transfers between devices, swap(): return lax.ppermute(array, axis, [(0, 1), (1, 0)])  25.2 us
    psum x1, blocking collectives, per_device(): lax.psum(jnp.sum(gathered, axis=0, keepdims=True), ('dp', 'x', 'core'))  11.8 us
    pallas_call x1, Pallas kernels, attention(): pl.pallas_call(attention_kernel, out_shape=(shape((ROWS, 2 * HEAD), bf16)...  9.88 us
    ppermute x3, starting transfers between devices, hop(): lax.ppermute(array, SEQ, [(i, j) for i, j in pairs if 0 <= j < shards])  8.13 us
    ppermute x7, waiting for transfers between devices, swap(): return lax.ppermute(array, axis, [(0, 1), (1, 0)])  6.72 us
    ppermute x1, starting transfers between devices, per_device(): lax.ppermute(jnp.where(lead, kv_other, kv_two_x), ('x', 'core'), pairs)  3.15 us
    pallas_call x4, Pallas kernels, small(): pl.pallas_call(kernel, out_shape=tuple((jax.ShapeDtypeStruct(*out) for ou...  2.55 us
  transfers between devices with their start and end apart: 11, of which 2 were waited for; matrix products, arithmetic and copies ran while one was open for 2% of the time, Pallas kernels for 2%

profile of v10, /device:TPU:1, one launch (start us, length us, event | category | flops | bytes accessed | tf_op | source)
XLA Modules:
  0.0 100.2 jit_solution(15142192715821414729)
XLA Ops:
  0.6 0.0 copy-start.8
  0.7 0.7 copy-done.8
  1.3 1.1 %broadcast_select_fusion.6 = (bf16[256,256]{1,0:T(8,128)(2,1)S(1)}, bf16[256,256]{1,0:T(8,128)(2,1)S(1)}, bf16[256,256]{1,0:T(8,128)(2,1)S(1)}, bf16[256,256]{1,0:T(8,128)(2,1)S(1)}) fusion(pred[]{:T(512)S(6)} %not.3, bf16[256,512]{1,0:T(8,128)(2,1)} %bitcast.22, pred[]{:T(512)S(6)} %eq.6, bf16[256,512]{1,0:T(8,128)(2,1)} %bitcast.23), kind=kLoop, calls=%fused_computation.11 | loop fusion | flops 262144 | bytes 1048578 | tf_op jit(solution)/shard_map/jit(_where)/select_n | solution.py:245
  2.5 0.0 copy-start.6
  2.5 5.5 %collective-permute-start.5 = (bf16[272,512]{1,0:T(8,128)(2,1)S(1)}, bf16[272,512]{1,0:T(8,128)(2,1)S(1)}, u32[]{:S(2)}, u32[]{:S(2)}) collective-permute-start(bf16[272,512]{1,0:T(8,128)(2,1)S(1)} %get-tuple-element.33), channel_id=1, source_target_pairs={{0,5},{1,4},{2,7},{3,6},{4,9},{5,8},{6,11},{7,10},{8,13},{9,12},{1... | collective-permute-start | bytes 835592 | tf_op jit(solution)/shard_map/ppermute | solution.py:233
  8.1 4.7 %collective-permute-start = (bf16[272,512]{1,0:T(8,128)(2,1)S(1)}, bf16[272,512]{1,0:T(8,128)(2,1)S(1)}, u32[]{:S(2)}, u32[]{:S(2)}) collective-permute-start(bf16[272,512]{1,0:T(8,128)(2,1)S(1)} %get-tuple-element.33), channel_id=1, source_target_pairs={{0,1},{1,0},{2,3},{3,2},{4,5},{5,4},{6,7},{7,6},{8,9},{9,8},{10,11... | collective-permute-start | bytes 835592 | tf_op jit(solution)/shard_map/ppermute | solution.py:236
  12.8 1.3 %collective-permute-start.3 = (bf16[272,512]{1,0:T(8,128)(2,1)S(1)}, bf16[272,512]{1,0:T(8,128)(2,1)S(1)}, u32[]{:S(2)}, u32[]{:S(2)}) collective-permute-start(bf16[272,512]{1,0:T(8,128)(2,1)S(1)} %get-tuple-element.35.kv_own), channel_id=1, source_target_pairs={{0,4},{1,5},{2,6},{3,7},{4,8},{5,9},{6,10},{7,11},{8,12},{9,13},{1... | collective-permute-start | bytes 835592 | tf_op jit(solution)/shard_map/ppermute | solution.py:233
  14.1 0.0 copy-done.6
  14.1 2.6 %collective-permute-start.1 = (bf16[256,512]{1,0:T(8,128)(2,1)S(1)}, bf16[256,512]{1,0:T(8,128)(2,1)S(1)}, u32[]{:S(2)}, u32[]{:S(2)}) collective-permute-start(bf16[256,512]{1,0:T(8,128)(2,1)S(1)} %get-tuple-element.62), channel_id=1, source_target_pairs={{0,1},{1,0},{2,3},{3,2},{4,5},{5,4},{6,7},{7,6},{8,9},{9,8},{10,11... | collective-permute-start | bytes 786440 | tf_op jit(solution)/shard_map/ppermute | solution.py:236
  16.8 0.0 collective-permute-done.5.kv_two_x
  16.8 0.0 copy-start.7
  16.8 3.1 %collective-permute-start.6 = (bf16[272,512]{1,0:T(8,128)(2,1)S(1)}, bf16[272,512]{1,0:T(8,128)(2,1)S(1)}, u32[]{:S(2)}, u32[]{:S(2)}) collective-permute-start(bf16[272,512]{1,0:T(8,128)(2,1)S(1)} %broadcast_select_fusion), channel_id=1, source_target_pairs={{0,3},{1,2},{2,0},{3,1},{4,7},{5,6},{6,4},{7,5},{8,11},{9,10},{10,... | collective-permute-start | bytes 835592 | tf_op jit(solution)/shard_map/ppermute | solution.py:259
  20.0 0.0 collective-permute-done.3.kv_two
  20.0 2.6 %collective-permute-start.4 = (bf16[272,512]{1,0:T(8,128)(2,1)S(1)}, bf16[272,512]{1,0:T(8,128)(2,1)S(1)}, u32[]{:S(2)}, u32[]{:S(2)}) collective-permute-start(bf16[272,512]{1,0:T(8,128)(2,1)S(1)} %broadcast_select_fusion.1), channel_id=1, source_target_pairs={{0,2},{2,0},{1,3},{3,1},{4,6},{6,4},{5,7},{7,5},{8,10},{10,8},{9,1... | collective-permute-start | bytes 835592 | tf_op jit(solution)/shard_map/ppermute | solution.py:236
  22.7 0.0 copy-done.7
  22.7 0.0 copy-start.10
  22.7 0.0 copy-start.9
  22.7 3.6 %collective-permute-start.2 = (bf16[256,512]{1,0:T(8,128)(2,1)S(1)}, bf16[256,512]{1,0:T(8,128)(2,1)S(1)}, u32[]{:S(2)}, u32[]{:S(2)}) collective-permute-start(bf16[256,512]{1,0:T(8,128)(2,1)S(1)} %get-tuple-element.60), channel_id=1, source_target_pairs={{0,1},{1,0},{2,3},{3,2},{4,5},{5,4},{6,7},{7,6},{8,9},{9,8},{10,11... | collective-permute-start | bytes 786440 | tf_op jit(solution)/shard_map/ppermute | solution.py:236
  26.3 0.0 copy-done.10
  26.3 0.0 copy-done.9
  26.4 0.0 collective-permute-done.kv_peer
  26.4 0.0 copy-start
  26.4 0.0 collective-permute-done.1.q_peer
  26.4 1.1 %collective-permute-done.2.g_peer = bf16[256,512]{1,0:T(8,128)(2,1)S(1)} collective-permute-done((bf16[256,512]{1,0:T(8,128)(2,1)S(1)}, bf16[256,512]{1,0:T(8,128)(2,1)S(1)}, u32[]{:S(2)}, u32[]{:S(2)}) %collective-permute-start.2) | collective-permute-done | bytes 262176 | tf_op jit(solution)/shard_map/ppermute | solution.py:236
  27.5 0.0 collective-permute-done.6.kv_one_x
  27.5 5.6 %collective-permute-done.4.kv_one = bf16[272,512]{1,0:T(8,128)(2,1)S(1)} collective-permute-done((bf16[272,512]{1,0:T(8,128)(2,1)S(1)}, bf16[272,512]{1,0:T(8,128)(2,1)S(1)}, u32[]{:S(2)}, u32[]{:S(2)}) %collective-permute-start.4) | collective-permute-done | bytes 278560 | tf_op jit(solution)/shard_map/ppermute | solution.py:236
  33.1 9.9 %attention.1 = (bf16[256,512]{1,0:T(8,128)(2,1)S(1)}, bf16[256,512]{1,0:T(8,128)(2,1)S(1)}, bf16[256,1024]{1,0:T(8,128)(2,1)}, f32[2,256,512]{2,1,0:T(8,128)S(1)...) custom-call(f32[1,512]{1,0:T(1,128)S(1)} %bitcast.16, ...), custom_call_target="tpu_custom_call" | custom-call | flops 8589934592 | bytes 8388608 | tf_op jit(solution)/shard_map/attention/pallas_call | solution.py:179
  43.0 0.0 copy-done
  43.0 2.8 %collective-permute-start.7 = (bf16[2,256,512]{2,1,0:T(8,128)(2,1)S(1)}, bf16[2,256,512]{2,1,0:T(8,128)(2,1)S(1)}, u32[]{:S(2)}, u32[]{:S(2)}) collective-permute-start(bf16[2,256,512]{2,1,0:T(8,128)(2,1)S(1)} %get-tuple-element.41), channel_id=1, source_target_pairs={{0,2},{2,0},{1,3},{3,1},{4,6},{6,4},{5,7},{7,5},{8,10},{10,8},{9,1... | collective-permute-start | bytes 1572872 | tf_op jit(solution)/shard_map/ppermute | solution.py:236
  45.8 0.1 broadcast_in_dim.25
  45.8 27.1 %all_to_all.9 = f32[64,1,512]{2,1,0:T(1,128)S(1)} all-to-all(f32[64,1,512]{2,1,0:T(1,128)S(1)} %broadcast_in_dim.25), channel_id=1, replica_groups=mesh['dp'=2,'y'=8,'z'=8,'x'=2,'core'=2] {'y','z'}, dimensions={0} | all-to-all | bytes 262144 | tf_op jit(solution)/shard_map/all_to_all | solution.py:273
  72.9 0.7 copy.15
  73.6 0.0 copy-done.2
  73.6 0.0 copy-done.4
  73.6 0.0 collective-permute-done.7.side
  73.6 0.2 onward.1
  73.8 1.3 %collective-permute-start.9 = (bf16[2,256,512]{2,1,0:T(8,128)(2,1)S(1)}, bf16[2,256,512]{2,1,0:T(8,128)(2,1)S(1)}, u32[]{:S(2)}, u32[]{:S(2)}) collective-permute-start(bf16[2,256,512]{2,1,0:T(8,128)(2,1)S(1)} %onward.1), channel_id=1, source_target_pairs={{4,0},{5,1},{6,2},{7,3},{8,4},{9,5},{10,6},{11,7},{12,8},{13,9},{1... | collective-permute-start | bytes 1572872 | tf_op jit(solution)/shard_map/ppermute | solution.py:233
  75.1 4.5 %collective-permute-start.8 = (bf16[256,1024]{1,0:T(8,128)(2,1)}, bf16[256,1024]{1,0:T(8,128)(2,1)S(1)}, u32[]{:S(2)}, u32[]{:S(2)}) collective-permute-start(bf16[256,1024]{1,0:T(8,128)(2,1)} %get-tuple-element.46), channel_id=1, source_target_pairs={{0,1},{1,0},{2,3},{3,2},{4,5},{5,4},{6,7},{7,6},{8,9},{9,8},{10,11... | collective-permute-start | bytes 1572872 | tf_op jit(solution)/shard_map/ppermute | solution.py:236
  79.6 0.9 reduce_sum.9
  80.5 11.8 %psum.7.gains = f32[1,512]{1,0:T(1,128)S(1)} all-reduce(f32[1,512]{1,0:T(1,128)S(1)} %bitcast.24), channel_id=1, replica_groups=mesh['dp'=2,'y'=8,'z'=8,'x'=2,'core'=2] {'dp','x','core'}, use_global_device_ids=true, to_apply=%region_1.2 | all-reduce | flops 512 | bytes 4096 | tf_op jit(solution)/shard_map/psum | solution.py:284
  92.3 0.0 collective-permute-done.9.ahead
  92.3 1.0 copy-done.1
  93.2 0.4 finish.1
  93.7 4.5 %collective-permute-start.10 = (bf16[256,512]{1,0:T(8,128)(2,1)S(1)}, bf16[256,512]{1,0:T(8,128)(2,1)S(1)}, u32[]{:S(2)}, u32[]{:S(2)}) collective-permute-start(bf16[256,512]{1,0:T(8,128)(2,1)S(1)} %get-tuple-element.54), channel_id=1, source_target_pairs={{0,1},{1,0},{2,3},{3,2},{4,5},{5,4},{6,7},{7,6},{8,9},{9,8},{10,11... | collective-permute-start | bytes 786440 | tf_op jit(solution)/shard_map/ppermute | solution.py:236
  98.2 0.0 collective-permute-done.8.from_peer
  98.2 1.1 %join_queries.1 = (bf16[256,1024]{1,0:T(8,128)(2,1)}, bf16[256,1024]{1,0:T(8,128)(2,1)}) custom-call(bf16[256,512]{1,0:T(8,128)(2,1)S(1)} %copy-done.3, bf16[256,512]{1,0:T(8,128)(2,1)S(1)} %copy-done.5, bf16[256,1024]{1,0:T(8,128)(2,1)S(1)} %collective-permute-done.8.from_peer), custom_call_target="tpu_custom_call" | custom-call | tf_op jit(solution)/shard_map/join_queries/pallas_call | solution.py:213
  99.3 0.0 collective-permute-done.10.other
  99.3 0.9 join_keys.1
  (14 shorter events, 0.2 us)
Async XLA Ops:
  0.6 0.7 copy-start.8
  2.5 11.6 %copy-start.6 = (bf16[1,256,1024]{2,1,0:T(8,128)(2,1)S(1)}, bf16[1,256,1024]{2,1,0:T(8,128)(2,1)}, u32[]{:S(2)}) copy-start(bf16[1,256,1024]{2,1,0:T(8,128)(2,1)} %param.7) | copy-start | bytes 1572868
  2.5 14.2 %collective-permute-start.5 = (bf16[272,512]{1,0:T(8,128)(2,1)S(1)}, bf16[272,512]{1,0:T(8,128)(2,1)S(1)}, u32[]{:S(2)}, u32[]{:S(2)}) collective-permute-start(bf16[272,512]{1,0:T(8,128)(2,1)S(1)} %get-tuple-element.33), channel_id=1, source_target_pairs={{0,5},{1,4},{2,7},{3,6},{4,9},{5,8},{6,11},{7,10},{8,13},{9,12},{1... | collective-permute-start | bytes 835592 | tf_op jit(solution)/shard_map/ppermute | solution.py:233
  8.1 18.3 %collective-permute-start = (bf16[272,512]{1,0:T(8,128)(2,1)S(1)}, bf16[272,512]{1,0:T(8,128)(2,1)S(1)}, u32[]{:S(2)}, u32[]{:S(2)}) collective-permute-start(bf16[272,512]{1,0:T(8,128)(2,1)S(1)} %get-tuple-element.33), channel_id=1, source_target_pairs={{0,1},{1,0},{2,3},{3,2},{4,5},{5,4},{6,7},{7,6},{8,9},{9,8},{10,11... | collective-permute-start | bytes 835592 | tf_op jit(solution)/shard_map/ppermute | solution.py:236
  12.8 7.2 %collective-permute-start.3 = (bf16[272,512]{1,0:T(8,128)(2,1)S(1)}, bf16[272,512]{1,0:T(8,128)(2,1)S(1)}, u32[]{:S(2)}, u32[]{:S(2)}) collective-permute-start(bf16[272,512]{1,0:T(8,128)(2,1)S(1)} %get-tuple-element.35.kv_own), channel_id=1, source_target_pairs={{0,4},{1,5},{2,6},{3,7},{4,8},{5,9},{6,10},{7,11},{8,12},{9,13},{1... | collective-permute-start | bytes 835592 | tf_op jit(solution)/shard_map/ppermute | solution.py:233
  14.1 12.2 %collective-permute-start.1 = (bf16[256,512]{1,0:T(8,128)(2,1)S(1)}, bf16[256,512]{1,0:T(8,128)(2,1)S(1)}, u32[]{:S(2)}, u32[]{:S(2)}) collective-permute-start(bf16[256,512]{1,0:T(8,128)(2,1)S(1)} %get-tuple-element.62), channel_id=1, source_target_pairs={{0,1},{1,0},{2,3},{3,2},{4,5},{5,4},{6,7},{7,6},{8,9},{9,8},{10,11... | collective-permute-start | bytes 786440 | tf_op jit(solution)/shard_map/ppermute | solution.py:236
  16.8 5.9 %copy-start.7 = (bf16[1,256,1024]{2,1,0:T(8,128)(2,1)S(1)}, bf16[1,256,1024]{2,1,0:T(8,128)(2,1)}, u32[]{:S(2)}) copy-start(bf16[1,256,1024]{2,1,0:T(8,128)(2,1)} %param.10) | copy-start | bytes 1572868
  16.8 10.6 %collective-permute-start.6 = (bf16[272,512]{1,0:T(8,128)(2,1)S(1)}, bf16[272,512]{1,0:T(8,128)(2,1)S(1)}, u32[]{:S(2)}, u32[]{:S(2)}) collective-permute-start(bf16[272,512]{1,0:T(8,128)(2,1)S(1)} %broadcast_select_fusion), channel_id=1, source_target_pairs={{0,3},{1,2},{2,0},{3,1},{4,7},{5,6},{6,4},{7,5},{8,11},{9,10},{10,... | collective-permute-start | bytes 835592 | tf_op jit(solution)/shard_map/ppermute | solution.py:259
  20.0 13.1 %collective-permute-start.4 = (bf16[272,512]{1,0:T(8,128)(2,1)S(1)}, bf16[272,512]{1,0:T(8,128)(2,1)S(1)}, u32[]{:S(2)}, u32[]{:S(2)}) collective-permute-start(bf16[272,512]{1,0:T(8,128)(2,1)S(1)} %broadcast_select_fusion.1), channel_id=1, source_target_pairs={{0,2},{2,0},{1,3},{3,1},{4,6},{6,4},{5,7},{7,5},{8,10},{10,8},{9,1... | collective-permute-start | bytes 835592 | tf_op jit(solution)/shard_map/ppermute | solution.py:236
  22.7 3.7 %copy-start.10 = (f32[256]{0:T(256)S(1)}, f32[256]{0:T(256)}, u32[]{:S(2)}) copy-start(f32[256]{0:T(256)} %param.11) | copy-start | bytes 3076
  22.7 3.6 %copy-start.9 = (f32[256]{0:T(256)S(1)}, f32[256]{0:T(256)}, u32[]{:S(2)}) copy-start(f32[256]{0:T(256)} %param.12) | copy-start | bytes 3076
  22.7 4.7 %collective-permute-start.2 = (bf16[256,512]{1,0:T(8,128)(2,1)S(1)}, bf16[256,512]{1,0:T(8,128)(2,1)S(1)}, u32[]{:S(2)}, u32[]{:S(2)}) collective-permute-start(bf16[256,512]{1,0:T(8,128)(2,1)S(1)} %get-tuple-element.60), channel_id=1, source_target_pairs={{0,1},{1,0},{2,3},{3,2},{4,5},{5,4},{6,7},{7,6},{8,9},{9,8},{10,11... | collective-permute-start | bytes 786440 | tf_op jit(solution)/shard_map/ppermute | solution.py:236
  26.4 16.6 %copy-start = (bf16[272,512]{1,0:T(8,128)(2,1)}, bf16[272,512]{1,0:T(8,128)(2,1)S(1)}, u32[]{:S(2)}) copy-start(bf16[272,512]{1,0:T(8,128)(2,1)S(1)} %collective-permute-done.kv_peer) | copy-start | bytes 835588
  43.0 30.6 %copy-start.2 = (bf16[256,512]{1,0:T(8,128)(2,1)}, bf16[256,512]{1,0:T(8,128)(2,1)S(1)}, u32[]{:S(2)}) copy-start(bf16[256,512]{1,0:T(8,128)(2,1)S(1)} %get-tuple-element.38.att_mine) | copy-start | bytes 786436
  43.0 30.6 %copy-start.4 = (bf16[256,512]{1,0:T(8,128)(2,1)}, bf16[256,512]{1,0:T(8,128)(2,1)S(1)}, u32[]{:S(2)}) copy-start(bf16[256,512]{1,0:T(8,128)(2,1)S(1)} %get-tuple-element.39.grad_mine) | copy-start | bytes 786436
  43.0 30.6 %collective-permute-start.7 = (bf16[2,256,512]{2,1,0:T(8,128)(2,1)S(1)}, bf16[2,256,512]{2,1,0:T(8,128)(2,1)S(1)}, u32[]{:S(2)}, u32[]{:S(2)}) collective-permute-start(bf16[2,256,512]{2,1,0:T(8,128)(2,1)S(1)} %get-tuple-element.41), channel_id=1, source_target_pairs={{0,2},{2,0},{1,3},{3,1},{4,6},{6,4},{5,7},{7,5},{8,10},{10,8},{9,1... | collective-permute-start | bytes 1572872 | tf_op jit(solution)/shard_map/ppermute | solution.py:236
  73.8 18.5 %collective-permute-start.9 = (bf16[2,256,512]{2,1,0:T(8,128)(2,1)S(1)}, bf16[2,256,512]{2,1,0:T(8,128)(2,1)S(1)}, u32[]{:S(2)}, u32[]{:S(2)}) collective-permute-start(bf16[2,256,512]{2,1,0:T(8,128)(2,1)S(1)} %onward.1), channel_id=1, source_target_pairs={{4,0},{5,1},{6,2},{7,3},{8,4},{9,5},{10,6},{11,7},{12,8},{13,9},{1... | collective-permute-start | bytes 1572872 | tf_op jit(solution)/shard_map/ppermute | solution.py:233
  75.1 23.1 %collective-permute-start.8 = (bf16[256,1024]{1,0:T(8,128)(2,1)}, bf16[256,1024]{1,0:T(8,128)(2,1)S(1)}, u32[]{:S(2)}, u32[]{:S(2)}) collective-permute-start(bf16[256,1024]{1,0:T(8,128)(2,1)} %get-tuple-element.46), channel_id=1, source_target_pairs={{0,1},{1,0},{2,3},{3,2},{4,5},{5,4},{6,7},{7,6},{8,9},{9,8},{10,11... | collective-permute-start | bytes 1572872 | tf_op jit(solution)/shard_map/ppermute | solution.py:236
  92.3 1.0 copy-start.1
  93.2 4.9 %copy-start.3 = (bf16[256,512]{1,0:T(8,128)(2,1)S(1)}, bf16[256,512]{1,0:T(8,128)(2,1)}, u32[]{:S(2)}) copy-start(bf16[256,512]{1,0:T(8,128)(2,1)} %copy-done.2) | copy-start | bytes 786436
  93.2 4.9 %copy-start.5 = (bf16[256,512]{1,0:T(8,128)(2,1)S(1)}, bf16[256,512]{1,0:T(8,128)(2,1)}, u32[]{:S(2)}) copy-start(bf16[256,512]{1,0:T(8,128)(2,1)} %copy-done.4) | copy-start | bytes 786436
  93.7 5.6 %collective-permute-start.10 = (bf16[256,512]{1,0:T(8,128)(2,1)S(1)}, bf16[256,512]{1,0:T(8,128)(2,1)S(1)}, u32[]{:S(2)}, u32[]{:S(2)}) collective-permute-start(bf16[256,512]{1,0:T(8,128)(2,1)S(1)} %get-tuple-element.54), channel_id=1, source_target_pairs={{0,1},{1,0},{2,3},{3,2},{4,5},{5,4},{6,7},{7,6},{8,9},{9,8},{10,11... | collective-permute-start | bytes 786440 | tf_op jit(solution)/shard_map/ppermute | solution.py:236

commit v11 on v9

--- a/solution.py
+++ b/solution.py
@@ -273,8 +273,7 @@
     kv_two, kv_two_x = hop(kv_mine, 2), hop(kv_other, 2, True)
     kv_one = swap(jnp.where(lead, kv_mine, kv_two), "x")
     pairs = [(c, 2 + (1 - c)) for c in range(2)] + [(2 + c, c) for c in range(2)]
-    relayed, kv_other = lax.optimization_barrier((jnp.where(lead, kv_other, kv_two_x), kv_other))
-    kv_one_x = lax.ppermute(relayed, ("x", "core"), pairs)
+    kv_one_x = lax.ppermute(jnp.where(lead, kv_other, kv_two_x), ("x", "core"), pairs)
     kv_peer = swap(kv_other)
     gain, kv_peer = lax.optimization_barrier((gain, kv_peer))
 

time: 99.1 us -> 97.1 us (0.980)
  blocking collectives: 36 us -> 34.5 us
  waiting for transfers between devices: 13.3 us -> 12.2 us
    ppermute x3, starting transfers between devices: 10.8 us -> 8.13 us  [hop(): lax.ppermute(array, SEQ, [(i, j) for i, j in pairs if 0 <= j < shards])]
    ppermute x7, starting transfers between devices: 22.1 us -> 24.1 us  [swap(): return lax.ppermute(array, axis, [(0, 1), (1, 0)])]
    ppermute x1, starting transfers between devices: 1.92 us -> 3.15 us  [per_device(): lax.ppermute(jnp.where(lead, kv_other, kv_two_x), ('x', 'core'), pairs)]
    all_to_all x1, blocking collectives: 28.2 us -> 27 us  [per_device(): lax.all_to_all(jnp.broadcast_to(gains, (lines, wide)), ('y', 'z'), 0, 0,...]
    ppermute x1, waiting for transfers between devices: 1.11 us -> 0.01 us  [per_device(): lax.ppermute(jnp.where(lead, kv_other, kv_two_x), ('x', 'core'), pairs)]
  transfers between devices with their start and end apart: 11 -> 11, of which waited for: 5 -> 4; matrix products, arithmetic and copies ran while one was open for 0% -> 0% of each run, Pallas kernels for 1% -> 1%
where the time goes in v11:
time: 97.1 us; the launch traced here: 96.6 us
  starting transfers between devices  35.4 us (36%)
  blocking collectives  34.5 us (36%)
  waiting for transfers between devices  12.2 us (13%)
  Pallas kernels  11.4 us (12%)
  other arithmetic  1.37 us (1%)
    all_to_all x1, blocking collectives, per_device(): lax.all_to_all(jnp.broadcast_to(gains, (lines, wide)), ('y', 'z'), 0, 0,...  27 us
    ppermute x7, starting transfers between devices, swap(): return lax.ppermute(array, axis, [(0, 1), (1, 0)])  24.1 us
    pallas_call x1, Pallas kernels, attention(): pl.pallas_call(attention_kernel, out_shape=(shape((ROWS, 2 * HEAD), bf16)...  8.85 us
    ppermute x3, starting transfers between devices, hop(): lax.ppermute(array, SEQ, [(i, j) for i, j in pairs if 0 <= j < shards])  8.13 us
    ppermute x7, waiting for transfers between devices, swap(): return lax.ppermute(array, axis, [(0, 1), (1, 0)])  7.86 us
    psum x1, blocking collectives, per_device(): gains = lax.psum(jnp.sum(gathered, axis=0, keepdims=True), ('dp', 'x'))  7.53 us
    ppermute x3, waiting for transfers between devices, hop(): lax.ppermute(array, SEQ, [(i, j) for i, j in pairs if 0 <= j < shards])  4.37 us
    ppermute x1, starting transfers between devices, per_device(): lax.ppermute(jnp.where(lead, kv_other, kv_two_x), ('x', 'core'), pairs)  3.15 us
  transfers between devices with their start and end apart: 11, of which 4 were waited for; matrix products, arithmetic and copies ran while one was open for 0% of the time, Pallas kernels for 1%

profile of v11, /device:TPU:1, one launch (start us, length us, event | category | flops | bytes accessed | tf_op | source)
XLA Modules:
  0.0 96.6 jit_solution(4522122698881865719)
XLA Ops:
  0.6 0.0 copy-start.2
  0.7 0.7 copy-done.2
  1.3 1.1 %broadcast_select_fusion.6 = (bf16[256,256]{1,0:T(8,128)(2,1)S(1)}, bf16[256,256]{1,0:T(8,128)(2,1)S(1)}, bf16[256,256]{1,0:T(8,128)(2,1)S(1)}, bf16[256,256]{1,0:T(8,128)(2,1)S(1)}) fusion(pred[]{:T(512)S(6)} %not.3, bf16[256,512]{1,0:T(8,128)(2,1)} %bitcast.22, pred[]{:T(512)S(6)} %eq.6, bf16[256,512]{1,0:T(8,128)(2,1)} %bitcast.23), kind=kLoop, calls=%fused_computation.11 | loop fusion | flops 262144 | bytes 1048578 | tf_op jit(solution)/shard_map/jit(_where)/select_n | solution.py:262
  2.5 0.0 copy-start
  2.5 5.5 %collective-permute-start.5 = (bf16[272,512]{1,0:T(8,128)(2,1)S(1)}, bf16[272,512]{1,0:T(8,128)(2,1)S(1)}, u32[]{:S(2)}, u32[]{:S(2)}) collective-permute-start(bf16[272,512]{1,0:T(8,128)(2,1)S(1)} %get-tuple-element.36), channel_id=1, source_target_pairs={{0,5},{1,4},{2,7},{3,6},{4,9},{5,8},{6,11},{7,10},{8,13},{9,12},{1... | collective-permute-start | bytes 835592 | tf_op jit(solution)/shard_map/ppermute | solution.py:250
  8.1 4.7 %collective-permute-start = (bf16[272,512]{1,0:T(8,128)(2,1)S(1)}, bf16[272,512]{1,0:T(8,128)(2,1)S(1)}, u32[]{:S(2)}, u32[]{:S(2)}) collective-permute-start(bf16[272,512]{1,0:T(8,128)(2,1)S(1)} %get-tuple-element.36), channel_id=1, source_target_pairs={{0,1},{1,0},{2,3},{3,2},{4,5},{5,4},{6,7},{7,6},{8,9},{9,8},{10,11... | collective-permute-start | bytes 835592 | tf_op jit(solution)/shard_map/ppermute | solution.py:253
  12.8 1.3 %collective-permute-start.3 = (bf16[272,512]{1,0:T(8,128)(2,1)S(1)}, bf16[272,512]{1,0:T(8,128)(2,1)S(1)}, u32[]{:S(2)}, u32[]{:S(2)}) collective-permute-start(bf16[272,512]{1,0:T(8,128)(2,1)S(1)} %get-tuple-element.38.kv_own), channel_id=1, source_target_pairs={{0,4},{1,5},{2,6},{3,7},{4,8},{5,9},{6,10},{7,11},{8,12},{9,13},{1... | collective-permute-start | bytes 835592 | tf_op jit(solution)/shard_map/ppermute | solution.py:250
  14.1 0.0 copy-done
  14.1 2.6 %collective-permute-start.1 = (bf16[256,512]{1,0:T(8,128)(2,1)S(1)}, bf16[256,512]{1,0:T(8,128)(2,1)S(1)}, u32[]{:S(2)}, u32[]{:S(2)}) collective-permute-start(bf16[256,512]{1,0:T(8,128)(2,1)S(1)} %get-tuple-element.68), channel_id=1, source_target_pairs={{0,1},{1,0},{2,3},{3,2},{4,5},{5,4},{6,7},{7,6},{8,9},{9,8},{10,11... | collective-permute-start | bytes 786440 | tf_op jit(solution)/shard_map/ppermute | solution.py:253
  16.8 0.0 collective-permute-done.5.kv_two_x
  16.8 0.0 copy-start.1
  16.8 3.1 %collective-permute-start.6 = (bf16[272,512]{1,0:T(8,128)(2,1)S(1)}, bf16[272,512]{1,0:T(8,128)(2,1)S(1)}, u32[]{:S(2)}, u32[]{:S(2)}) collective-permute-start(bf16[272,512]{1,0:T(8,128)(2,1)S(1)} %broadcast_select_fusion), channel_id=1, source_target_pairs={{0,3},{1,2},{2,0},{3,1},{4,7},{5,6},{6,4},{7,5},{8,11},{9,10},{10,... | collective-permute-start | bytes 835592 | tf_op jit(solution)/shard_map/ppermute | solution.py:276
  20.0 0.0 collective-permute-done.3.kv_two
  20.0 2.6 %collective-permute-start.4 = (bf16[272,512]{1,0:T(8,128)(2,1)S(1)}, bf16[272,512]{1,0:T(8,128)(2,1)S(1)}, u32[]{:S(2)}, u32[]{:S(2)}) collective-permute-start(bf16[272,512]{1,0:T(8,128)(2,1)S(1)} %broadcast_select_fusion.1), channel_id=1, source_target_pairs={{0,2},{2,0},{1,3},{3,1},{4,6},{6,4},{5,7},{7,5},{8,10},{10,8},{9,1... | collective-permute-start | bytes 835592 | tf_op jit(solution)/shard_map/ppermute | solution.py:253
  22.7 0.0 copy-done.1
  22.7 0.0 copy-start.4
  22.7 0.0 copy-start.3
  22.7 3.6 %collective-permute-start.2 = (bf16[256,512]{1,0:T(8,128)(2,1)S(1)}, bf16[256,512]{1,0:T(8,128)(2,1)S(1)}, u32[]{:S(2)}, u32[]{:S(2)}) collective-permute-start(bf16[256,512]{1,0:T(8,128)(2,1)S(1)} %get-tuple-element.66), channel_id=1, source_target_pairs={{0,1},{1,0},{2,3},{3,2},{4,5},{5,4},{6,7},{7,6},{8,9},{9,8},{10,11... | collective-permute-start | bytes 786440 | tf_op jit(solution)/shard_map/ppermute | solution.py:253
  26.3 0.0 copy-done.4
  26.3 0.0 copy-done.3
  26.4 0.0 collective-permute-done.kv_peer
  26.4 0.0 collective-permute-done.1.q_peer
  26.4 1.1 %collective-permute-done.2.g_peer = bf16[256,512]{1,0:T(8,128)(2,1)S(1)} collective-permute-done((bf16[256,512]{1,0:T(8,128)(2,1)S(1)}, bf16[256,512]{1,0:T(8,128)(2,1)S(1)}, u32[]{:S(2)}, u32[]{:S(2)}) %collective-permute-start.2) | collective-permute-done | bytes 262176 | tf_op jit(solution)/shard_map/ppermute | solution.py:253
  27.5 0.0 collective-permute-done.6.kv_one_x
  27.5 5.6 %collective-permute-done.4.kv_one = bf16[272,512]{1,0:T(8,128)(2,1)S(1)} collective-permute-done((bf16[272,512]{1,0:T(8,128)(2,1)S(1)}, bf16[272,512]{1,0:T(8,128)(2,1)S(1)}, u32[]{:S(2)}, u32[]{:S(2)}) %collective-permute-start.4) | collective-permute-done | bytes 278560 | tf_op jit(solution)/shard_map/ppermute | solution.py:253
  33.1 8.8 %attention.1 = (bf16[256,512]{1,0:T(8,128)(2,1)S(1)}, bf16[256,512]{1,0:T(8,128)(2,1)S(1)}, bf16[272,1024]{1,0:T(8,128)(2,1)S(1)}, f32[2,256,512]{2,1,0:T(8,128)...) custom-call(f32[1,512]{1,0:T(1,128)S(1)} %bitcast.16, ...), custom_call_target="tpu_custom_call" | custom-call | flops 8589934592 | bytes 8388608 | tf_op jit(solution)/shard_map/attention/pallas_call | solution.py:196
  41.9 2.7 %collective-permute-start.7 = (bf16[272,1024]{1,0:T(8,128)(2,1)S(1)}, bf16[272,1024]{1,0:T(8,128)(2,1)S(1)}, u32[]{:S(2)}, u32[]{:S(2)}) collective-permute-start(bf16[272,1024]{1,0:T(8,128)(2,1)S(1)} %get-tuple-element.43), channel_id=1, source_target_pairs={{0,1},{1,0},{2,3},{3,2},{4,5},{5,4},{6,7},{7,6},{8,9},{9,8},{10,11... | collective-permute-start | bytes 1671176 | tf_op jit(solution)/shard_map/ppermute | solution.py:253
  44.6 3.0 %collective-permute-start.8 = (bf16[2,256,512]{2,1,0:T(8,128)(2,1)S(1)}, bf16[2,256,512]{2,1,0:T(8,128)(2,1)S(1)}, u32[]{:S(2)}, u32[]{:S(2)}) collective-permute-start(bf16[2,256,512]{2,1,0:T(8,128)(2,1)S(1)} %get-tuple-element.52), channel_id=1, source_target_pairs={{0,2},{2,0},{1,3},{3,1},{4,6},{6,4},{5,7},{7,5},{8,10},{10,8},{9,1... | collective-permute-start | bytes 1572872 | tf_op jit(solution)/shard_map/ppermute | solution.py:253
  47.6 0.0 collective-permute-done.7.from_peer
  47.7 1.1 %join_queries.1 = (bf16[256,1024]{1,0:T(8,128)(2,1)}, bf16[256,1024]{1,0:T(8,128)(2,1)}, f32[1,512]{1,0:T(1,128)S(1)}) custom-call(bf16[256,512]{1,0:T(8,128)(2,1)S(1)} %get-tuple-element.41.att_mine, bf16[256,512]{1,0:T(8,128)(2,1)S(1)} %get-tuple-element.42.grad_mine, bf16[272,1024]{1,0:T(8,128)(2,1)S(1)} %collective-permute-done.7.from_peer, ...), custom_call_target="tpu_custom_call" | custom-call | tf_op jit(solution)/shard_map/join_queries/pallas_call | solution.py:230
  48.8 0.1 broadcast_in_dim.27
  48.8 27.0 %all_to_all.9 = f32[64,1,512]{2,1,0:T(1,128)S(1)} all-to-all(f32[64,1,512]{2,1,0:T(1,128)S(1)} %broadcast_in_dim.27), channel_id=1, replica_groups=mesh['dp'=2,'y'=8,'z'=8,'x'=2,'core'=2] {'y','z'}, dimensions={0} | all-to-all | bytes 262144 | tf_op jit(solution)/shard_map/all_to_all | solution.py:297
  75.8 0.0 collective-permute-done.8.side
  75.9 0.2 onward.1
  76.0 1.3 %collective-permute-start.9 = (bf16[2,256,512]{2,1,0:T(8,128)(2,1)S(1)}, bf16[2,256,512]{2,1,0:T(8,128)(2,1)S(1)}, u32[]{:S(2)}, u32[]{:S(2)}) collective-permute-start(bf16[2,256,512]{2,1,0:T(8,128)(2,1)S(1)} %onward.1), channel_id=1, source_target_pairs={{4,0},{5,1},{6,2},{7,3},{8,4},{9,5},{10,6},{11,7},{12,8},{13,9},{1... | collective-permute-start | bytes 1572872 | tf_op jit(solution)/shard_map/ppermute | solution.py:250
  77.4 7.5 %psum.7.gains = f32[1,512]{1,0:T(1,128)S(1)} all-reduce(f32[1,512]{1,0:T(1,128)S(1)} %bitcast.24), channel_id=1, replica_groups=mesh['dp'=2,'y'=8,'z'=8,'x'=2,'core'=2] {'dp','x'}, use_global_device_ids=true, to_apply=%region_1.2 | all-reduce | flops 512 | bytes 4096 | tf_op jit(solution)/shard_map/psum | solution.py:304
  84.9 4.4 %collective-permute-done.9.ahead = bf16[2,256,512]{2,1,0:T(8,128)(2,1)S(1)} collective-permute-done((bf16[2,256,512]{2,1,0:T(8,128)(2,1)S(1)}, bf16[2,256,512]{2,1,0:T(8,128)(2,1)S(1)}, u32[]{:S(2)}, u32[]{:S(2)}) %collective-permute-start.9) | collective-permute-done | bytes 524320 | tf_op jit(solution)/shard_map/ppermute | solution.py:250
  89.3 0.4 finish.1
  89.7 4.9 %collective-permute-start.10 = (bf16[256,512]{1,0:T(8,128)(2,1)S(1)}, bf16[256,512]{1,0:T(8,128)(2,1)S(1)}, u32[]{:S(2)}, u32[]{:S(2)}) collective-permute-start(bf16[256,512]{1,0:T(8,128)(2,1)S(1)} %get-tuple-element.60), channel_id=1, source_target_pairs={{0,1},{1,0},{2,3},{3,2},{4,5},{5,4},{6,7},{7,6},{8,9},{9,8},{10,11... | collective-permute-start | bytes 786440 | tf_op jit(solution)/shard_map/ppermute | solution.py:253
  94.6 1.1 %collective-permute-done.10.other = bf16[256,512]{1,0:T(8,128)(2,1)S(1)} collective-permute-done((bf16[256,512]{1,0:T(8,128)(2,1)S(1)}, bf16[256,512]{1,0:T(8,128)(2,1)S(1)}, u32[]{:S(2)}, u32[]{:S(2)}) %collective-permute-start.10) | collective-permute-done | bytes 262176 | tf_op jit(solution)/shard_map/ppermute | solution.py:253
  95.7 0.9 join_keys.1
  (9 shorter events, 0.2 us)
Async XLA Ops:
  0.6 0.7 copy-start.2
  2.5 11.6 %copy-start = (bf16[1,256,1024]{2,1,0:T(8,128)(2,1)S(1)}, bf16[1,256,1024]{2,1,0:T(8,128)(2,1)}, u32[]{:S(2)}) copy-start(bf16[1,256,1024]{2,1,0:T(8,128)(2,1)} %param.7) | copy-start | bytes 1572868
  2.5 14.2 %collective-permute-start.5 = (bf16[272,512]{1,0:T(8,128)(2,1)S(1)}, bf16[272,512]{1,0:T(8,128)(2,1)S(1)}, u32[]{:S(2)}, u32[]{:S(2)}) collective-permute-start(bf16[272,512]{1,0:T(8,128)(2,1)S(1)} %get-tuple-element.36), channel_id=1, source_target_pairs={{0,5},{1,4},{2,7},{3,6},{4,9},{5,8},{6,11},{7,10},{8,13},{9,12},{1... | collective-permute-start | bytes 835592 | tf_op jit(solution)/shard_map/ppermute | solution.py:250
  8.1 18.3 %collective-permute-start = (bf16[272,512]{1,0:T(8,128)(2,1)S(1)}, bf16[272,512]{1,0:T(8,128)(2,1)S(1)}, u32[]{:S(2)}, u32[]{:S(2)}) collective-permute-start(bf16[272,512]{1,0:T(8,128)(2,1)S(1)} %get-tuple-element.36), channel_id=1, source_target_pairs={{0,1},{1,0},{2,3},{3,2},{4,5},{5,4},{6,7},{7,6},{8,9},{9,8},{10,11... | collective-permute-start | bytes 835592 | tf_op jit(solution)/shard_map/ppermute | solution.py:253
  12.8 7.2 %collective-permute-start.3 = (bf16[272,512]{1,0:T(8,128)(2,1)S(1)}, bf16[272,512]{1,0:T(8,128)(2,1)S(1)}, u32[]{:S(2)}, u32[]{:S(2)}) collective-permute-start(bf16[272,512]{1,0:T(8,128)(2,1)S(1)} %get-tuple-element.38.kv_own), channel_id=1, source_target_pairs={{0,4},{1,5},{2,6},{3,7},{4,8},{5,9},{6,10},{7,11},{8,12},{9,13},{1... | collective-permute-start | bytes 835592 | tf_op jit(solution)/shard_map/ppermute | solution.py:250
  14.1 12.2 %collective-permute-start.1 = (bf16[256,512]{1,0:T(8,128)(2,1)S(1)}, bf16[256,512]{1,0:T(8,128)(2,1)S(1)}, u32[]{:S(2)}, u32[]{:S(2)}) collective-permute-start(bf16[256,512]{1,0:T(8,128)(2,1)S(1)} %get-tuple-element.68), channel_id=1, source_target_pairs={{0,1},{1,0},{2,3},{3,2},{4,5},{5,4},{6,7},{7,6},{8,9},{9,8},{10,11... | collective-permute-start | bytes 786440 | tf_op jit(solution)/shard_map/ppermute | solution.py:253
  16.8 5.9 %copy-start.1 = (bf16[1,256,1024]{2,1,0:T(8,128)(2,1)S(1)}, bf16[1,256,1024]{2,1,0:T(8,128)(2,1)}, u32[]{:S(2)}) copy-start(bf16[1,256,1024]{2,1,0:T(8,128)(2,1)} %param.10) | copy-start | bytes 1572868
  16.8 10.6 %collective-permute-start.6 = (bf16[272,512]{1,0:T(8,128)(2,1)S(1)}, bf16[272,512]{1,0:T(8,128)(2,1)S(1)}, u32[]{:S(2)}, u32[]{:S(2)}) collective-permute-start(bf16[272,512]{1,0:T(8,128)(2,1)S(1)} %broadcast_select_fusion), channel_id=1, source_target_pairs={{0,3},{1,2},{2,0},{3,1},{4,7},{5,6},{6,4},{7,5},{8,11},{9,10},{10,... | collective-permute-start | bytes 835592 | tf_op jit(solution)/shard_map/ppermute | solution.py:276
  20.0 13.1 %collective-permute-start.4 = (bf16[272,512]{1,0:T(8,128)(2,1)S(1)}, bf16[272,512]{1,0:T(8,128)(2,1)S(1)}, u32[]{:S(2)}, u32[]{:S(2)}) collective-permute-start(bf16[272,512]{1,0:T(8,128)(2,1)S(1)} %broadcast_select_fusion.1), channel_id=1, source_target_pairs={{0,2},{2,0},{1,3},{3,1},{4,6},{6,4},{5,7},{7,5},{8,10},{10,8},{9,1... | collective-permute-start | bytes 835592 | tf_op jit(solution)/shard_map/ppermute | solution.py:253
  22.7 3.7 %copy-start.4 = (f32[256]{0:T(256)S(1)}, f32[256]{0:T(256)}, u32[]{:S(2)}) copy-start(f32[256]{0:T(256)} %param.11) | copy-start | bytes 3076
  22.7 3.6 %copy-start.3 = (f32[256]{0:T(256)S(1)}, f32[256]{0:T(256)}, u32[]{:S(2)}) copy-start(f32[256]{0:T(256)} %param.12) | copy-start | bytes 3076
  22.7 4.7 %collective-permute-start.2 = (bf16[256,512]{1,0:T(8,128)(2,1)S(1)}, bf16[256,512]{1,0:T(8,128)(2,1)S(1)}, u32[]{:S(2)}, u32[]{:S(2)}) collective-permute-start(bf16[256,512]{1,0:T(8,128)(2,1)S(1)} %get-tuple-element.66), channel_id=1, source_target_pairs={{0,1},{1,0},{2,3},{3,2},{4,5},{5,4},{6,7},{7,6},{8,9},{9,8},{10,11... | collective-permute-start | bytes 786440 | tf_op jit(solution)/shard_map/ppermute | solution.py:253
  41.9 5.7 %collective-permute-start.7 = (bf16[272,1024]{1,0:T(8,128)(2,1)S(1)}, bf16[272,1024]{1,0:T(8,128)(2,1)S(1)}, u32[]{:S(2)}, u32[]{:S(2)}) collective-permute-start(bf16[272,1024]{1,0:T(8,128)(2,1)S(1)} %get-tuple-element.43), channel_id=1, source_target_pairs={{0,1},{1,0},{2,3},{3,2},{4,5},{5,4},{6,7},{7,6},{8,9},{9,8},{10,11... | collective-permute-start | bytes 1671176 | tf_op jit(solution)/shard_map/ppermute | solution.py:253
  44.6 31.2 %collective-permute-start.8 = (bf16[2,256,512]{2,1,0:T(8,128)(2,1)S(1)}, bf16[2,256,512]{2,1,0:T(8,128)(2,1)S(1)}, u32[]{:S(2)}, u32[]{:S(2)}) collective-permute-start(bf16[2,256,512]{2,1,0:T(8,128)(2,1)S(1)} %get-tuple-element.52), channel_id=1, source_target_pairs={{0,2},{2,0},{1,3},{3,1},{4,6},{6,4},{5,7},{7,5},{8,10},{10,8},{9,1... | collective-permute-start | bytes 1572872 | tf_op jit(solution)/shard_map/ppermute | solution.py:253
  76.0 13.2 %collective-permute-start.9 = (bf16[2,256,512]{2,1,0:T(8,128)(2,1)S(1)}, bf16[2,256,512]{2,1,0:T(8,128)(2,1)S(1)}, u32[]{:S(2)}, u32[]{:S(2)}) collective-permute-start(bf16[2,256,512]{2,1,0:T(8,128)(2,1)S(1)} %onward.1), channel_id=1, source_target_pairs={{4,0},{5,1},{6,2},{7,3},{8,4},{9,5},{10,6},{11,7},{12,8},{13,9},{1... | collective-permute-start | bytes 1572872 | tf_op jit(solution)/shard_map/ppermute | solution.py:250
  89.7 6.1 %collective-permute-start.10 = (bf16[256,512]{1,0:T(8,128)(2,1)S(1)}, bf16[256,512]{1,0:T(8,128)(2,1)S(1)}, u32[]{:S(2)}, u32[]{:S(2)}) collective-permute-start(bf16[256,512]{1,0:T(8,128)(2,1)S(1)} %get-tuple-element.60), channel_id=1, source_target_pairs={{0,1},{1,0},{2,3},{3,2},{4,5},{5,4},{6,7},{7,6},{8,9},{9,8},{10,11... | collective-permute-start | bytes 786440 | tf_op jit(solution)/shard_map/ppermute | solution.py:253
